TPU v7x, 32 devices: a whole 2x2x4 slice. The times are simulated.
32 devices in a mesh: dp: 8 (over z, y), bank: 4 (over x, core).
Axes of the slice: x: 2, y: 2, z: 4, core: 2. Of those that a mesh axis runs over, the one named last changes fastest.
Arguments:
- char_ids: int32 [1024, 4, 50], P('dp'), may hold values from 0 to 261
- resets: int32 [1024, 4], P(('dp', 'bank')), may hold values 0 or 1
- out_grad: bfloat16 [1024, 4, 1024], P(('dp', 'bank')), may hold values from -6 to 6
- char_table: bfloat16 [262, 16], replicated, may hold values from -6 to 6
- conv_weight: bfloat16 [4, 7, 16, 1024], P('bank'), may hold values from -0.75 to 0.75
- conv_bias: bfloat16 [4, 1024], P('bank'), may hold values from -3 to 3
- highway_weight: bfloat16 [2, 2048, 4096], P(None, ('dp', 'bank')), may hold values from -0.125 to 0.125
- highway_bias: bfloat16 [2, 4096], P(None, ('dp', 'bank')), may hold values from -3 to 3
- proj_weight: bfloat16 [2048, 512], P(('dp', 'bank')), may hold values from -0.125 to 0.125
- proj_bias: bfloat16 [512], P(('dp', 'bank')), may hold values from -3 to 3
- lstm_weight: bfloat16 [2, 1024, 16384], P(None, ('dp', 'bank')), may hold values from -0.1875 to 0.1875
- lstm_bias: bfloat16 [2, 16384], P(None, ('dp', 'bank')), may hold values from -3 to 3
- lstm_proj: bfloat16 [2, 4096, 512], P(None, None, ('dp', 'bank')), may hold values from -0.25 to 0.25
Outputs:
- table_grad: float32 [262, 16], replicated
- conv_weight_grad: float32 [4, 7, 16, 1024], P('bank')
- conv_bias_grad: float32 [4, 1024], P('bank')
- highway_weight_grad: float32 [2, 2048, 4096], P(None, ('dp', 'bank'))
- highway_bias_grad: float32 [2, 4096], P(None, ('dp', 'bank'))
- proj_weight_grad: float32 [2048, 512], P(('dp', 'bank'))
- proj_bias_grad: float32 [512], P(('dp', 'bank'))
- lstm_weight_grad: float32 [2, 1024, 16384], P(None, ('dp', 'bank'))
- lstm_bias_grad: float32 [2, 16384], P(None, ('dp', 'bank'))
- lstm_proj_grad: float32 [2, 4096, 512], P(None, None, ('dp', 'bank'))
All inputs are finite; a program needn't handle non-finite values. No bound on the sum of `resets` on one device may be relied on, other than what follows from the above.
Results may differ from a plain program's by a relative error of at most 0.015.
Values may be sent and summed in bfloat16 or wider, within the bound.
A program may use at most 576 MiB of HBM per device.

v0:
```python
from functools import partial
import math

import jax
import jax.numpy as jnp
from jax import lax
from jax.sharding import PartitionSpec as P


def bank_plan(bank_cols):
    return [
        [
            (1, 0, bank_cols // 32),
            (2, bank_cols // 32, bank_cols // 32),
            (3, bank_cols // 16, bank_cols // 16),
            (4, bank_cols // 8, bank_cols // 8),
        ],
        [(5, 0, bank_cols // 4)],
        [(6, 0, bank_cols // 2)],
        [(7, 0, bank_cols)],
    ]


def used_columns(bank_specs):
    return sum((columns for filter_width, first_col, columns in bank_specs))


def block_group(stream_count):
    if stream_count % 4 == 0:
        return 4
    if stream_count % 2 == 0:
        return 2
    return 1


def transposed(former, latter):
    return lax.dot_general(
        former, latter, (((1,), (1,)), ((), ())), preferred_element_type=jnp.float32
    )


def outer_sum(former, latter):
    return lax.dot_general(
        former, latter, (((0,), (0,)), ((), ())), preferred_element_type=jnp.float32
    )


def column_sum(values):
    ones_row = jnp.ones((1, values.shape[0]), values.dtype)
    return jnp.dot(ones_row, values, preferred_element_type=jnp.float32)[0]


def log_sum_exp(values):
    highest = jnp.max(values, axis=1, keepdims=True)
    return highest[:, 0, :] + jnp.log(jnp.sum(jnp.exp(values - highest), axis=1))


def embed_chars(block_ids, char_table):
    vocab_size = char_table.shape[0]
    selector = block_ids[:, :, None] == lax.broadcasted_iota(jnp.int32, (1, 1, vocab_size), 2)
    embedded = jnp.einsum(
        "tcv,vd->tcd", selector.astype(jnp.bfloat16), char_table, preferred_element_type=jnp.float32
    )
    return (embedded.astype(jnp.bfloat16), selector)


def conv_outputs(embedded, kernel, bias_vec, filter_width, first_col, columns):
    row_count, char_count, embed_dims = embedded.shape
    positions = char_count - filter_width + 1
    windows = jnp.concatenate(
        [embedded[:, offset : offset + positions, :] for offset in range(filter_width)], axis=2
    )
    windows = windows.reshape(row_count * positions, filter_width * embed_dims)
    weights = kernel[:filter_width, :, first_col : first_col + columns].reshape(
        filter_width * embed_dims, columns
    )
    conv_out = jnp.dot(windows, weights, preferred_element_type=jnp.float32) + bias_vec[
        first_col : first_col + columns
    ].astype(jnp.float32)
    return (windows, weights, conv_out.reshape(row_count, positions, columns))


def bank_pool(bank_specs, char_ids, char_table, kernel, bias_vec):
    group_size = block_group(char_ids.shape[0])
    blocks = char_ids.reshape(
        char_ids.shape[0] // group_size, group_size * char_ids.shape[1], char_ids.shape[2]
    )
    bank_cols = kernel.shape[2]

    def pool_block(block_ids):
        embedded, selector = embed_chars(block_ids, char_table)
        pieces = []
        for filter_width, first_col, columns in bank_specs:
            windows, weights, conv_out = conv_outputs(
                embedded, kernel, bias_vec, filter_width, first_col, columns
            )
            pieces.append(jax.nn.silu(log_sum_exp(conv_out) - math.log(conv_out.shape[1])))
        pieces.append(
            jnp.zeros((block_ids.shape[0], bank_cols - used_columns(bank_specs)), jnp.float32)
        )
        return jnp.concatenate(pieces, axis=1)

    return lax.map(pool_block, blocks).reshape(char_ids.shape[0] * char_ids.shape[1], bank_cols)


def bank_grads(bank_specs, char_ids, char_table, kernel, bias_vec, pooled_grad):
    group_size = block_group(char_ids.shape[0])
    block_count = char_ids.shape[0] // group_size
    blocks = char_ids.reshape(block_count, group_size * char_ids.shape[1], char_ids.shape[2])
    grad_blocks = pooled_grad.reshape(
        block_count, group_size * char_ids.shape[1], pooled_grad.shape[1]
    )
    kernel_width, embed_dims, bank_cols = kernel.shape

    def grad_block(totals, sliced):
        grad_kernel, grad_bias, grad_table = totals
        block_ids, block_grad = sliced
        embedded, selector = embed_chars(block_ids, char_table)
        row_count, char_count = block_ids.shape
        grad_embedded = jnp.zeros((row_count, char_count, embed_dims), jnp.float32)
        for filter_width, first_col, columns in bank_specs:
            windows, weights, conv_out = conv_outputs(
                embedded, kernel, bias_vec, filter_width, first_col, columns
            )
            positions = conv_out.shape[1]
            pooled_lse = log_sum_exp(conv_out)
            softened = jnp.exp(conv_out - pooled_lse[:, None, :])
            pooled_pre = pooled_lse - math.log(positions)
            squashed = jax.nn.sigmoid(pooled_pre)
            upstream = (
                block_grad[:, first_col : first_col + columns].astype(jnp.float32)
                * squashed
                * (1.0 + pooled_pre * (1.0 - squashed))
            )
            grad_conv = (
                (softened * upstream[:, None, :])
                .astype(jnp.bfloat16)
                .reshape(row_count * positions, columns)
            )
            part_kernel = outer_sum(windows, grad_conv).reshape(filter_width, embed_dims, columns)
            grad_kernel = grad_kernel + jnp.pad(
                part_kernel,
                (
                    (0, kernel_width - filter_width),
                    (0, 0),
                    (first_col, bank_cols - first_col - columns),
                ),
            )
            grad_bias = grad_bias + jnp.pad(
                column_sum(grad_conv), (first_col, bank_cols - first_col - columns)
            )
            grad_windows = transposed(grad_conv, weights).reshape(
                row_count, positions, filter_width, embed_dims
            )
            for offset in range(filter_width):
                grad_embedded = grad_embedded + jnp.pad(
                    grad_windows[:, :, offset, :],
                    ((0, 0), (offset, char_count - positions - offset), (0, 0)),
                )
        grad_table = grad_table + jnp.einsum(
            "tcv,tcd->vd",
            selector.astype(jnp.float32),
            grad_embedded,
            precision=lax.Precision.HIGHEST,
        )
        return ((grad_kernel, grad_bias, grad_table), None)

    initial = (
        jnp.zeros(kernel.shape, jnp.float32),
        jnp.zeros((bank_cols,), jnp.float32),
        jnp.zeros(char_table.shape, jnp.float32),
    )
    return lax.scan(grad_block, initial, (blocks, grad_blocks))[0]


def gate_parts(gates_pre, cell_width):
    in_gate = jax.nn.sigmoid(gates_pre[:, :cell_width])
    forget_gate = jax.nn.sigmoid(gates_pre[:, cell_width : 2 * cell_width])
    candidate = jnp.tanh(gates_pre[:, 2 * cell_width : 3 * cell_width])
    out_gate = jax.nn.sigmoid(gates_pre[:, 3 * cell_width :])
    return (in_gate, forget_gate, candidate, out_gate)


def forward_step(weight_rec, proj_mat, carry, sliced):
    cell_state, hidden_state = carry
    gate_inputs, keep_now = sliced
    keep_col = keep_now[:, None]
    cell_start = cell_state * keep_col
    state_start = hidden_state * keep_col.astype(jnp.bfloat16)
    gates_pre = gate_inputs + jnp.dot(state_start, weight_rec, preferred_element_type=jnp.float32)
    in_gate, forget_gate, candidate, out_gate = gate_parts(gates_pre, cell_state.shape[1])
    cell_new = 3.0 * jnp.tanh((forget_gate * cell_start + in_gate * candidate) / 3.0)
    full_state = (out_gate * jnp.tanh(cell_new)).astype(jnp.bfloat16)
    projected = jnp.dot(full_state, proj_mat, preferred_element_type=jnp.float32)
    state_new = (3.0 * jnp.tanh(projected / 3.0)).astype(jnp.bfloat16)
    return ((cell_new, state_new), (gates_pre, cell_start, state_start, full_state, projected))


def backward_step(weight_rec, proj_mat, carry, sliced):
    grad_cell, grad_state = carry
    gates_pre, cell_start, projected, keep_now, grad_out_now = sliced
    grad_state = grad_state + grad_out_now.astype(jnp.float32)
    squashed = jnp.tanh(projected / 3.0)
    grad_projected = (grad_state * (1.0 - squashed * squashed)).astype(jnp.bfloat16)
    grad_full = transposed(grad_projected, proj_mat)
    in_gate, forget_gate, candidate, out_gate = gate_parts(gates_pre, cell_start.shape[1])
    clipped = jnp.tanh((forget_gate * cell_start + in_gate * candidate) / 3.0)
    tanh_cell = jnp.tanh(3.0 * clipped)
    grad_cell_total = grad_cell + grad_full * out_gate * (1.0 - tanh_cell * tanh_cell)
    grad_raw = grad_cell_total * (1.0 - clipped * clipped)
    grad_gates = jnp.concatenate(
        [
            grad_raw * candidate * in_gate * (1.0 - in_gate),
            grad_raw * cell_start * forget_gate * (1.0 - forget_gate),
            grad_raw * in_gate * (1.0 - candidate * candidate),
            grad_full * tanh_cell * out_gate * (1.0 - out_gate),
        ],
        axis=1,
    ).astype(jnp.bfloat16)
    keep_col = keep_now[:, None]
    grad_state_prev = transposed(grad_gates, weight_rec) * keep_col
    grad_cell_prev = grad_raw * forget_gate * keep_col
    return ((grad_cell_prev, grad_state_prev), (grad_gates, grad_projected))


def run_direction(
    time_input, keep_time, grad_out_time, weight_full, bias_full, proj_mat, backwards
):
    step_count, own_streams = keep_time.shape
    proj_width = time_input.shape[1]
    gate_width = weight_full.shape[1]
    cell_width = proj_mat.shape[0]
    weight_in = weight_full[:proj_width]
    weight_rec = weight_full[proj_width:]
    input_gates = (
        jnp.dot(time_input, weight_in, preferred_element_type=jnp.float32)
        + bias_full.astype(jnp.float32)
    ).reshape(step_count, own_streams, gate_width)
    initial = (
        jnp.zeros((own_streams, cell_width), jnp.float32),
        jnp.zeros((own_streams, proj_width), jnp.bfloat16),
    )
    history = lax.scan(
        partial(forward_step, weight_rec, proj_mat),
        initial,
        (input_gates, keep_time),
        reverse=backwards,
    )[1]
    gates_all, cell_starts, state_starts, full_states, projected_all = history
    initial_grad = (
        jnp.zeros((own_streams, cell_width), jnp.float32),
        jnp.zeros((own_streams, proj_width), jnp.float32),
    )
    grad_history = lax.scan(
        partial(backward_step, weight_rec, proj_mat),
        initial_grad,
        (gates_all, cell_starts, projected_all, keep_time, grad_out_time),
        reverse=not backwards,
    )[1]
    grad_gates, grad_projected = grad_history
    flat_gates = grad_gates.reshape(step_count * own_streams, gate_width)
    grad_weight = jnp.concatenate(
        [
            outer_sum(time_input, flat_gates),
            outer_sum(state_starts.reshape(step_count * own_streams, proj_width), flat_gates),
        ],
        axis=0,
    )
    grad_bias = column_sum(flat_gates)
    grad_proj = outer_sum(
        full_states.reshape(step_count * own_streams, cell_width),
        grad_projected.reshape(step_count * own_streams, proj_width),
    )
    grad_input = transposed(flat_gates, weight_in)
    return (grad_input, grad_weight, grad_bias, grad_proj)


def shards(
    char_ids,
    resets,
    out_grad,
    char_table,
    conv_weight,
    conv_bias,
    highway_weight,
    highway_bias,
    proj_weight,
    proj_bias,
    lstm_weight,
    lstm_bias,
    lstm_proj,
):
    own_streams, step_count = resets.shape
    bank_cols = conv_weight.shape[3]
    bank_layout = bank_plan(bank_cols)
    widths_used = [used_columns(bank_specs) for bank_specs in bank_layout]
    bank_count = lax.axis_size("bank")
    (
        highway_full,
        highway_bias_full,
        project_full,
        project_bias,
        lstm_first,
        bias_first,
        proj_first,
    ) = (
        lax.all_gather(highway_weight, ("dp", "bank"), axis=1, tiled=True),
        lax.all_gather(highway_bias, ("dp", "bank"), axis=1, tiled=True),
        lax.all_gather(proj_weight, ("dp", "bank"), axis=0, tiled=True),
        lax.all_gather(proj_bias, ("dp", "bank"), axis=0, tiled=True),
        lax.all_gather(lstm_weight[0], ("dp", "bank"), axis=0, tiled=True),
        lax.all_gather(lstm_bias[0], ("dp", "bank"), axis=0, tiled=True),
        lax.all_gather(lstm_proj[0], ("dp", "bank"), axis=1, tiled=True),
    )
    branches = [partial(bank_pool, bank_specs) for bank_specs in bank_layout]
    pooled = lax.switch(
        lax.axis_index("bank"), branches, char_ids, char_table, conv_weight[0], conv_bias[0]
    )
    received = lax.all_to_all(
        pooled.astype(jnp.bfloat16), "bank", split_axis=0, concat_axis=1, tiled=True
    )
    features = jnp.concatenate(
        [
            received[:, bank_index * bank_cols : bank_index * bank_cols + widths_used[bank_index]]
            for bank_index in range(bank_count)
        ],
        axis=1,
    )
    feature_count = features.shape[1]
    hidden_f32 = features.astype(jnp.float32)
    saved = []
    for highway_level in range(2):
        operand = features if highway_level == 0 else hidden_f32.astype(jnp.bfloat16)
        mixed = jnp.dot(
            operand, highway_full[highway_level], preferred_element_type=jnp.float32
        ) + highway_bias_full[highway_level].astype(jnp.float32)
        saved.append((operand, hidden_f32, mixed))
        carry_gate = jax.nn.sigmoid(mixed[:, feature_count:])
        hidden_f32 = carry_gate * hidden_f32 + (1.0 - carry_gate) * jax.nn.silu(
            mixed[:, :feature_count]
        )
    top_rows = hidden_f32.astype(jnp.bfloat16)
    lstm_input = (
        jnp.dot(top_rows, project_full, preferred_element_type=jnp.float32)
        + project_bias.astype(jnp.float32)
    ).astype(jnp.bfloat16)
    proj_width = lstm_input.shape[1]
    time_input = jnp.swapaxes(
        lstm_input.reshape(own_streams, step_count, proj_width), 0, 1
    ).reshape(step_count * own_streams, proj_width)
    cleared = resets.astype(jnp.float32)
    keep_forward = jnp.swapaxes(1.0 - cleared, 0, 1)
    keep_backward = jnp.swapaxes(
        1.0 - jnp.concatenate([cleared[:, 1:], jnp.zeros((own_streams, 1), jnp.float32)], axis=1),
        0,
        1,
    )
    grad_time = jnp.swapaxes(out_grad, 0, 1)
    results_first = run_direction(
        time_input,
        keep_forward,
        grad_time[:, :, :proj_width],
        lstm_first,
        bias_first,
        proj_first,
        False,
    )
    shard_first = (
        lax.psum_scatter(results_first[1], ("dp", "bank"), scatter_dimension=0, tiled=True),
        lax.psum_scatter(results_first[2], ("dp", "bank"), scatter_dimension=0, tiled=True),
        lax.psum_scatter(results_first[3], ("dp", "bank"), scatter_dimension=1, tiled=True),
    )
    lstm_second, bias_second, proj_second = (
        lax.all_gather(lstm_weight[1], ("dp", "bank"), axis=0, tiled=True),
        lax.all_gather(lstm_bias[1], ("dp", "bank"), axis=0, tiled=True),
        lax.all_gather(lstm_proj[1], ("dp", "bank"), axis=1, tiled=True),
    )
    results_second = run_direction(
        time_input,
        keep_backward,
        grad_time[:, :, proj_width:],
        lstm_second,
        bias_second,
        proj_second,
        True,
    )
    grad_time_input = results_first[0] + results_second[0]
    grad_input = (
        jnp.swapaxes(grad_time_input.reshape(step_count, own_streams, proj_width), 0, 1)
        .reshape(own_streams * step_count, proj_width)
        .astype(jnp.bfloat16)
    )
    grad_project_w = outer_sum(top_rows, grad_input)
    grad_project_b = column_sum(grad_input)
    grad_hidden = transposed(grad_input, project_full)
    weight_levels = [None, None]
    bias_levels = [None, None]
    for highway_level in (1, 0):
        operand, hidden_in, mixed = saved[highway_level]
        carry_gate = jax.nn.sigmoid(mixed[:, feature_count:])
        pre_act = mixed[:, :feature_count]
        act_sig = jax.nn.sigmoid(pre_act)
        grad_act = grad_hidden * (1.0 - carry_gate) * act_sig * (1.0 + pre_act * (1.0 - act_sig))
        grad_carry = grad_hidden * (hidden_in - pre_act * act_sig) * carry_gate * (1.0 - carry_gate)
        grad_mixed = jnp.concatenate([grad_act, grad_carry], axis=1).astype(jnp.bfloat16)
        weight_levels[highway_level] = outer_sum(operand, grad_mixed)
        bias_levels[highway_level] = column_sum(grad_mixed)
        grad_hidden = grad_hidden * carry_gate + transposed(grad_mixed, highway_full[highway_level])
    grad_features = grad_hidden.astype(jnp.bfloat16)
    shard_last = (
        lax.psum_scatter(results_second[1], ("dp", "bank"), scatter_dimension=0, tiled=True),
        lax.psum_scatter(results_second[2], ("dp", "bank"), scatter_dimension=0, tiled=True),
        lax.psum_scatter(results_second[3], ("dp", "bank"), scatter_dimension=1, tiled=True),
        lax.psum_scatter(jnp.stack(weight_levels), ("dp", "bank"), scatter_dimension=1, tiled=True),
        lax.psum_scatter(jnp.stack(bias_levels), ("dp", "bank"), scatter_dimension=1, tiled=True),
        lax.psum_scatter(grad_project_w, ("dp", "bank"), scatter_dimension=0, tiled=True),
        lax.psum_scatter(grad_project_b, ("dp", "bank"), scatter_dimension=0, tiled=True),
    )
    col_starts = [sum(widths_used[:bank_index]) for bank_index in range(bank_count)]
    bank_pieces = [
        jnp.pad(
            grad_features[
                :, col_starts[bank_index] : col_starts[bank_index] + widths_used[bank_index]
            ],
            ((0, 0), (0, bank_cols - widths_used[bank_index])),
        )
        for bank_index in range(bank_count)
    ]
    returned = lax.all_to_all(
        jnp.concatenate(bank_pieces, axis=1), "bank", split_axis=1, concat_axis=0, tiled=True
    )
    branches_back = [partial(bank_grads, bank_specs) for bank_specs in bank_layout]
    grad_kernel, grad_bias, grad_table = lax.switch(
        lax.axis_index("bank"),
        branches_back,
        char_ids,
        char_table,
        conv_weight[0],
        conv_bias[0],
        returned,
    )
    grad_kernel = grad_kernel[None]
    grad_bias = grad_bias[None]
    grad_kernel, grad_bias = lax.psum((grad_kernel, grad_bias), "dp")
    grad_table = lax.psum(grad_table, ("dp", "bank"))
    lstm_weight_grad = jnp.stack([shard_first[0], shard_last[0]])
    lstm_bias_grad = jnp.stack([shard_first[1], shard_last[1]])
    lstm_proj_grad = jnp.stack([shard_first[2], shard_last[2]])
    return (
        grad_table,
        grad_kernel,
        grad_bias,
        shard_last[3],
        shard_last[4],
        shard_last[5],
        shard_last[6],
        lstm_weight_grad,
        lstm_bias_grad,
        lstm_proj_grad,
    )


def solution(mesh):
    placed = (
        P("dp", None, None),
        P(("dp", "bank"), None),
        P(("dp", "bank"), None, None),
        P(),
        P("bank", None, None, None),
        P("bank", None),
        P(None, ("dp", "bank"), None),
        P(None, ("dp", "bank")),
        P(("dp", "bank"), None),
        P(("dp", "bank")),
        P(None, ("dp", "bank"), None),
        P(None, ("dp", "bank")),
        P(None, None, ("dp", "bank")),
    )
    return jax.shard_map(
        shards,
        mesh=mesh,
        in_specs=placed,
        out_specs=(
            P(),
            P("bank", None, None, None),
            P("bank", None),
            P(None, ("dp", "bank"), None),
            P(None, ("dp", "bank")),
            P(("dp", "bank"), None),
            P(("dp", "bank")),
            P(None, ("dp", "bank"), None),
            P(None, ("dp", "bank")),
            P(None, None, ("dp", "bank")),
        ),
        check_vma=False,
    )
```

profile of v0, /device:TPU:14, one launch (start us, length us, event | category | flops | bytes accessed | tf_op | source)
XLA Modules:
  0.0 3916.1 jit_solution(12794597341024316109)
XLA Ops:
  15.4 168.5 %conditional.2 = (bf16[32,16,1024]{2,1,0:T(8,128)(2,1)}) conditional(s32[]{:T(128)} %clamp.4, (s32[128,4,50]{0,1,2:T(4,128)S(1)}, bf16[262,16]{0,1:T(8,128)(2,1)}, bf16[7,16,1024]{2,1,0:T(8,128)(2,1)S(1)}, bf16[1024]{0:T(1024)(128)(2,1)}) %tuple.618, (s32[128,4,50]{0,1,2:T(4,128)S(1)}, bf16[262,16]{0,1:T(8,128)(2,1)}, ...), branch_computations={%region_0.11_spmd, %region_11.16_spmd, %region_16.21_spmd, %region... | conditional | flops 171360448 | bytes 16962296 | solution.py:316
  16.3 167.6 %while.198 = (s32[]{:T(128)}, bf16[32,16,1024]{2,1,0:T(8,128)(2,1)}, s32[32,16,50]{2,1,0:T(8,128)}, bf16[262,16]{0,1:T(8,128)(2,1)}, bf16[7,16,1024]{2,1,0:T(8,1...) while((s32[]{:T(128)}, bf16[32,16,1024]{2,1,0:T(8,128)(2,1)}, s32[32,16,50]{2,1,0:T(8,128)}, ...), condition=%wide.region_20.20_spmd, body=%wide.region_17.19_spmd.sunk | while | flops 79224512 | bytes 9381033 | solution.py:103
  183.9 156.3 %all-to-all-start = ((bf16[4,128,1024]{2,1,0:T(8,128)(2,1)}), bf16[4,128,1024]{2,1,0:T(8,128)(2,1)S(1)}, u32[]{:S(2)}, u32[]{:S(2)}) async-start(bf16[4,128,1024]{2,1,0:T(8,128)(2,1)} %bitcast.33), calls=%async_computation | async-start | bytes 2097152 | tf_op jit(solution)/shard_map/all_to_all | solution.py:319
  341.5 46.9 %all-reduce.44 = bf16[512]{0:T(512)(128)(2,1)S(1)} all-reduce(bf16[512]{0:T(512)(128)(2,1)S(1)} %dynamic-update-slice), channel_id=1, replica_groups=mesh['dp'=8,'bank'=4] {'dp','bank'}, use_global_device_ids=true, to_apply=%add.44 | all-reduce | flops 512 | bytes 2048
  388.5 29.5 all-gather.1
  418.1 39.8 %all-gather.4 = bf16[1,16384]{1,0:T(2,128)(2,1)S(1)} all-gather(bf16[1,512]{1,0:T(2,128)(2,1)S(1)} %get-tuple-element.2469), channel_id=6, replica_groups=mesh['dp'=8,'bank'=4] {'dp','bank'}, dimensions={1}, use_global_device_ids=true | all-gather | bytes 33792 | tf_op jit(solution)/shard_map/all_gather | solution.py:375
  458.6 37.3 all_gather.31
  530.5 56.4 %all-gather.17.cloned.1.call-done = bf16[1,1024,16384]{2,1,0:T(8,128)(2,1)} async-done(((bf16[1,32,16384]{2,1,0:T(8,128)(2,1)}), bf16[1,1024,16384]{2,1,0:T(8,128)(2,1)}) %all-gather.17.cloned.1.call-update) | async-done | bytes 33554448 | tf_op jit(solution)/shard_map/all_gather | solution.py:311
  618.4 54.1 %while.204 = (s32[]{:T(128)}, f32[32,4096]{1,0:T(8,128)S(1)}, bf16[32,512]{1,0:T(8,128)(2,1)S(1)}, f32[4,32,16384]{2,1,0:T(8,128)}, f32[4,32,4096]{2,1,0:T(8,128...) while((s32[]{:T(128)}, f32[32,4096]{1,0:T(8,128)S(1)}, ...), condition=%wide.region_27.28_spmd.clone, body=%wide.region_26.27_spmd.clone.sunk | while | flops 674398272 | bytes 49350344 | solution.py:243
  675.7 91.8 %while.205 = (s32[]{:T(128)}, f32[32,4096]{1,0:T(8,128)}, f32[32,512]{1,0:T(8,128)S(1)}, bf16[4,32,16384]{2,1,0:T(8,128)(2,1)}, bf16[4,32,512]{2,1,0:T(8,128)(2,...) while((s32[]{:T(128)}, f32[32,4096]{1,0:T(8,128)}, ...), condition=%wide.region_29.30_spmd.clone, body=%wide.region_28.29_spmd.clone.sunk | while | flops 686833664 | bytes 39125700 | solution.py:254
  813.7 54.0 %while.206 = (s32[]{:T(128)}, f32[32,4096]{1,0:T(8,128)S(1)}, bf16[32,512]{1,0:T(8,128)(2,1)S(1)}, f32[4,32,16384]{2,1,0:T(8,128)}, f32[4,32,4096]{2,1,0:T(8,128...) while((s32[]{:T(128)}, f32[32,4096]{1,0:T(8,128)S(1)}, ...), condition=%wide.region_31.32_spmd.clone, body=%wide.region_30.31_spmd.clone.sunk | while | flops 674398272 | bytes 49350364 | solution.py:243
  870.8 85.5 %while.207 = (s32[]{:T(128)}, f32[32,4096]{1,0:T(8,128)}, f32[32,512]{1,0:T(8,128)S(1)}, bf16[4,32,16384]{2,1,0:T(8,128)(2,1)}, bf16[4,32,512]{2,1,0:T(8,128)(2,...) while((s32[]{:T(128)}, f32[32,4096]{1,0:T(8,128)}, ...), condition=%wide.region_33.34_spmd.clone, body=%wide.region_32.33_spmd.clone.sunk | while | flops 686833664 | bytes 39125680 | solution.py:254
  1044.5 44.8 %pad_maximum_fusion.8 = f32[1024,16384]{1,0:T(8,128)} fusion(f32[512,16384]{1,0:T(8,128)} %convolution_bitcast_fusion.5, f32[512,16384]{1,0:T(8,128)} %convolution_bitcast_fusion.6), kind=kLoop, calls=%fused_computation.499 | loop fusion | flops 16777216 | bytes 134217728 | tf_op jit(solution)/shard_map/concatenate | solution.py:262
  1118.0 44.8 %pad_maximum_fusion.7 = f32[1024,16384]{1,0:T(8,128)} fusion(f32[512,16384]{1,0:T(8,128)} %convolution_bitcast_fusion.7, f32[512,16384]{1,0:T(8,128)} %convolution_bitcast_fusion.8), kind=kLoop, calls=%fused_computation.498 | loop fusion | flops 16777216 | bytes 134217728 | tf_op jit(solution)/shard_map/concatenate | solution.py:262
  1176.7 20.2 all_to_all.35
  1196.9 540.7 %conditional.3 = (f32[7,16,1024]{2,1,0:T(8,128)}, f32[1024]{0:T(1024)}, f32[262,16]{0,1:T(8,128)}) conditional(s32[]{:T(128)} %clamp.4, (s32[128,4,50]{0,1,2:T(4,128)S(1)}, bf16[512,1024]{1,0:T(8,128)(2,1)}, bf16[262,16]{0,1:T(8,128)(2,1)}, bf16[7,16,1024]{2,1,0:T(8,128)(2,1)S(1)}, ...), branch_computations={%region_34.45_spmd, %region_45.50_spmd, %region_50.55_spmd, %regio... | conditional | flops 538777664 | bytes 72293160 | solution.py:433
  1197.3 540.3 %while.202 = (s32[]{:T(128)}, f32[7,16,1024]{2,1,0:T(8,128)}, f32[1024]{0:T(1024)}, f32[262,16]{0,1:T(8,128)}, s32[32,16,50]{2,1,0:T(8,128)S(1)}, /*index=5*/bf1...) while((s32[]{:T(128)}, f32[7,16,1024]{2,1,0:T(8,128)}, ...), condition=%wide.region_54.54_spmd.clone, body=%wide.region_51.53_spmd.clone.sunk | while | flops 263414848 | bytes 31096000 | solution.py:173
  1771.0 44.5 %pad_maximum_fusion.6 = f32[2,2048,4096]{2,1,0:T(8,128)} fusion(f32[1,2048,4096]{2,1,0:T(8,128)} %convolution_bitcast_fusion.9, f32[1,2048,4096]{2,1,0:T(8,128)} %convolution_bitcast_fusion.10), kind=kLoop, calls=%fused_computation.497 | loop fusion | flops 16777216 | bytes 134217728 | tf_op jit(solution)/shard_map/stack | solution.py:414
  1820.1 665.1 %all-reduce.48 = (f32[262,16]{0,1:T(8,128)}, f32[512]{0:T(512)S(1)}) all-reduce(f32[262,16]{0,1:T(8,128)} %get-tuple-element.1519, f32[512]{0:T(512)S(1)} %bitcast.1018), channel_id=1, replica_groups=mesh['dp'=8,'bank'=4] {'dp','bank'}, use_global_device_ids=true, to_apply=%region_60.61 | all-reduce | flops 4704 | bytes 37632 | tf_op jit(solution)/shard_map/psum | solution.py:445
  2485.8 16.3 psum.23
  2504.0 475.0 %reduce-scatter.14.cloned.1.call-done = f32[32,16384]{1,0:T(8,128)} async-done(((f32[1024,16384]{1,0:T(8,128)}), f32[32,16384]{1,0:T(8,128)}) %reduce-scatter.14.cloned.1.call-update) | async-done | bytes 2097168 | tf_op jit(solution)/shard_map/reduce_scatter | solution.py:369
  2983.6 72.4 %all-reduce.53.cloned.1.call-done = f32[1,7,16,1024]{3,2,1,0:T(8,128)} async-done(((f32[1,7,16,1024]{3,2,1,0:T(8,128)}), f32[1,7,16,1024]{3,2,1,0:T(8,128)}) %all-reduce.53.cloned.1.call-update) | async-done | bytes 458768 | tf_op jit(solution)/shard_map/psum | solution.py:444
  3056.0 110.9 %reduce-scatter.12.cloned.1.call-done = f32[64,512]{1,0:T(8,128)} async-done(((f32[2048,512]{1,0:T(8,128)}), f32[64,512]{1,0:T(8,128)}) %reduce-scatter.12.cloned.1.call-update) | async-done | bytes 131088 | tf_op jit(solution)/shard_map/reduce_scatter | solution.py:416
  3166.9 740.4 %reduce-scatter.10.cloned.1.call-done = f32[2,64,4096]{2,1,0:T(8,128)} async-done(((f32[2,2048,4096]{2,1,0:T(8,128)}), f32[2,64,4096]{2,1,0:T(8,128)}) %reduce-scatter.10.cloned.1.call-update) | async-done | bytes 2097168 | tf_op jit(solution)/shard_map/reduce_scatter | solution.py:414
  (2244 shorter events, 1290.2 us)
Async XLA Ops:
  7.2 490.3 %all-gather.19.cloned.1.call-start = ((), (), s32[]{:S(2)}) async-start(), calls=%async_computation.19 | async-start | bytes 4325376 | tf_op jit(solution)/shard_map/all_gather | solution.py:313
  8.9 495.3 %all-gather.23.cloned.1.call-start = ((), (), s32[]{:S(2)}) async-start(), calls=%async_computation.21 | async-start | bytes 4325376 | tf_op jit(solution)/shard_map/all_gather | solution.py:376
  9.7 501.1 %all-gather.13.cloned.1.call-start = ((), (), s32[]{:S(2)}) async-start(), calls=%async_computation.9 | async-start | bytes 34603008 | tf_op jit(solution)/shard_map/all_gather | solution.py:307
  10.4 517.8 %all-gather.15.cloned.1.call-start = ((), (), s32[]{:S(2)}) async-start(), calls=%async_computation.10 | async-start | bytes 2162688 | tf_op jit(solution)/shard_map/all_gather | solution.py:309
  11.0 575.9 %all-gather.17.cloned.1.call-start = ((), (), s32[]{:S(2)}) async-start(), calls=%async_computation.18 | async-start | bytes 34603008 | tf_op jit(solution)/shard_map/all_gather | solution.py:311
  14.2 768.4 %all-gather.21.cloned.1.call-start = ((), (), s32[]{:S(2)}) async-start(), calls=%async_computation.20 | async-start | bytes 34603008 | tf_op jit(solution)/shard_map/all_gather | solution.py:374
  15.4 325.9 %copy-start.71 = (bf16[16]{0:T(256)(128)(2,1)S(1)}, bf16[16]{0:T(256)(128)(2,1)}, u32[]{:S(2)}) copy-start(bf16[16]{0:T(256)(128)(2,1)} %param.54) | copy-start | bytes 100
  15.4 373.1 %copy-start.66 = (bf16[2,512]{1,0:T(2,128)(2,1)S(1)}, bf16[2,512]{1,0:T(2,128)(2,1)}, u32[]{:S(2)}) copy-start(bf16[2,512]{1,0:T(2,128)(2,1)} %param.56) | copy-start | bytes 6148
  183.9 274.7 %copy-start.67 = (s32[32,4]{0,1:T(4,128)S(1)}, s32[32,4]{0,1:T(4,128)}, u32[]{:S(2)}) copy-start(s32[32,4]{0,1:T(4,128)} %param.46) | copy-start | bytes 1540
  183.9 274.7 %copy-start.70 = (bf16[2,128]{1,0:T(2,128)(2,1)S(1)}, bf16[2,128]{1,0:T(2,128)(2,1)}, u32[]{:S(2)}) copy-start(bf16[2,128]{1,0:T(2,128)(2,1)} %param.52) | copy-start | bytes 1540
  183.9 313.3 %all-to-all-start = ((bf16[4,128,1024]{2,1,0:T(8,128)(2,1)}), bf16[4,128,1024]{2,1,0:T(8,128)(2,1)S(1)}, u32[]{:S(2)}, u32[]{:S(2)}) async-start(bf16[4,128,1024]{2,1,0:T(8,128)(2,1)} %bitcast.33), calls=%async_computation | async-start | bytes 2097152 | tf_op jit(solution)/shard_map/all_to_all | solution.py:319
  340.2 1476.4 %all-reduce.55.cloned.1.call-start = ((), (), s32[]{:S(2)}) async-start(), calls=%async_computation.23 | async-start | bytes 262144
  528.2 70.2 %copy-start.20 = (bf16[128,2048]{1,0:T(8,128)(2,1)}, bf16[128,2048]{1,0:T(8,128)(2,1)S(1)}, u32[]{:S(2)}) copy-start(bf16[128,2048]{1,0:T(8,128)(2,1)S(1)} %add_convert_fusion) | copy-start | bytes 1572868
  530.5 67.9 %copy-start.25 = (bf16[32,4,512]{2,1,0:T(4,128)(2,1)}, bf16[32,4,512]{2,1,0:T(4,128)(2,1)S(1)}, u32[]{:S(2)}) copy-start(bf16[32,4,512]{2,1,0:T(4,128)(2,1)S(1)} %reshape.891) | copy-start | bytes 393220
  530.5 67.8 %copy-start.62 = (bf16[32,4,512]{2,0,1:T(8,128)(2,1)}, bf16[32,4,512]{2,0,1:T(8,128)(2,1)S(1)}, u32[]{:S(2)}) copy-start(bf16[32,4,512]{2,0,1:T(8,128)(2,1)S(1)} %copy.374) | copy-start | bytes 393220
  767.4 28.9 copy-start.64
  1000.3 818.4 %reduce-scatter.22.cloned.1.call-start = ((), (), s32[]{:S(2)}) async-start(), calls=%async_computation.22 | async-start | bytes 2162688
  1002.4 1499.7 %reduce-scatter.20.cloned.1.call-start = ((), (), s32[]{:S(2)}) async-start(), calls=%async_computation.17 | async-start | bytes 8650752 | tf_op jit(solution)/shard_map/reduce_scatter | solution.py:413
  1008.0 1494.2 %reduce-scatter.18.cloned.1.call-start = ((), (), s32[]{:S(2)}) async-start(), calls=%async_computation.16 | async-start | bytes 8650752 | tf_op jit(solution)/shard_map/reduce_scatter | solution.py:371
  1014.7 1489.3 %reduce-scatter.16.cloned.1.call-start = ((), (), s32[]{:S(2)}) async-start(), calls=%async_computation.15 | async-start | bytes 69206016 | tf_op jit(solution)/shard_map/reduce_scatter | solution.py:411
  1089.3 1889.8 %reduce-scatter.14.cloned.1.call-start = ((), (), s32[]{:S(2)}) async-start(), calls=%async_computation.14 | async-start | bytes 69206016 | tf_op jit(solution)/shard_map/reduce_scatter | solution.py:369
  1162.9 1893.1 %all-reduce.53.cloned.1.call-start = ((), (), s32[]{:S(2)}) async-start(), calls=%async_computation.11 | async-start | bytes 917504 | tf_op jit(solution)/shard_map/psum | solution.py:444
  1737.7 1429.2 %reduce-scatter.12.cloned.1.call-start = ((), (), s32[]{:S(2)}) async-start(), calls=%async_computation.13 | async-start | bytes 4325376 | tf_op jit(solution)/shard_map/reduce_scatter | solution.py:416
  1741.8 2165.5 %reduce-scatter.10.cloned.1.call-start = ((), (), s32[]{:S(2)}) async-start(), calls=%async_computation.12 | async-start | bytes 69206016 | tf_op jit(solution)/shard_map/reduce_scatter | solution.py:414
  (189 other events, 878.1 us)
Sparse Core Ops, SparseCore 0:
  10.9 62.4 all-gather.18
  76.8 60.6 all-gather.22
  140.4 191.6 all-gather.12
  334.9 55.8 all-gather.14
  393.5 193.3 all-gather.16
  589.6 192.9 all-gather.20
  1000.4 122.8 all-reduce.54
  1125.5 104.8 reduce-scatter.21
  1232.8 144.3 reduce-scatter.19
  1379.5 144.8 reduce-scatter.17
  1526.8 738.2 reduce-scatter.15
  2267.4 711.6 reduce-scatter.13
  2983.4 72.5 all-reduce.52
  3058.7 108.1 reduce-scatter.11
  3169.7 737.5 reduce-scatter.9
where the time goes:
time: 3950 us; the launch traced here: 3920 us
  waiting for transfers between devices  1470 us (37%)
  blocking collectives  855 us (22%)
  matrix products  617 us (16%)
  other arithmetic  452 us (11%)
  local copies, waits for them, and re-layouts  336 us (9%)
  starting transfers between devices  158 us (4%)
    reduce_scatter x1, waiting for transfers between devices, shards(): lax.psum_scatter(jnp.stack(weight_levels), ('dp', 'bank'), scatter_dimens...  740 us
    psum x1, blocking collectives, shards(): grad_table = lax.psum(grad_table, ('dp', 'bank'))  665 us
    reduce_scatter x1, waiting for transfers between devices, shards(): lax.psum_scatter(results_first[1], ('dp', 'bank'), scatter_dimension=0, t...  475 us
    dot_general x53, matrix products, transposed(): lax.dot_general(former, latter, (((1,), (1,)), ((), ())), preferred_eleme...  192 us
    all_to_all x1, starting transfers between devices, shards(): lax.all_to_all(pooled.astype(jnp.bfloat16), 'bank', split_axis=0, concat_...  156 us
    reduce_scatter x1, waiting for transfers between devices, shards(): lax.psum_scatter(grad_project_w, ('dp', 'bank'), scatter_dimension=0, til...  111 us
    dot_general x41, matrix products, outer_sum(): lax.dot_general(former, latter, (((0,), (0,)), ((), ())), preferred_eleme...  108 us
    concatenate x2, other arithmetic, run_direction(): jnp.concatenate([outer_sum(time_input, flat_gates), outer_sum(state_start...  89.6 us
  transfers between devices with their start and end apart: 16, of which 6 were waited for; matrix products, arithmetic and copies ran while one was open for 30% of the time, Pallas kernels for 0%

commit v1 on v0

--- a/solution.py
+++ b/solution.py
@@ -4,7 +4,19 @@
 import jax
 import jax.numpy as jnp
 from jax import lax
+from jax.experimental import pallas as pl
+from jax.experimental.pallas import tpu as pltpu
 from jax.sharding import PartitionSpec as P
+
+CHAR_COUNT = 50
+EMBED = 16
+WIDEST = 7
+TAPS = WIDEST * EMBED
+LANES = 128
+PLACES = 64
+TIGHT = 48
+CHUNK = 256
+TOKEN_BLOCK = 16
 
 
 def bank_plan(bank_cols):
@@ -21,18 +33,6 @@
     ]
 
 
-def used_columns(bank_specs):
-    return sum((columns for filter_width, first_col, columns in bank_specs))
-
-
-def block_group(stream_count):
-    if stream_count % 4 == 0:
-        return 4
-    if stream_count % 2 == 0:
-        return 2
-    return 1
-
-
 def transposed(former, latter):
     return lax.dot_general(
         former, latter, (((1,), (1,)), ((), ())), preferred_element_type=jnp.float32
@@ -50,127 +50,240 @@
     return jnp.dot(ones_row, values, preferred_element_type=jnp.float32)[0]
 
 
-def log_sum_exp(values):
-    highest = jnp.max(values, axis=1, keepdims=True)
-    return highest[:, 0, :] + jnp.log(jnp.sum(jnp.exp(values - highest), axis=1))
-
-
-def embed_chars(block_ids, char_table):
-    vocab_size = char_table.shape[0]
-    selector = block_ids[:, :, None] == lax.broadcasted_iota(jnp.int32, (1, 1, vocab_size), 2)
-    embedded = jnp.einsum(
-        "tcv,vd->tcd", selector.astype(jnp.bfloat16), char_table, preferred_element_type=jnp.float32
-    )
-    return (embedded.astype(jnp.bfloat16), selector)
-
-
-def conv_outputs(embedded, kernel, bias_vec, filter_width, first_col, columns):
-    row_count, char_count, embed_dims = embedded.shape
-    positions = char_count - filter_width + 1
-    windows = jnp.concatenate(
-        [embedded[:, offset : offset + positions, :] for offset in range(filter_width)], axis=2
-    )
-    windows = windows.reshape(row_count * positions, filter_width * embed_dims)
-    weights = kernel[:filter_width, :, first_col : first_col + columns].reshape(
-        filter_width * embed_dims, columns
-    )
-    conv_out = jnp.dot(windows, weights, preferred_element_type=jnp.float32) + bias_vec[
-        first_col : first_col + columns
-    ].astype(jnp.float32)
-    return (windows, weights, conv_out.reshape(row_count, positions, columns))
-
-
-def bank_pool(bank_specs, char_ids, char_table, kernel, bias_vec):
-    group_size = block_group(char_ids.shape[0])
-    blocks = char_ids.reshape(
-        char_ids.shape[0] // group_size, group_size * char_ids.shape[1], char_ids.shape[2]
-    )
-    bank_cols = kernel.shape[2]
-
-    def pool_block(block_ids):
-        embedded, selector = embed_chars(block_ids, char_table)
-        pieces = []
-        for filter_width, first_col, columns in bank_specs:
-            windows, weights, conv_out = conv_outputs(
-                embedded, kernel, bias_vec, filter_width, first_col, columns
-            )
-            pieces.append(jax.nn.silu(log_sum_exp(conv_out) - math.log(conv_out.shape[1])))
-        pieces.append(
-            jnp.zeros((block_ids.shape[0], bank_cols - used_columns(bank_specs)), jnp.float32)
+def filter_columns(bank_cols):
+    columns = []
+    for bank_index, bank_specs in enumerate(bank_plan(bank_cols)):
+        for filter_width, first_col, count in bank_specs:
+            columns.append((filter_width, bank_index, first_col, count))
+    return columns
+
+
+def shift_rows(values, amount):
+    count = values.shape[0]
+    return values if amount % count == 0 else pltpu.roll(values, amount % count, 0)
+
+
+def block_windows(tiled_ref, windows_wide, windows_tight):
+    tokens, places, lanes = tiled_ref.shape
+    rows = tokens * places
+    tiled = tiled_ref[...].astype(jnp.float32).reshape(rows, lanes)
+    lane = lax.broadcasted_iota(jnp.int32, (rows, lanes), 1)
+    place = lax.broadcasted_iota(jnp.int32, (rows, lanes), 0) % places
+    windows = tiled
+    for offset in range(1, WIDEST):
+        windows = jnp.where(lane // EMBED == offset, shift_rows(tiled, rows - offset), windows)
+    late = place >= CHAR_COUNT - WIDEST + 1 + (lane - TAPS - 1)
+    extra = jnp.where((lane == TAPS) | ((lane <= TAPS + WIDEST) & late), 1.0, 0.0)
+    windows = jnp.where(lane < TAPS, windows, extra)
+    windows_wide[...] = windows.astype(jnp.bfloat16)
+    windows_tight[...] = (
+        windows.reshape(tokens, places, lanes)[:, :TIGHT]
+        .reshape(tokens * TIGHT, lanes)
+        .astype(jnp.bfloat16)
+    )
+
+
+def column_chunks(total, tight_from):
+    return [
+        (start, start < tight_from) for start in range(0, total, CHUNK)
+    ]
+
+
+def pool_kernel(tight_from, tiled_ref, weight_ref, count_ref, features_ref, lse_ref, wide, tight):
+    tokens, places, lanes = tiled_ref.shape
+    block_windows(tiled_ref, wide, tight)
+    for start, is_wide in column_chunks(weight_ref.shape[1], tight_from):
+        cols = pl.ds(start, CHUNK)
+        windows = wide if is_wide else tight
+        conv_out = jnp.dot(
+            windows[...], weight_ref[:, cols], preferred_element_type=jnp.float32
+        ).reshape(tokens, -1, CHUNK)
+        highest = jnp.max(conv_out, axis=1)
+        total = jnp.sum(jnp.exp(conv_out - highest[:, None, :]), axis=1)
+        pooled_lse = highest + jnp.log(total)
+        lse_ref[:, cols] = pooled_lse
+        pooled_pre = pooled_lse - count_ref[0:1, cols]
+        features_ref[:, cols] = (pooled_pre * jax.nn.sigmoid(pooled_pre)).astype(jnp.bfloat16)
+
+
+def pool_grad_kernel(
+    tight_from,
+    tiled_ref,
+    weight_ref,
+    count_ref,
+    lse_ref,
+    upstream_ref,
+    grad_weight_ref,
+    aligned_ref,
+    wide,
+    tight,
+    spread,
+):
+    tokens, places, lanes = tiled_ref.shape
+    block_windows(tiled_ref, wide, tight)
+
+    @pl.when(pl.program_id(0) == 0)
+    def _():
+        grad_weight_ref[...] = jnp.zeros_like(grad_weight_ref)
+
+    spread[...] = jnp.zeros_like(spread)
+    wide_turned = wide[...].T
+    tight_turned = tight[...].T
+    for start, is_wide in column_chunks(weight_ref.shape[1], tight_from):
+        cols = pl.ds(start, CHUNK)
+        windows, turned = (wide, wide_turned) if is_wide else (tight, tight_turned)
+        weights = weight_ref[:, cols]
+        conv_out = jnp.dot(
+            windows[...], weights, preferred_element_type=jnp.float32
+        ).reshape(tokens, -1, CHUNK)
+        pooled_lse = lse_ref[:, cols]
+        pooled_pre = pooled_lse - count_ref[0:1, cols]
+        squashed = jax.nn.sigmoid(pooled_pre)
+        upstream = (
+            upstream_ref[:, cols].astype(jnp.float32)
+            * squashed
+            * (1.0 + pooled_pre * (1.0 - squashed))
         )
-        return jnp.concatenate(pieces, axis=1)
-
-    return lax.map(pool_block, blocks).reshape(char_ids.shape[0] * char_ids.shape[1], bank_cols)
-
-
-def bank_grads(bank_specs, char_ids, char_table, kernel, bias_vec, pooled_grad):
-    group_size = block_group(char_ids.shape[0])
-    block_count = char_ids.shape[0] // group_size
-    blocks = char_ids.reshape(block_count, group_size * char_ids.shape[1], char_ids.shape[2])
-    grad_blocks = pooled_grad.reshape(
-        block_count, group_size * char_ids.shape[1], pooled_grad.shape[1]
-    )
-    kernel_width, embed_dims, bank_cols = kernel.shape
-
-    def grad_block(totals, sliced):
-        grad_kernel, grad_bias, grad_table = totals
-        block_ids, block_grad = sliced
-        embedded, selector = embed_chars(block_ids, char_table)
-        row_count, char_count = block_ids.shape
-        grad_embedded = jnp.zeros((row_count, char_count, embed_dims), jnp.float32)
-        for filter_width, first_col, columns in bank_specs:
-            windows, weights, conv_out = conv_outputs(
-                embedded, kernel, bias_vec, filter_width, first_col, columns
-            )
-            positions = conv_out.shape[1]
-            pooled_lse = log_sum_exp(conv_out)
-            softened = jnp.exp(conv_out - pooled_lse[:, None, :])
-            pooled_pre = pooled_lse - math.log(positions)
-            squashed = jax.nn.sigmoid(pooled_pre)
-            upstream = (
-                block_grad[:, first_col : first_col + columns].astype(jnp.float32)
-                * squashed
-                * (1.0 + pooled_pre * (1.0 - squashed))
-            )
-            grad_conv = (
-                (softened * upstream[:, None, :])
-                .astype(jnp.bfloat16)
-                .reshape(row_count * positions, columns)
-            )
-            part_kernel = outer_sum(windows, grad_conv).reshape(filter_width, embed_dims, columns)
-            grad_kernel = grad_kernel + jnp.pad(
-                part_kernel,
-                (
-                    (0, kernel_width - filter_width),
-                    (0, 0),
-                    (first_col, bank_cols - first_col - columns),
-                ),
-            )
-            grad_bias = grad_bias + jnp.pad(
-                column_sum(grad_conv), (first_col, bank_cols - first_col - columns)
-            )
-            grad_windows = transposed(grad_conv, weights).reshape(
-                row_count, positions, filter_width, embed_dims
-            )
-            for offset in range(filter_width):
-                grad_embedded = grad_embedded + jnp.pad(
-                    grad_windows[:, :, offset, :],
-                    ((0, 0), (offset, char_count - positions - offset), (0, 0)),
-                )
-        grad_table = grad_table + jnp.einsum(
-            "tcv,tcd->vd",
-            selector.astype(jnp.float32),
-            grad_embedded,
-            precision=lax.Precision.HIGHEST,
+        softened = jnp.exp(conv_out - pooled_lse[:, None, :])
+        grad_conv = (softened * upstream[:, None, :]).astype(jnp.bfloat16)
+        places_here = grad_conv.shape[1]
+        grad_conv = grad_conv.reshape(tokens * places_here, CHUNK)
+        grad_weight_ref[:, cols] += jnp.dot(turned, grad_conv, preferred_element_type=jnp.float32)
+        part = lax.dot_general(
+            grad_conv, weights, (((1,), (1,)), ((), ())), preferred_element_type=jnp.float32
+        ).reshape(tokens, places_here, lanes)
+        spread[:, :places_here, :] += part
+    rows = tokens * places
+    flat = spread[...].reshape(rows, lanes)
+    lane = lax.broadcasted_iota(jnp.int32, (rows, lanes), 1)
+    aligned = jnp.where(lane < EMBED, flat, 0.0)
+    for offset in range(1, WIDEST):
+        aligned = jnp.where(lane // EMBED == offset, shift_rows(flat, offset), aligned)
+    aligned_ref[...] = aligned.reshape(tokens, places, lanes)
+
+
+def filter_matrix(conv_weight, conv_bias):
+    bank_cols = conv_bias.shape[1]
+    taps, biases, masks, counts = [], [], [], []
+    for filter_width, bank_index, first_col, count in filter_columns(bank_cols):
+        piece = conv_weight[bank_index, :filter_width, :, first_col : first_col + count]
+        piece = piece.reshape(filter_width * EMBED, count)
+        taps.append(jnp.pad(piece, ((0, TAPS - filter_width * EMBED), (0, 0))))
+        biases.append(conv_bias[bank_index, first_col : first_col + count])
+        rows = lax.broadcasted_iota(jnp.int32, (LANES - TAPS - 1, count), 0)
+        masks.append(jnp.where(rows == WIDEST - filter_width, -1e30, 0.0).astype(jnp.bfloat16))
+        counts.append(jnp.full((8, count), math.log(CHAR_COUNT - filter_width + 1), jnp.float32))
+    weights = jnp.concatenate(
+        [
+            jnp.concatenate(taps, axis=1),
+            jnp.concatenate(biases)[None],
+            jnp.concatenate(masks, axis=1),
+        ],
+        axis=0,
+    )
+    return (weights, jnp.concatenate(counts, axis=1))
+
+
+def wide_columns(bank_cols):
+    total = sum(count for width, bank, first, count in filter_columns(bank_cols) if CHAR_COUNT - width + 1 > TIGHT - 2)
+    return -(-total // CHUNK) * CHUNK
+
+
+def char_selector(token_ids, vocab_size):
+    return token_ids.reshape(-1)[:, None] == lax.broadcasted_iota(jnp.int32, (1, vocab_size), 1)
+
+
+def pool_tokens(token_ids, char_table, weights, counts, tight_from):
+    tokens = token_ids.shape[0]
+    padded = jnp.pad(token_ids, ((0, 0), (0, PLACES - token_ids.shape[1])), constant_values=-1)
+    table_tiled = jnp.pad(jnp.tile(char_table, (1, WIDEST)), ((0, 0), (0, LANES - TAPS)))
+    selector = char_selector(padded, char_table.shape[0]).astype(jnp.bfloat16)
+    tiled = jnp.dot(selector, table_tiled, preferred_element_type=jnp.float32)
+    tiled = tiled.astype(jnp.bfloat16).reshape(tokens, PLACES, LANES)
+    block = math.gcd(tokens, TOKEN_BLOCK)
+    total = weights.shape[1]
+    features, pooled_lse = pl.pallas_call(
+        partial(pool_kernel, tight_from),
+        grid=(tokens // block,),
+        in_specs=[
+            pl.BlockSpec((block, PLACES, LANES), lambda i: (i, 0, 0)),
+            pl.BlockSpec((LANES, total), lambda i: (0, 0)),
+            pl.BlockSpec((8, total), lambda i: (0, 0)),
+        ],
+        out_specs=[
+            pl.BlockSpec((block, total), lambda i: (i, 0)),
+            pl.BlockSpec((block, total), lambda i: (i, 0)),
+        ],
+        out_shape=[
+            jax.ShapeDtypeStruct((tokens, total), jnp.bfloat16),
+            jax.ShapeDtypeStruct((tokens, total), jnp.float32),
+        ],
+        scratch_shapes=[
+            pltpu.VMEM((block * PLACES, LANES), jnp.bfloat16),
+            pltpu.VMEM((block * TIGHT, LANES), jnp.bfloat16),
+        ],
+        compiler_params=pltpu.CompilerParams(vmem_limit_bytes=40 * 1024 * 1024),
+        name="pool_tokens",
+    )(tiled, weights, counts)
+    return (padded, tiled, features, pooled_lse)
+
+
+def pool_grads(padded, tiled, weights, counts, pooled_lse, upstream, vocab_size, tight_from):
+    tokens = tiled.shape[0]
+    block = math.gcd(tokens, TOKEN_BLOCK)
+    total = weights.shape[1]
+    grad_weight, aligned = pl.pallas_call(
+        partial(pool_grad_kernel, tight_from),
+        grid=(tokens // block,),
+        in_specs=[
+            pl.BlockSpec((block, PLACES, LANES), lambda i: (i, 0, 0)),
+            pl.BlockSpec((LANES, total), lambda i: (0, 0)),
+            pl.BlockSpec((8, total), lambda i: (0, 0)),
+            pl.BlockSpec((block, total), lambda i: (i, 0)),
+            pl.BlockSpec((block, total), lambda i: (i, 0)),
+        ],
+        out_specs=[
+            pl.BlockSpec((LANES, total), lambda i: (0, 0)),
+            pl.BlockSpec((block, PLACES, LANES), lambda i: (i, 0, 0)),
+        ],
+        out_shape=[
+            jax.ShapeDtypeStruct((LANES, total), jnp.float32),
+            jax.ShapeDtypeStruct((tokens, PLACES, LANES), jnp.float32),
+        ],
+        scratch_shapes=[
+            pltpu.VMEM((block * PLACES, LANES), jnp.bfloat16),
+            pltpu.VMEM((block * TIGHT, LANES), jnp.bfloat16),
+            pltpu.VMEM((block, PLACES, LANES), jnp.float32),
+        ],
+        compiler_params=pltpu.CompilerParams(vmem_limit_bytes=40 * 1024 * 1024),
+        name="pool_grads",
+    )(tiled, weights, counts, pooled_lse, upstream)
+    aligned = aligned.reshape(tokens * PLACES, LANES)
+    selector = char_selector(padded, vocab_size).astype(jnp.bfloat16)
+    high = aligned.astype(jnp.bfloat16)
+    low = (aligned - high.astype(jnp.float32)).astype(jnp.bfloat16)
+    by_tap = outer_sum(selector, high) + outer_sum(selector, low)
+    grad_table = by_tap[:, :TAPS].reshape(vocab_size, WIDEST, EMBED).sum(axis=1)
+    return (grad_weight, grad_table)
+
+
+def split_banks(grad_weight, bank_cols):
+    taps = grad_weight[:TAPS].reshape(WIDEST, EMBED, -1)
+    bias_row = grad_weight[TAPS]
+    kernels, biases, at = [], [], 0
+    for bank_specs in bank_plan(bank_cols):
+        pieces, bias_pieces, used = [], [], 0
+        for filter_width, first_col, count in bank_specs:
+            piece = taps[:filter_width, :, at : at + count]
+            pieces.append(jnp.pad(piece, ((0, WIDEST - filter_width), (0, 0), (0, 0))))
+            bias_pieces.append(bias_row[at : at + count])
+            at += count
+            used += count
+        kernels.append(
+            jnp.pad(jnp.concatenate(pieces, axis=2), ((0, 0), (0, 0), (0, bank_cols - used)))
         )
-        return ((grad_kernel, grad_bias, grad_table), None)
-
-    initial = (
-        jnp.zeros(kernel.shape, jnp.float32),
-        jnp.zeros((bank_cols,), jnp.float32),
-        jnp.zeros(char_table.shape, jnp.float32),
-    )
-    return lax.scan(grad_block, initial, (blocks, grad_blocks))[0]
+        biases.append(jnp.pad(jnp.concatenate(bias_pieces), (0, bank_cols - used)))
+    return (jnp.stack(kernels), jnp.stack(biases))
 
 
 def gate_parts(gates_pre, cell_width):
@@ -275,6 +388,12 @@
     return (grad_input, grad_weight, grad_bias, grad_proj)
 
 
+def scatter_sum(values, axes, scatter_dimension, tiled):
+    return lax.psum_scatter(
+        values.astype(jnp.bfloat16), axes, scatter_dimension=scatter_dimension, tiled=tiled
+    ).astype(jnp.float32)
+
+
 def shards(
     char_ids,
     resets,
@@ -292,9 +411,6 @@
 ):
     own_streams, step_count = resets.shape
     bank_cols = conv_weight.shape[3]
-    bank_layout = bank_plan(bank_cols)
-    widths_used = [used_columns(bank_specs) for bank_specs in bank_layout]
-    bank_count = lax.axis_size("bank")
     (
         highway_full,
         highway_bias_full,
@@ -312,19 +428,15 @@
         lax.all_gather(lstm_bias[0], ("dp", "bank"), axis=0, tiled=True),
         lax.all_gather(lstm_proj[0], ("dp", "bank"), axis=1, tiled=True),
     )
-    branches = [partial(bank_pool, bank_specs) for bank_specs in bank_layout]
-    pooled = lax.switch(
-        lax.axis_index("bank"), branches, char_ids, char_table, conv_weight[0], conv_bias[0]
-    )
-    received = lax.all_to_all(
-        pooled.astype(jnp.bfloat16), "bank", split_axis=0, concat_axis=1, tiled=True
-    )
-    features = jnp.concatenate(
-        [
-            received[:, bank_index * bank_cols : bank_index * bank_cols + widths_used[bank_index]]
-            for bank_index in range(bank_count)
-        ],
-        axis=1,
+    conv_weight_all = lax.all_gather(conv_weight, "bank", axis=0, tiled=True)
+    conv_bias_all = lax.all_gather(conv_bias, "bank", axis=0, tiled=True)
+    own_ids = lax.dynamic_slice_in_dim(
+        char_ids, lax.axis_index("bank") * own_streams, own_streams, axis=0
+    ).reshape(own_streams * step_count, char_ids.shape[2])
+    filters, counts = filter_matrix(conv_weight_all, conv_bias_all)
+    tight_from = wide_columns(bank_cols)
+    padded_ids, tiled, features, pooled_lse = pool_tokens(
+        own_ids, char_table, filters, counts, tight_from
     )
     feature_count = features.shape[1]
     hidden_f32 = features.astype(jnp.float32)
@@ -366,9 +478,9 @@
         False,
     )
     shard_first = (
-        lax.psum_scatter(results_first[1], ("dp", "bank"), scatter_dimension=0, tiled=True),
+        scatter_sum(results_first[1], ("dp", "bank"), scatter_dimension=0, tiled=True),
         lax.psum_scatter(results_first[2], ("dp", "bank"), scatter_dimension=0, tiled=True),
-        lax.psum_scatter(results_first[3], ("dp", "bank"), scatter_dimension=1, tiled=True),
+        scatter_sum(results_first[3], ("dp", "bank"), scatter_dimension=1, tiled=True),
     )
     lstm_second, bias_second, proj_second = (
         lax.all_gather(lstm_weight[1], ("dp", "bank"), axis=0, tiled=True),
@@ -408,40 +520,29 @@
         grad_hidden = grad_hidden * carry_gate + transposed(grad_mixed, highway_full[highway_level])
     grad_features = grad_hidden.astype(jnp.bfloat16)
     shard_last = (
-        lax.psum_scatter(results_second[1], ("dp", "bank"), scatter_dimension=0, tiled=True),
+        scatter_sum(results_second[1], ("dp", "bank"), scatter_dimension=0, tiled=True),
         lax.psum_scatter(results_second[2], ("dp", "bank"), scatter_dimension=0, tiled=True),
-        lax.psum_scatter(results_second[3], ("dp", "bank"), scatter_dimension=1, tiled=True),
-        lax.psum_scatter(jnp.stack(weight_levels), ("dp", "bank"), scatter_dimension=1, tiled=True),
+        scatter_sum(results_second[3], ("dp", "bank"), scatter_dimension=1, tiled=True),
+        scatter_sum(jnp.stack(weight_levels), ("dp", "bank"), scatter_dimension=1, tiled=True),
         lax.psum_scatter(jnp.stack(bias_levels), ("dp", "bank"), scatter_dimension=1, tiled=True),
-        lax.psum_scatter(grad_project_w, ("dp", "bank"), scatter_dimension=0, tiled=True),
+        scatter_sum(grad_project_w, ("dp", "bank"), scatter_dimension=0, tiled=True),
         lax.psum_scatter(grad_project_b, ("dp", "bank"), scatter_dimension=0, tiled=True),
     )
-    col_starts = [sum(widths_used[:bank_index]) for bank_index in range(bank_count)]
-    bank_pieces = [
-        jnp.pad(
-            grad_features[
-                :, col_starts[bank_index] : col_starts[bank_index] + widths_used[bank_index]
-            ],
-            ((0, 0), (0, bank_cols - widths_used[bank_index])),
-        )
-        for bank_index in range(bank_count)
-    ]
-    returned = lax.all_to_all(
-        jnp.concatenate(bank_pieces, axis=1), "bank", split_axis=1, concat_axis=0, tiled=True
-    )
-    branches_back = [partial(bank_grads, bank_specs) for bank_specs in bank_layout]
-    grad_kernel, grad_bias, grad_table = lax.switch(
-        lax.axis_index("bank"),
-        branches_back,
-        char_ids,
-        char_table,
-        conv_weight[0],
-        conv_bias[0],
-        returned,
-    )
-    grad_kernel = grad_kernel[None]
-    grad_bias = grad_bias[None]
-    grad_kernel, grad_bias = lax.psum((grad_kernel, grad_bias), "dp")
+    grad_filters, grad_table = pool_grads(
+        padded_ids,
+        tiled,
+        filters,
+        counts,
+        pooled_lse,
+        grad_features,
+        char_table.shape[0],
+        tight_from,
+    )
+    grad_kernel, grad_bias = split_banks(grad_filters, bank_cols)
+    grad_kernel = lax.psum(
+        lax.psum_scatter(grad_kernel, "bank", scatter_dimension=0, tiled=True), "dp"
+    )
+    grad_bias = lax.psum(lax.psum_scatter(grad_bias, "bank", scatter_dimension=0, tiled=True), "dp")
     grad_table = lax.psum(grad_table, ("dp", "bank"))
     lstm_weight_grad = jnp.stack([shard_first[0], shard_last[0]])
     lstm_bias_grad = jnp.stack([shard_first[1], shard_last[1]])

time: 3950 us -> 2940 us (0.74)
  blocking collectives: 855 us -> 229 us
  waiting for transfers between devices: 1470 us -> 2000 us
  other arithmetic: 452 us -> 140 us
  matrix products: 617 us -> 384 us
  local copies, waits for them, and re-layouts: 336 us -> 112 us
  starting transfers between devices: 158 us -> 1.11 us
  Pallas kernels: 0 us -> 47.8 us
    psum x1, blocking collectives: 665 us -> 42.6 us  [shards(): grad_table = lax.psum(grad_table, ('dp', 'bank'))]
    reduce_scatter x6 -> x7, waiting for transfers between devices: 1330 us -> 1560 us  [the longest x6 1500 us: scatter_sum(): lax.psum_scatter(values.astype(jnp.bfloat16), axes, scatter_dimension=sca...]
    dot_general x160 -> x1, matrix products: 171 us -> 1.94 us  [pool_tokens(): tiled = jnp.dot(selector, table_tiled, preferred_element_type=jnp.float32)]
    all_to_all x1 -> x0, starting transfers between devices: 156 us -> none  [shards(): lax.all_to_all(pooled.astype(jnp.bfloat16), 'bank', split_axis=0, concat_...]
    all_gather x1, waiting for transfers between devices: 56.4 us -> 194 us  [shards(): lax.all_gather(lstm_weight[0], ('dp', 'bank'), axis=0, tiled=True)]
    all_gather x1, waiting for transfers between devices: 0.01 us -> 116 us  [shards(): lax.all_gather(highway_weight, ('dp', 'bank'), axis=1, tiled=True)]
    convert_element_type x96 -> x10, other arithmetic: 120 us -> 7.04 us  [the longest x2 4.26 us: scatter_sum(): return lax.psum_scatter(values.astype(jnp.bfloat16), axes, scatter_dimens...]
    add x64 -> x1, other arithmetic: 100 us -> 0.02 us  [pool_grads(): by_tap = outer_sum(selector, high) + outer_sum(selector, low)]
  transfers between devices with their start and end apart: 16 -> 16, of which waited for: 6 -> 13; matrix products, arithmetic and copies ran while one was open for 30% -> 13% of each run, Pallas kernels for 0% -> 1%
where the time goes in v1:
time: 2940 us; the launch traced here: 2930 us
  waiting for transfers between devices  2000 us (68%)
  matrix products  384 us (13%)
  blocking collectives  229 us (8%)
  other arithmetic  140 us (5%)
  local copies, waits for them, and re-layouts  112 us (4%)
  Pallas kernels  47.8 us (2%)
    reduce_scatter x6, waiting for transfers between devices, scatter_sum(): lax.psum_scatter(values.astype(jnp.bfloat16), axes, scatter_dimension=sca...  1500 us
    all_gather x1, waiting for transfers between devices, shards(): lax.all_gather(lstm_weight[0], ('dp', 'bank'), axis=0, tiled=True)  194 us
    dot_general x21, matrix products, transposed(): lax.dot_general(former, latter, (((1,), (1,)), ((), ())), preferred_eleme...  172 us
    all_gather x1, waiting for transfers between devices, shards(): lax.all_gather(highway_weight, ('dp', 'bank'), axis=1, tiled=True)  116 us
    dot_general x8, matrix products, forward_step(): jnp.dot(state_start, weight_rec, preferred_element_type=jnp.float32)  87.6 us
    psum x1, waiting for transfers between devices, shards(): lax.psum(lax.psum_scatter(grad_kernel, 'bank', scatter_dimension=0, tiled...  73.5 us
    dot_general x11, matrix products, outer_sum(): lax.dot_general(former, latter, (((0,), (0,)), ((), ())), preferred_eleme...  72.3 us
  transfers between devices with their start and end apart: 16, of which 13 were waited for; matrix products, arithmetic and copies ran while one was open for 13% of the time, Pallas kernels for 1%

profile of v1, /device:TPU:14, one launch (start us, length us, event | category | flops | bytes accessed | tf_op | source)
XLA Modules:
  0.0 2928.7 jit_solution(11758859529298160288)
XLA Ops:
  30.4 41.5 %all-reduce.21 = bf16[512]{0:T(512)(128)(2,1)S(1)} all-reduce(bf16[512]{0:T(512)(128)(2,1)S(1)} %dynamic-update-slice), channel_id=1, replica_groups=mesh['dp'=8,'bank'=4] {'dp','bank'}, use_global_device_ids=true, to_apply=%add.21 | all-reduce | flops 512 | bytes 2048
  71.9 29.0 all-gather.1
  100.9 38.7 %all-gather.4 = bf16[1,16384]{1,0:T(2,128)(2,1)S(1)} all-gather(bf16[1,512]{1,0:T(2,128)(2,1)S(1)} %get-tuple-element.1094), channel_id=6, replica_groups=mesh['dp'=8,'bank'=4] {'dp','bank'}, dimensions={1}, use_global_device_ids=true | all-gather | bytes 33792 | tf_op jit(solution)/shard_map/all_gather | solution.py:487
  165.5 36.5 %all_gather.39 = bf16[2,4096]{1,0:T(2,128)(2,1)S(1)} all-gather(bf16[2,128]{1,0:T(2,128)(2,1)S(1)} %copy-done.59), channel_id=1, replica_groups=mesh['dp'=8,'bank'=4] {'dp','bank'}, dimensions={1}, use_global_device_ids=true | all-gather | bytes 16896 | tf_op jit(solution)/shard_map/all_gather | solution.py:424
  216.8 115.8 %all-gather.14.cloned.1.call-done = bf16[2,2048,4096]{2,1,0:T(8,128)(2,1)} async-done(((bf16[2,64,4096]{2,1,0:T(8,128)(2,1)}), bf16[2,2048,4096]{2,1,0:T(8,128)(2,1)}) %all-gather.14.cloned.1.call-update) | async-done | bytes 33554448 | tf_op jit(solution)/shard_map/all_gather | solution.py:423
  349.9 41.2 %all-gather.16.cloned.1.call-done = bf16[2048,512]{1,0:T(8,128)(2,1)} async-done(((bf16[64,512]{1,0:T(8,128)(2,1)}), bf16[2048,512]{1,0:T(8,128)(2,1)}) %all-gather.16.cloned.1.call-update) | async-done | bytes 2097168 | tf_op jit(solution)/shard_map/all_gather | solution.py:425
  393.3 193.6 %all-gather.18.cloned.1.call-done = bf16[1,1024,16384]{2,1,0:T(8,128)(2,1)} async-done(((bf16[1,32,16384]{2,1,0:T(8,128)(2,1)}), bf16[1,1024,16384]{2,1,0:T(8,128)(2,1)}) %all-gather.18.cloned.1.call-update) | async-done | bytes 33554448 | tf_op jit(solution)/shard_map/all_gather | solution.py:427
  619.3 56.4 %while.88 = (s32[]{:T(128)}, f32[32,4096]{1,0:T(8,128)S(1)}, bf16[32,512]{1,0:T(8,128)(2,1)S(1)}, f32[4,32,16384]{2,1,0:T(8,128)}, f32[4,32,4096]{2,1,0:T(8,128)...) while((s32[]{:T(128)}, f32[32,4096]{1,0:T(8,128)S(1)}, ...), condition=%wide.region_1.2_spmd.clone, body=%wide.region_0.1_spmd.clone.sunk | while | flops 674398272 | bytes 49350344 | solution.py:356
  678.8 89.2 %while.89 = (s32[]{:T(128)}, f32[32,4096]{1,0:T(8,128)}, f32[32,512]{1,0:T(8,128)S(1)}, bf16[4,32,16384]{2,1,0:T(8,128)(2,1)}, bf16[4,32,512]{2,1,0:T(8,128)(2,1...) while((s32[]{:T(128)}, f32[32,4096]{1,0:T(8,128)}, ...), condition=%wide.region_3.4_spmd.clone, body=%wide.region_2.3_spmd.clone.sunk | while | flops 686833664 | bytes 39125700 | solution.py:367
  814.7 56.3 %while.90 = (s32[]{:T(128)}, f32[32,4096]{1,0:T(8,128)S(1)}, bf16[32,512]{1,0:T(8,128)(2,1)S(1)}, f32[4,32,16384]{2,1,0:T(8,128)}, f32[4,32,4096]{2,1,0:T(8,128)...) while((s32[]{:T(128)}, f32[32,4096]{1,0:T(8,128)S(1)}, ...), condition=%wide.region_5.6_spmd.clone, body=%wide.region_4.5_spmd.clone.sunk | while | flops 674398272 | bytes 49350364 | solution.py:356
  874.0 86.2 %while.91 = (s32[]{:T(128)}, f32[32,4096]{1,0:T(8,128)}, f32[32,512]{1,0:T(8,128)S(1)}, bf16[4,32,16384]{2,1,0:T(8,128)(2,1)}, bf16[4,32,512]{2,1,0:T(8,128)(2,1...) while((s32[]{:T(128)}, f32[32,4096]{1,0:T(8,128)}, ...), condition=%wide.region_7.8_spmd.clone, body=%wide.region_6.7_spmd.clone.sunk | while | flops 686833664 | bytes 39125680 | solution.py:367
  1014.7 28.1 pool_grads.1
  1085.7 22.9 pad_maximum_fusion.2
  1129.6 23.3 pad_maximum_fusion.1
  1171.4 22.9 pad_maximum_fusion
  1203.4 42.6 %all-reduce.26 = (f32[262,16]{0,1:T(8,128)}, f32[512]{0:T(512)S(1)}) all-reduce(f32[262,16]{0,1:T(8,128)S(1)} %reduce_sum.9, f32[512]{0:T(512)S(1)} %bitcast.416), channel_id=1, replica_groups=mesh['dp'=8,'bank'=4] {'dp','bank'}, use_global_device_ids=true, to_apply=%region_9.10 | all-reduce | flops 4704 | bytes 37632 | tf_op jit(solution)/shard_map/psum | solution.py:546
  1280.2 58.0 %reduce-scatter.11.cloned.1.call-done = f32[1,7,16,1024]{3,2,1,0:T(8,128)} async-done(((f32[4,7,16,1024]{3,2,1,0:T(8,128)}), f32[1,7,16,1024]{3,2,1,0:T(8,128)}) %reduce-scatter.11.cloned.1.call-update) | async-done | bytes 458768 | tf_op jit(solution)/shard_map/reduce_scatter | solution.py:543
  1338.3 107.3 %reduce-scatter.15.cloned.1.call-done = bf16[64,512]{1,0:T(8,128)(2,1)} async-done(((bf16[2048,512]{1,0:T(8,128)(2,1)}), bf16[64,512]{1,0:T(8,128)(2,1)}) %reduce-scatter.15.cloned.1.call-update) | async-done | bytes 65552 | tf_op jit(solution)/shard_map/reduce_scatter | solution.py:392
  1447.0 137.3 %reduce-scatter.23.cloned.1.call-done = bf16[4096,16]{0,1:T(8,128)(2,1)} async-done(((bf16[4096,512]{0,1:T(8,128)(2,1)}), bf16[4096,16]{0,1:T(8,128)(2,1)}) %reduce-scatter.23.cloned.1.call-update) | async-done | bytes 131088 | tf_op jit(solution)/shard_map/reduce_scatter | solution.py:392
  1584.3 139.1 %reduce-scatter.21.cloned.1.call-done = bf16[4096,16]{0,1:T(8,128)(2,1)} async-done(((bf16[4096,512]{0,1:T(8,128)(2,1)}), bf16[4096,16]{0,1:T(8,128)(2,1)}) %reduce-scatter.21.cloned.1.call-update) | async-done | bytes 131088 | tf_op jit(solution)/shard_map/reduce_scatter | solution.py:392
  1725.2 390.1 %reduce-scatter.19.cloned.1.call-done = bf16[32,16384]{1,0:T(8,128)(2,1)} async-done(((bf16[1024,16384]{1,0:T(8,128)(2,1)}), bf16[32,16384]{1,0:T(8,128)(2,1)}) %reduce-scatter.19.cloned.1.call-update) | async-done | bytes 1048592 | tf_op jit(solution)/shard_map/reduce_scatter | solution.py:392
  2115.3 364.2 %reduce-scatter.17.cloned.1.call-done = bf16[32,16384]{1,0:T(8,128)(2,1)} async-done(((bf16[1024,16384]{1,0:T(8,128)(2,1)}), bf16[32,16384]{1,0:T(8,128)(2,1)}) %reduce-scatter.17.cloned.1.call-update) | async-done | bytes 1048592 | tf_op jit(solution)/shard_map/reduce_scatter | solution.py:392
  2483.3 360.4 %reduce-scatter.13.cloned.1.call-done = bf16[2,64,4096]{2,1,0:T(8,128)(2,1)} async-done(((bf16[2,2048,4096]{2,1,0:T(8,128)(2,1)}), bf16[2,64,4096]{2,1,0:T(8,128)(2,1)}) %reduce-scatter.13.cloned.1.call-update) | async-done | bytes 1048592 | tf_op jit(solution)/shard_map/reduce_scatter | solution.py:392
  2846.4 73.5 %all-reduce.31.cloned.1.call-done = f32[1,7,16,1024]{3,2,1,0:T(8,128)} async-done(((f32[1,7,16,1024]{3,2,1,0:T(8,128)}), f32[1,7,16,1024]{3,2,1,0:T(8,128)}) %all-reduce.31.cloned.1.call-update) | async-done | bytes 458768 | tf_op jit(solution)/shard_map/psum | solution.py:542
  (447 shorter events, 646.6 us)
Async XLA Ops:
  7.2 196.1 %all-gather.20.cloned.1.call-start = ((), (), s32[]{:S(2)}) async-start(), calls=%async_computation.19 | async-start | bytes 4325376 | tf_op jit(solution)/shard_map/all_gather | solution.py:429
  9.0 201.3 %all-gather.24.cloned.1.call-start = ((), (), s32[]{:S(2)}) async-start(), calls=%async_computation.21 | async-start | bytes 4325376 | tf_op jit(solution)/shard_map/all_gather | solution.py:488
  9.8 322.8 %all-gather.14.cloned.1.call-start = ((), (), s32[]{:S(2)}) async-start(), calls=%async_computation.8 | async-start | bytes 34603008 | tf_op jit(solution)/shard_map/all_gather | solution.py:423
  10.5 380.6 %all-gather.16.cloned.1.call-start = ((), (), s32[]{:S(2)}) async-start(), calls=%async_computation.9 | async-start | bytes 2162688 | tf_op jit(solution)/shard_map/all_gather | solution.py:425
  11.2 129.2 %copy-start.57 = (s32[32,4]{0,1:T(4,128)S(1)}, s32[32,4]{0,1:T(4,128)}, u32[]{:S(2)}) copy-start(s32[32,4]{0,1:T(4,128)} %param.22) | copy-start | bytes 1540
  11.2 575.7 %all-gather.18.cloned.1.call-start = ((), (), s32[]{:S(2)}) async-start(), calls=%async_computation.18 | async-start | bytes 34603008 | tf_op jit(solution)/shard_map/all_gather | solution.py:427
  14.2 127.1 %copy-start.54 = (bf16[262,16]{0,1:T(8,128)(2,1)S(1)}, bf16[262,16]{0,1:T(8,128)(2,1)}, u32[]{:S(2)}) copy-start(bf16[262,16]{0,1:T(8,128)(2,1)} %param.24) | copy-start | bytes 25156
  14.3 768.4 %all-gather.22.cloned.1.call-start = ((), (), s32[]{:S(2)}) async-start(), calls=%async_computation.20 | async-start | bytes 34603008 | tf_op jit(solution)/shard_map/all_gather | solution.py:486
  14.8 1261.5 %all-reduce.33.cloned.1.call-start = ((), (), s32[]{:S(2)}) async-start(), calls=%async_computation.23 | async-start | bytes 262144
  24.5 118.8 %copy-start.52 = (s32[8192]{0:T(1024)}, s32[8192]{0:T(1024)S(1)}, u32[]{:S(2)}) copy-start(s32[8192]{0:T(1024)S(1)} %eq.71) | copy-start | bytes 98308
  165.5 174.2 %copy-start.7 = (bf16[128,2048]{1,0:T(8,128)(2,1)}, bf16[128,2048]{1,0:T(8,128)(2,1)S(1)}, u32[]{:S(2)}) copy-start(bf16[128,2048]{1,0:T(8,128)(2,1)S(1)} %get-tuple-element.621) | copy-start | bytes 1572868
  349.9 248.8 %copy-start.26 = (bf16[128,2048]{1,0:T(8,128)(2,1)}, bf16[128,2048]{1,0:T(8,128)(2,1)S(1)}, u32[]{:S(2)}) copy-start(bf16[128,2048]{1,0:T(8,128)(2,1)S(1)} %add_convert_fusion) | copy-start | bytes 1572868
  393.2 205.4 %copy-start.29 = (bf16[32,4,512]{2,1,0:T(4,128)(2,1)}, bf16[32,4,512]{2,1,0:T(4,128)(2,1)S(1)}, u32[]{:S(2)}) copy-start(bf16[32,4,512]{2,1,0:T(4,128)(2,1)S(1)} %reshape.282) | copy-start | bytes 393220
  393.3 205.4 %copy-start.49 = (bf16[32,4,512]{2,0,1:T(8,128)(2,1)}, bf16[32,4,512]{2,0,1:T(8,128)(2,1)S(1)}, u32[]{:S(2)}) copy-start(bf16[32,4,512]{2,0,1:T(8,128)(2,1)S(1)} %copy.55) | copy-start | bytes 393220
  1048.3 230.4 %reduce-scatter.25.cloned.1.call-start = ((), (), s32[]{:S(2)}) async-start(), calls=%async_computation.22 | async-start | bytes 2162688
  1050.6 287.6 %reduce-scatter.11.cloned.1.call-start = ((), (), s32[]{:S(2)}) async-start(), calls=%async_computation.10 | async-start | bytes 2293760 | tf_op jit(solution)/shard_map/reduce_scatter | solution.py:543
  1052.0 393.5 %reduce-scatter.15.cloned.1.call-start = ((), (), s32[]{:S(2)}) async-start(), calls=%async_computation.13 | async-start | bytes 2162688 | tf_op jit(solution)/shard_map/reduce_scatter | solution.py:392
  1054.2 530.2 %reduce-scatter.23.cloned.1.call-start = ((), (), s32[]{:S(2)}) async-start(), calls=%async_computation.17 | async-start | bytes 4325376 | tf_op jit(solution)/shard_map/reduce_scatter | solution.py:392
  1058.5 664.9 %reduce-scatter.21.cloned.1.call-start = ((), (), s32[]{:S(2)}) async-start(), calls=%async_computation.16 | async-start | bytes 4325376 | tf_op jit(solution)/shard_map/reduce_scatter | solution.py:392
  1064.0 1051.3 %reduce-scatter.19.cloned.1.call-start = ((), (), s32[]{:S(2)}) async-start(), calls=%async_computation.15 | async-start | bytes 34603008 | tf_op jit(solution)/shard_map/reduce_scatter | solution.py:392
  1108.7 1370.8 %reduce-scatter.17.cloned.1.call-start = ((), (), s32[]{:S(2)}) async-start(), calls=%async_computation.14 | async-start | bytes 34603008 | tf_op jit(solution)/shard_map/reduce_scatter | solution.py:392
  1153.0 1690.7 %reduce-scatter.13.cloned.1.call-start = ((), (), s32[]{:S(2)}) async-start(), calls=%async_computation.12 | async-start | bytes 34603008 | tf_op jit(solution)/shard_map/reduce_scatter | solution.py:392
  1194.3 1725.6 %all-reduce.31.cloned.1.call-start = ((), (), s32[]{:S(2)}) async-start(), calls=%async_computation.11 | async-start | bytes 917504 | tf_op jit(solution)/shard_map/psum | solution.py:542
  2479.5 442.3 %copy-start.1 = (s32[128,4,50]{0,1,2:T(4,128)S(1)}, s32[128,4,50]{0,1,2:T(4,128)}, u32[]{:S(2)}) copy-start(s32[128,4,50]{0,1,2:T(4,128)} %param.21) | copy-start | bytes 307204
  (60 other events, 664.9 us)
Sparse Core Ops, SparseCore 0:
  11.5 62.3 all-gather.19
  77.3 60.6 all-gather.23
  140.9 191.6 all-gather.13
  335.3 55.7 all-gather.15
  394.4 192.4 all-gather.17
  589.6 192.9 all-gather.21
  1048.5 122.7 all-reduce.32
  1174.1 104.5 reduce-scatter.24
  1281.5 56.7 reduce-scatter.10
  1340.3 105.1 reduce-scatter.14
  1447.9 136.3 reduce-scatter.22
  1586.5 136.7 reduce-scatter.20
  1725.8 389.4 reduce-scatter.18
  2117.5 361.8 reduce-scatter.16
  2481.7 361.9 reduce-scatter.12
  2847.3 72.5 all-reduce.30

commit v2 on v1

v2 whole, which is shorter than its diff:
```python
from functools import partial
import math

import jax
import jax.numpy as jnp
from jax import lax
from jax.experimental import pallas as pl
from jax.experimental.pallas import tpu as pltpu
from jax.sharding import Mesh, PartitionSpec as P

CHAR_COUNT = 50
EMBED = 16
WIDEST = 7
TAPS = WIDEST * EMBED
LANES = 128
PLACES = 64
TIGHT = 48
CHUNK = 256
TOKEN_BLOCK = 16


def bank_plan(bank_cols):
    return [
        [
            (1, 0, bank_cols // 32),
            (2, bank_cols // 32, bank_cols // 32),
            (3, bank_cols // 16, bank_cols // 16),
            (4, bank_cols // 8, bank_cols // 8),
        ],
        [(5, 0, bank_cols // 4)],
        [(6, 0, bank_cols // 2)],
        [(7, 0, bank_cols)],
    ]


def transposed(former, latter):
    return lax.dot_general(
        former, latter, (((1,), (1,)), ((), ())), preferred_element_type=jnp.float32
    )


def outer_sum(former, latter):
    return lax.dot_general(
        former, latter, (((0,), (0,)), ((), ())), preferred_element_type=jnp.float32
    )


def column_sum(values):
    ones_row = jnp.ones((1, values.shape[0]), values.dtype)
    return jnp.dot(ones_row, values, preferred_element_type=jnp.float32)[0]


def filter_columns(bank_cols):
    columns = []
    for bank_index, bank_specs in enumerate(bank_plan(bank_cols)):
        for filter_width, first_col, count in bank_specs:
            columns.append((filter_width, bank_index, first_col, count))
    return columns


def shift_rows(values, amount):
    count = values.shape[0]
    return values if amount % count == 0 else pltpu.roll(values, amount % count, 0)


def block_windows(tiled_ref, windows_wide, windows_tight):
    tokens, places, lanes = tiled_ref.shape
    rows = tokens * places
    tiled = tiled_ref[...].astype(jnp.float32).reshape(rows, lanes)
    lane = lax.broadcasted_iota(jnp.int32, (rows, lanes), 1)
    place = lax.broadcasted_iota(jnp.int32, (rows, lanes), 0) % places
    windows = tiled
    for offset in range(1, WIDEST):
        windows = jnp.where(lane // EMBED == offset, shift_rows(tiled, rows - offset), windows)
    late = place >= CHAR_COUNT - WIDEST + 1 + (lane - TAPS - 1)
    extra = jnp.where((lane == TAPS) | ((lane <= TAPS + WIDEST) & late), 1.0, 0.0)
    windows = jnp.where(lane < TAPS, windows, extra)
    windows_wide[...] = windows.astype(jnp.bfloat16)
    windows_tight[...] = (
        windows.reshape(tokens, places, lanes)[:, :TIGHT]
        .reshape(tokens * TIGHT, lanes)
        .astype(jnp.bfloat16)
    )


def column_chunks(total, tight_from):
    return [
        (start, start < tight_from) for start in range(0, total, CHUNK)
    ]


def pool_kernel(tight_from, tiled_ref, weight_ref, count_ref, features_ref, lse_ref, wide, tight):
    tokens, places, lanes = tiled_ref.shape
    block_windows(tiled_ref, wide, tight)
    for start, is_wide in column_chunks(weight_ref.shape[1], tight_from):
        cols = pl.ds(start, CHUNK)
        windows = wide if is_wide else tight
        conv_out = jnp.dot(
            windows[...], weight_ref[:, cols], preferred_element_type=jnp.float32
        ).reshape(tokens, -1, CHUNK)
        highest = jnp.max(conv_out, axis=1)
        total = jnp.sum(jnp.exp(conv_out - highest[:, None, :]), axis=1)
        pooled_lse = highest + jnp.log(total)
        lse_ref[:, cols] = pooled_lse
        pooled_pre = pooled_lse - count_ref[0:1, cols]
        features_ref[:, cols] = (pooled_pre * jax.nn.sigmoid(pooled_pre)).astype(jnp.bfloat16)


def pool_grad_kernel(
    tight_from,
    tiled_ref,
    weight_ref,
    count_ref,
    lse_ref,
    upstream_ref,
    grad_weight_ref,
    aligned_ref,
    wide,
    tight,
    spread,
):
    tokens, places, lanes = tiled_ref.shape
    block_windows(tiled_ref, wide, tight)

    @pl.when(pl.program_id(0) == 0)
    def _():
        grad_weight_ref[...] = jnp.zeros_like(grad_weight_ref)

    spread[...] = jnp.zeros_like(spread)
    wide_turned = wide[...].T
    tight_turned = tight[...].T
    for start, is_wide in column_chunks(weight_ref.shape[1], tight_from):
        cols = pl.ds(start, CHUNK)
        windows, turned = (wide, wide_turned) if is_wide else (tight, tight_turned)
        weights = weight_ref[:, cols]
        conv_out = jnp.dot(
            windows[...], weights, preferred_element_type=jnp.float32
        ).reshape(tokens, -1, CHUNK)
        pooled_lse = lse_ref[:, cols]
        pooled_pre = pooled_lse - count_ref[0:1, cols]
        squashed = jax.nn.sigmoid(pooled_pre)
        upstream = (
            upstream_ref[:, cols].astype(jnp.float32)
            * squashed
            * (1.0 + pooled_pre * (1.0 - squashed))
        )
        softened = jnp.exp(conv_out - pooled_lse[:, None, :])
        grad_conv = (softened * upstream[:, None, :]).astype(jnp.bfloat16)
        places_here = grad_conv.shape[1]
        grad_conv = grad_conv.reshape(tokens * places_here, CHUNK)
        grad_weight_ref[:, cols] += jnp.dot(turned, grad_conv, preferred_element_type=jnp.float32)
        part = lax.dot_general(
            grad_conv, weights, (((1,), (1,)), ((), ())), preferred_element_type=jnp.float32
        ).reshape(tokens, places_here, lanes)
        spread[:, :places_here, :] += part
    rows = tokens * places
    flat = spread[...].reshape(rows, lanes)
    lane = lax.broadcasted_iota(jnp.int32, (rows, lanes), 1)
    aligned = jnp.where(lane < EMBED, flat, 0.0)
    for offset in range(1, WIDEST):
        aligned = jnp.where(lane // EMBED == offset, shift_rows(flat, offset), aligned)
    aligned_ref[...] = aligned.reshape(tokens, places, lanes)


def filter_matrix(conv_weight, conv_bias):
    bank_cols = conv_bias.shape[1]
    taps, biases, masks, counts = [], [], [], []
    for filter_width, bank_index, first_col, count in filter_columns(bank_cols):
        piece = conv_weight[bank_index, :filter_width, :, first_col : first_col + count]
        piece = piece.reshape(filter_width * EMBED, count)
        taps.append(jnp.pad(piece, ((0, TAPS - filter_width * EMBED), (0, 0))))
        biases.append(conv_bias[bank_index, first_col : first_col + count])
        rows = lax.broadcasted_iota(jnp.int32, (LANES - TAPS - 1, count), 0)
        masks.append(jnp.where(rows == WIDEST - filter_width, -1e30, 0.0).astype(jnp.bfloat16))
        counts.append(jnp.full((8, count), math.log(CHAR_COUNT - filter_width + 1), jnp.float32))
    weights = jnp.concatenate(
        [
            jnp.concatenate(taps, axis=1),
            jnp.concatenate(biases)[None],
            jnp.concatenate(masks, axis=1),
        ],
        axis=0,
    )
    return (weights, jnp.concatenate(counts, axis=1))


def wide_columns(bank_cols):
    total = sum(count for width, bank, first, count in filter_columns(bank_cols) if CHAR_COUNT - width + 1 > TIGHT - 2)
    return -(-total // CHUNK) * CHUNK


def char_selector(token_ids, vocab_size):
    return token_ids.reshape(-1)[:, None] == lax.broadcasted_iota(jnp.int32, (1, vocab_size), 1)


def pool_tokens(token_ids, char_table, weights, counts, tight_from):
    tokens = token_ids.shape[0]
    padded = jnp.pad(token_ids, ((0, 0), (0, PLACES - token_ids.shape[1])), constant_values=-1)
    table_tiled = jnp.pad(jnp.tile(char_table, (1, WIDEST)), ((0, 0), (0, LANES - TAPS)))
    selector = char_selector(padded, char_table.shape[0]).astype(jnp.bfloat16)
    tiled = jnp.dot(selector, table_tiled, preferred_element_type=jnp.float32)
    tiled = tiled.astype(jnp.bfloat16).reshape(tokens, PLACES, LANES)
    block = math.gcd(tokens, TOKEN_BLOCK)
    total = weights.shape[1]
    features, pooled_lse = pl.pallas_call(
        partial(pool_kernel, tight_from),
        grid=(tokens // block,),
        in_specs=[
            pl.BlockSpec((block, PLACES, LANES), lambda i: (i, 0, 0)),
            pl.BlockSpec((LANES, total), lambda i: (0, 0)),
            pl.BlockSpec((8, total), lambda i: (0, 0)),
        ],
        out_specs=[
            pl.BlockSpec((block, total), lambda i: (i, 0)),
            pl.BlockSpec((block, total), lambda i: (i, 0)),
        ],
        out_shape=[
            jax.ShapeDtypeStruct((tokens, total), jnp.bfloat16),
            jax.ShapeDtypeStruct((tokens, total), jnp.float32),
        ],
        scratch_shapes=[
            pltpu.VMEM((block * PLACES, LANES), jnp.bfloat16),
            pltpu.VMEM((block * TIGHT, LANES), jnp.bfloat16),
        ],
        compiler_params=pltpu.CompilerParams(vmem_limit_bytes=40 * 1024 * 1024),
        name="pool_tokens",
    )(tiled, weights, counts)
    return (padded, tiled, features, pooled_lse)


def pool_grads(padded, tiled, weights, counts, pooled_lse, upstream, vocab_size, tight_from):
    tokens = tiled.shape[0]
    block = math.gcd(tokens, TOKEN_BLOCK)
    total = weights.shape[1]
    grad_weight, aligned = pl.pallas_call(
        partial(pool_grad_kernel, tight_from),
        grid=(tokens // block,),
        in_specs=[
            pl.BlockSpec((block, PLACES, LANES), lambda i: (i, 0, 0)),
            pl.BlockSpec((LANES, total), lambda i: (0, 0)),
            pl.BlockSpec((8, total), lambda i: (0, 0)),
            pl.BlockSpec((block, total), lambda i: (i, 0)),
            pl.BlockSpec((block, total), lambda i: (i, 0)),
        ],
        out_specs=[
            pl.BlockSpec((LANES, total), lambda i: (0, 0)),
            pl.BlockSpec((block, PLACES, LANES), lambda i: (i, 0, 0)),
        ],
        out_shape=[
            jax.ShapeDtypeStruct((LANES, total), jnp.float32),
            jax.ShapeDtypeStruct((tokens, PLACES, LANES), jnp.float32),
        ],
        scratch_shapes=[
            pltpu.VMEM((block * PLACES, LANES), jnp.bfloat16),
            pltpu.VMEM((block * TIGHT, LANES), jnp.bfloat16),
            pltpu.VMEM((block, PLACES, LANES), jnp.float32),
        ],
        compiler_params=pltpu.CompilerParams(vmem_limit_bytes=40 * 1024 * 1024),
        name="pool_grads",
    )(tiled, weights, counts, pooled_lse, upstream)
    aligned = aligned.reshape(tokens * PLACES, LANES)
    selector = char_selector(padded, vocab_size).astype(jnp.bfloat16)
    high = aligned.astype(jnp.bfloat16)
    low = (aligned - high.astype(jnp.float32)).astype(jnp.bfloat16)
    by_tap = outer_sum(selector, high) + outer_sum(selector, low)
    grad_table = by_tap[:, :TAPS].reshape(vocab_size, WIDEST, EMBED).sum(axis=1)
    return (grad_weight, grad_table)


def split_banks(grad_weight, bank_cols):
    taps = grad_weight[:TAPS].reshape(WIDEST, EMBED, -1)
    bias_row = grad_weight[TAPS]
    kernels, biases, at = [], [], 0
    for bank_specs in bank_plan(bank_cols):
        pieces, bias_pieces, used = [], [], 0
        for filter_width, first_col, count in bank_specs:
            piece = taps[:filter_width, :, at : at + count]
            pieces.append(jnp.pad(piece, ((0, WIDEST - filter_width), (0, 0), (0, 0))))
            bias_pieces.append(bias_row[at : at + count])
            at += count
            used += count
        kernels.append(
            jnp.pad(jnp.concatenate(pieces, axis=2), ((0, 0), (0, 0), (0, bank_cols - used)))
        )
        biases.append(jnp.pad(jnp.concatenate(bias_pieces), (0, bank_cols - used)))
    return (jnp.stack(kernels), jnp.stack(biases))


TEAM = ("t", "x", "c")
GRID = ("g", "y")
EVERY = ("g", "t", "y", "x", "c")


def team_place():
    x_size, c_size = lax.axis_size("x"), lax.axis_size("c")
    return (lax.axis_index("t") * x_size + lax.axis_index("x")) * c_size + lax.axis_index("c")


def team_size():
    return lax.axis_size("t") * lax.axis_size("x") * lax.axis_size("c")


def team_coords(place):
    x_size, c_size = lax.axis_size("x"), lax.axis_size("c")
    return {
        "t": place // (x_size * c_size),
        "x": lax.rem(place // c_size, x_size),
        "c": lax.rem(place, c_size),
    }


def swap_team(values):
    return lax.all_to_all(values, TEAM, split_axis=0, concat_axis=0, tiled=True)


def share_team(values):
    team = team_size()
    return swap_team(jnp.broadcast_to(values[None], (team,) + values.shape))


def sigmoid(values):
    return 0.5 * jnp.tanh(0.5 * values) + 0.5


def wait_bytes(ref, sem):
    pltpu.make_async_copy(ref, ref, sem).wait()


def lstm_kernel(
    team,
    lin_ref,
    out_grad_ref,
    weight_ref,
    proj_ref,
    bias_ref,
    keep_ref,
    grad_lin_ref,
    grad_gates_ref,
    lin_all_ref,
    state_ref,
    full_ref,
    grad_proj_ref,
    gates,
    cell_start,
    projected,
    stage,
    received,
    received_back,
    grad_cell,
    grad_lin_sum,
    stage_lin,
    received_lin,
    lin_sems,
    send_sems,
    sum_sems,
    share_send_sems,
    share_sems,
):
    steps, own, width = lin_ref.shape
    group = team * own
    cells = proj_ref.shape[2]
    row_block = 32
    place = team_place()
    own_rows = pl.ds(pl.multiple_of(place * own, own), own)
    peers = [lax.rem(place + k, team) for k in range(1, team)]
    last = steps - 1

    barrier = pltpu.get_barrier_semaphore()
    for peer in peers:
        pl.semaphore_signal(
            barrier, inc=1, device_id=team_coords(peer), device_id_type=pl.DeviceIdType.MESH
        )
    pl.semaphore_wait(barrier, team - 1)

    def send(source, target, send_sem, recv_sem, peer):
        pltpu.make_async_remote_copy(
            src_ref=source,
            dst_ref=target,
            send_sem=send_sem,
            recv_sem=recv_sem,
            device_id=team_coords(peer),
            device_id_type=pl.DeviceIdType.MESH,
        ).start()

    for peer in peers:
        send(lin_ref, lin_all_ref.at[:, own_rows], lin_sems.at[0], lin_sems.at[1], peer)
    lin_all_ref[:, own_rows] = lin_ref[...]
    for d in range(2):
        first = 0 if d == 0 else last
        state_ref[d, first] = jnp.zeros((group, width), jnp.bfloat16)
        cell_start[d, first] = jnp.zeros((group, cells), jnp.float32)
        grad_cell[d] = jnp.zeros((group, cells), jnp.float32)
    grad_lin_sum[...] = jnp.zeros_like(grad_lin_sum)
    others = pl.ds(0, team - 1)
    wait_bytes(lin_all_ref.at[:, pl.ds(0, (team - 1) * own)], lin_sems.at[1])

    @pl.loop(0, steps)
    def _(t):
        for d in range(2):
            for q in range(4):
                cols = pl.ds(q * cells, cells)
                gates[d, t, :, cols] = (
                    jnp.dot(
                        lin_all_ref[t],
                        weight_ref[d, :width, cols],
                        preferred_element_type=jnp.float32,
                    )
                    + bias_ref[d, :, cols]
                )

    def time_of(d, s):
        return s if d == 0 else last - s

    @pl.loop(0, steps)
    def _(s):
        for d in range(2):
            t = time_of(d, s)
            later = time_of(d, jnp.minimum(s + 1, last))

            @pl.when(s > 0)
            def _():
                wait_bytes(
                    state_ref.at[d, t, pl.ds(0, (team - 1) * own)], share_sems.at[0, d, s]
                )
                for q in range(4):
                    cols = pl.ds(q * cells, cells)
                    gates[d, t, :, cols] += jnp.dot(
                        state_ref[d, t],
                        weight_ref[d, width:, cols],
                        preferred_element_type=jnp.float32,
                    )

            @pl.loop(0, group // row_block)
            def _(block):
                rows = pl.ds(pl.multiple_of(block * row_block, row_block), row_block)
                in_gate = sigmoid(gates[d, t, rows, pl.ds(0, cells)])
                forget_gate = sigmoid(gates[d, t, rows, pl.ds(cells, cells)])
                candidate = jnp.tanh(gates[d, t, rows, pl.ds(2 * cells, cells)])
                out_gate = sigmoid(gates[d, t, rows, pl.ds(3 * cells, cells)])
                gates[d, t, rows, pl.ds(0, cells)] = in_gate
                gates[d, t, rows, pl.ds(cells, cells)] = forget_gate
                gates[d, t, rows, pl.ds(2 * cells, cells)] = candidate
                gates[d, t, rows, pl.ds(3 * cells, cells)] = out_gate
                mixed = forget_gate * cell_start[d, t, rows] + in_gate * candidate
                cell_new = 3.0 * jnp.tanh(mixed * (1.0 / 3.0))
                full_ref[d, t, rows] = (out_gate * jnp.tanh(cell_new)).astype(jnp.bfloat16)

                @pl.when(s < last)
                def _():
                    cell_start[d, later, rows] = cell_new * keep_ref[d, later, rows]

            @pl.when(s > 0)
            def _():
                wait_bytes(stage.at[d, others], send_sems.at[d])

            part = lax.dot_general(
                full_ref[d, t],
                proj_ref[d],
                (((1,), (1,)), ((), ())),
                preferred_element_type=jnp.float32,
            )
            part = part.astype(jnp.bfloat16).reshape(team, own, width)
            stage[d] = part
            received[d, s, place] = stage[d, place]
            for peer in peers:
                send(
                    stage.at[d, peer],
                    received.at[d, s, place],
                    send_sems.at[d],
                    sum_sems.at[0, d, s],
                    peer,
                )
        for d in range(2):
            t = time_of(d, s)
            later = time_of(d, jnp.minimum(s + 1, last))
            wait_bytes(received.at[d, s, others], sum_sems.at[0, d, s])
            total = jnp.sum(received[d, s].astype(jnp.float32), axis=0)
            projected[d, t] = total

            @pl.when(s > 0)
            def _():
                wait_bytes(
                    state_ref.at[d, t, pl.ds(0, (team - 1) * own)], share_send_sems.at[0, d]
                )

            @pl.when(s < last)
            def _():
                state_new = (3.0 * jnp.tanh(total * (1.0 / 3.0))).astype(jnp.bfloat16)
                kept = state_new.astype(jnp.float32) * keep_ref[d, later, own_rows]
                state_ref[d, later, own_rows] = kept.astype(jnp.bfloat16)
                for peer in peers:
                    send(
                        state_ref.at[d, later, own_rows],
                        state_ref.at[d, later, own_rows],
                        share_send_sems.at[0, d],
                        share_sems.at[0, d, s + 1],
                        peer,
                    )

    @pl.loop(0, steps)
    def _(s):
        for d in range(2):
            t = time_of(1 - d, s)

            @pl.when(s > 0)
            def _():
                wait_bytes(
                    received_back.at[d, jnp.maximum(s - 1, 0), others],
                    sum_sems.at[1, d, jnp.maximum(s - 1, 0)],
                )
                grad_lin_ref[0] = jnp.sum(
                    received_back[d, jnp.maximum(s - 1, 0)].astype(jnp.float32), axis=0
                )

            @pl.when(s == 0)
            def _():
                grad_lin_ref[0] = jnp.zeros((own, width), jnp.float32)

            grad_state = grad_lin_ref[0] + out_grad_ref[d, t].astype(jnp.float32)
            squashed = jnp.tanh(projected[d, t] * (1.0 / 3.0))
            grad_proj_ref[d, t, own_rows] = (grad_state * (1.0 - squashed * squashed)).astype(
                jnp.bfloat16
            )
            for peer in peers:
                send(
                    grad_proj_ref.at[d, t, own_rows],
                    grad_proj_ref.at[d, t, own_rows],
                    share_send_sems.at[1, d],
                    share_sems.at[1, d, s],
                    peer,
                )
        for d in range(2):
            t = time_of(1 - d, s)
            wait_bytes(grad_proj_ref.at[d, t, pl.ds(0, (team - 1) * own)], share_sems.at[1, d, s])
            wait_bytes(
                grad_proj_ref.at[d, t, pl.ds(0, (team - 1) * own)], share_send_sems.at[1, d]
            )

            @pl.loop(0, group // row_block)
            def _(block):
                rows = pl.ds(pl.multiple_of(block * row_block, row_block), row_block)
                grad_full = jnp.dot(
                    grad_proj_ref[d, t, rows], proj_ref[d], preferred_element_type=jnp.float32
                )
                in_gate = gates[d, t, rows, pl.ds(0, cells)]
                forget_gate = gates[d, t, rows, pl.ds(cells, cells)]
                candidate = gates[d, t, rows, pl.ds(2 * cells, cells)]
                out_gate = gates[d, t, rows, pl.ds(3 * cells, cells)]
                start = cell_start[d, t, rows]
                clipped = jnp.tanh((forget_gate * start + in_gate * candidate) * (1.0 / 3.0))
                tanh_cell = jnp.tanh(3.0 * clipped)
                total = grad_cell[d, rows] + grad_full * out_gate * (1.0 - tanh_cell * tanh_cell)
                grad_raw = total * (1.0 - clipped * clipped)
                grad_gates_ref[d, t, rows, pl.ds(0, cells)] = (
                    grad_raw * candidate * in_gate * (1.0 - in_gate)
                ).astype(jnp.bfloat16)
                grad_gates_ref[d, t, rows, pl.ds(cells, cells)] = (
                    grad_raw * start * forget_gate * (1.0 - forget_gate)
                ).astype(jnp.bfloat16)
                grad_gates_ref[d, t, rows, pl.ds(2 * cells, cells)] = (
                    grad_raw * in_gate * (1.0 - candidate * candidate)
                ).astype(jnp.bfloat16)
                grad_gates_ref[d, t, rows, pl.ds(3 * cells, cells)] = (
                    grad_full * tanh_cell * out_gate * (1.0 - out_gate)
                ).astype(jnp.bfloat16)
                grad_cell[d, rows] = grad_raw * forget_gate * keep_ref[d, t, rows]

            wait_bytes(stage.at[d, others], send_sems.at[d])

            @pl.when(s < last)
            def _():
                part = (
                    lax.dot_general(
                        grad_gates_ref[d, t],
                        weight_ref[d, width:],
                        (((1,), (1,)), ((), ())),
                        preferred_element_type=jnp.float32,
                    )
                    * keep_ref[d, t]
                )
                stage[d] = part.astype(jnp.bfloat16).reshape(team, own, width)
                received_back[d, s, place] = stage[d, place]
                for peer in peers:
                    send(
                        stage.at[d, peer],
                        received_back.at[d, s, place],
                        send_sems.at[d],
                        sum_sems.at[1, d, s],
                        peer,
                    )

            grad_lin_sum[t] += lax.dot_general(
                grad_gates_ref[d, t],
                weight_ref[d, :width],
                (((1,), (1,)), ((), ())),
                preferred_element_type=jnp.float32,
            )

    for t in range(steps):
        stage_lin[:, t] = grad_lin_sum[t].astype(jnp.bfloat16).reshape(team, own, width)
    received_lin[place] = stage_lin[place]
    for peer in peers:
        send(
            stage_lin.at[peer], received_lin.at[place], lin_sems.at[2], lin_sems.at[3], peer
        )
    wait_bytes(received_lin.at[others], lin_sems.at[3])
    grad_lin_ref[...] = jnp.sum(received_lin[...].astype(jnp.float32), axis=0)
    wait_bytes(stage_lin.at[others], lin_sems.at[2])
    wait_bytes(lin_all_ref.at[:, pl.ds(0, (team - 1) * own)], lin_sems.at[0])


def run_lstm(lin_own, out_grad, weights, proj_turned, bias, keep):
    team = team_size()
    steps, own, width = lin_own.shape
    group = team * own
    cells = proj_turned.shape[2]
    bf16, f32 = jnp.bfloat16, jnp.float32
    vmem = pl.BlockSpec(memory_space=pltpu.VMEM)
    return pl.pallas_call(
        partial(lstm_kernel, team),
        in_specs=[vmem] * 6,
        out_specs=[vmem] * 6,
        out_shape=[
            jax.ShapeDtypeStruct((steps, own, width), f32),
            jax.ShapeDtypeStruct((2, steps, group, 4 * cells), bf16),
            jax.ShapeDtypeStruct((steps, group, width), bf16),
            jax.ShapeDtypeStruct((2, steps, group, width), bf16),
            jax.ShapeDtypeStruct((2, steps, group, cells), bf16),
            jax.ShapeDtypeStruct((2, steps, group, width), bf16),
        ],
        scratch_shapes=[
            pltpu.VMEM((2, steps, group, 4 * cells), f32),
            pltpu.VMEM((2, steps, group, cells), f32),
            pltpu.VMEM((2, steps, own, width), f32),
            pltpu.VMEM((2, team, own, width), bf16),
            pltpu.VMEM((2, steps, team, own, width), bf16),
            pltpu.VMEM((2, steps, team, own, width), bf16),
            pltpu.VMEM((2, group, cells), f32),
            pltpu.VMEM((steps, group, width), f32),
            pltpu.VMEM((team, steps, own, width), bf16),
            pltpu.VMEM((team, steps, own, width), bf16),
            pltpu.SemaphoreType.DMA((4,)),
            pltpu.SemaphoreType.DMA((2,)),
            pltpu.SemaphoreType.DMA((2, 2, steps)),
            pltpu.SemaphoreType.DMA((2, 2)),
            pltpu.SemaphoreType.DMA((2, 2, steps)),
        ],
        compiler_params=pltpu.CompilerParams(
            collective_id=1, has_side_effects=True, vmem_limit_bytes=62 * 1024 * 1024
        ),
        name="lstm_team",
    )(lin_own, out_grad, weights, proj_turned, bias, keep)


def natural_rows(gathered, rows):
    g, y = lax.axis_size("g"), lax.axis_size("y")
    t, x, c = lax.axis_size("t"), lax.axis_size("x"), lax.axis_size("c")
    lanes = gathered.shape[-1]
    split = gathered.reshape(g, y, t, x, c, 2, rows, lanes)
    return split.transpose(5, 0, 2, 1, 3, 4, 6, 7).reshape(2, g * y * t * x * c * rows, lanes)


def owner_rows(values):
    g, y = lax.axis_size("g"), lax.axis_size("y")
    t, x, c = lax.axis_size("t"), lax.axis_size("x"), lax.axis_size("c")
    rows = values.shape[1] // (g * y * t * x * c)
    lanes = values.shape[2]
    split = values.reshape(2, g, t, y, x, c, rows, lanes).transpose(1, 3, 2, 4, 5, 0, 6, 7)
    return split.reshape(g * y, t * x * c, 2 * rows, lanes)


def team_slices(values, parts):
    team = team_size()
    two, rows, columns = values.shape
    lanes = columns // (parts * team)
    split = values.reshape(two, rows, parts, team, lanes).transpose(3, 0, 1, 2, 4)
    return split.reshape(team, two * rows, parts * lanes)


def whole_columns(received, parts):
    team, two_rows, lanes = received.shape
    split = received.reshape(team, 2, two_rows // 2, parts, lanes // parts)
    return split.transpose(1, 2, 3, 0, 4).reshape(2, two_rows // 2, team * lanes)


def shards(
    char_ids,
    resets,
    out_grad,
    char_table,
    conv_weight,
    conv_bias,
    highway_weight,
    highway_bias,
    proj_weight,
    proj_bias,
    lstm_weight,
    lstm_bias,
    lstm_proj,
):
    f32, bf16 = jnp.float32, jnp.bfloat16
    own, steps = resets.shape
    team = team_size()
    place = team_place()
    devices = team * lax.axis_size("g") * lax.axis_size("y")
    bank_cols = conv_weight.shape[3]
    highway_rows = highway_weight.shape[1]
    features_all = highway_rows * devices
    part = features_all // team
    lstm_rows = lstm_weight.shape[1]
    width = proj_weight.shape[1]
    cells_all = lstm_proj.shape[1]
    cells = cells_all // team

    sizes = [highway_bias.size, proj_bias.size, lstm_bias.size, resets.size]
    small = jnp.concatenate(
        [
            highway_bias.reshape(-1),
            proj_bias.reshape(-1),
            lstm_bias.reshape(-1),
            resets.astype(bf16).reshape(-1),
        ]
    )
    small_all = lax.all_gather(small[None], EVERY, axis=0, tiled=True)
    cut = [sum(sizes[:k]) for k in range(5)]
    highway_bias_all = small_all[:, cut[0] : cut[1]].reshape(devices, 2, -1)
    highway_bias_all = highway_bias_all.transpose(1, 0, 2).reshape(2, 2, team, part)
    proj_bias_all = small_all[:, cut[1] : cut[2]].reshape(-1).astype(f32)
    lstm_bias_all = small_all[:, cut[2] : cut[3]].reshape(devices, 2, -1)
    lstm_bias_all = lstm_bias_all.transpose(1, 0, 2).reshape(2, 4, team, cells)
    resets_all = small_all[:, cut[3] : cut[4]].reshape(
        lax.axis_size("g"), lax.axis_size("t"), lax.axis_size("y"), -1, own, steps
    )
    resets_team = lax.dynamic_index_in_dim(resets_all, lax.axis_index("g"), 0, False)
    resets_team = lax.dynamic_index_in_dim(resets_team, lax.axis_index("y"), 1, False)
    resets_team = resets_team.reshape(team * own, steps).astype(f32)
    highway_bias_own = lax.dynamic_index_in_dim(highway_bias_all, place, 2, False)
    highway_bias_own = highway_bias_own.reshape(2, 2 * part).astype(f32)
    lstm_bias_own = lax.dynamic_index_in_dim(lstm_bias_all, place, 2, False)
    lstm_bias_own = lstm_bias_own.reshape(2, 1, 4 * cells).astype(f32)

    highway_swapped = swap_team(team_slices(highway_weight, 2))
    highway_own = natural_rows(
        lax.all_gather(highway_swapped, GRID, axis=0, tiled=False), highway_rows
    )
    lstm_swapped = swap_team(team_slices(lstm_weight, 4))
    lstm_own = natural_rows(lax.all_gather(lstm_swapped, GRID, axis=0, tiled=False), lstm_rows)
    turned_swapped = swap_team(team_slices(jnp.swapaxes(lstm_proj, 1, 2), 1))
    turned_own = natural_rows(
        lax.all_gather(turned_swapped, GRID, axis=0, tiled=False), lstm_proj.shape[2]
    )
    project_full = lax.all_gather(proj_weight, EVERY, axis=0, tiled=True)

    conv_weight_all = lax.all_gather(conv_weight, ("x", "c"), axis=0, tiled=True)
    conv_bias_all = lax.all_gather(conv_bias, ("x", "c"), axis=0, tiled=True)
    bank = lax.axis_index("x") * lax.axis_size("c") + lax.axis_index("c")
    own_ids = lax.dynamic_slice_in_dim(char_ids, bank * own, own, axis=0).reshape(
        own * steps, char_ids.shape[2]
    )
    filters, counts = filter_matrix(conv_weight_all, conv_bias_all)
    tight_from = wide_columns(bank_cols)
    padded_ids, tiled, features, pooled_lse = pool_tokens(
        own_ids, char_table, filters, counts, tight_from
    )

    tokens = own * steps
    operands, hiddens, mixes = [], [], []
    operand = share_team(features).reshape(team * tokens, features_all)
    hidden = lax.dynamic_slice_in_dim(operand, place * part, part, axis=1).astype(f32)
    for level in range(2):
        mixed = (
            jnp.dot(operand, highway_own[level], preferred_element_type=f32)
            + highway_bias_own[level]
        )
        operands.append(operand)
        hiddens.append(hidden)
        mixes.append(mixed)
        carry_gate = jax.nn.sigmoid(mixed[:, part:])
        hidden = carry_gate * hidden + (1.0 - carry_gate) * jax.nn.silu(mixed[:, :part])
        if level == 0:
            operand = share_team(hidden.astype(bf16)).transpose(1, 0, 2)
            operand = operand.reshape(team * tokens, features_all)
    top = swap_team(hidden.astype(bf16).reshape(team, tokens, part))
    top_rows = top.transpose(1, 0, 2).reshape(tokens, features_all)
    lin = (jnp.dot(top_rows, project_full, preferred_element_type=f32) + proj_bias_all).astype(bf16)

    keep_forward = 1.0 - resets_team
    keep_backward = 1.0 - jnp.concatenate(
        [resets_team[:, 1:], jnp.zeros((team * own, 1), f32)], axis=1
    )
    keep = jnp.stack([keep_forward.T, keep_backward.T])[..., None]
    lin_own = jnp.swapaxes(lin.reshape(own, steps, width), 0, 1)
    grad_time = out_grad.reshape(own, steps, 2, width).transpose(2, 1, 0, 3)
    grad_lin, grad_gates, lin_all, states, fulls, grad_projected = run_lstm(
        lin_own, grad_time, lstm_own, turned_own, lstm_bias_own, keep
    )

    count = steps * team * own
    flat_lin = lin_all.reshape(count, width)
    weight_parts, turned_parts, bias_parts = [], [], []
    for d in range(2):
        flat_gates = grad_gates[d].reshape(count, 4 * cells)
        weight_parts.append(
            jnp.concatenate(
                [
                    outer_sum(flat_lin, flat_gates).astype(bf16),
                    outer_sum(states[d].reshape(count, width), flat_gates).astype(bf16),
                ],
                axis=0,
            )
        )
        turned_parts.append(
            outer_sum(
                grad_projected[d].reshape(count, width), fulls[d].reshape(count, cells)
            ).astype(bf16)
        )
        bias_parts.append(column_sum(flat_gates))
    lstm_summed = lax.psum_scatter(
        owner_rows(jnp.stack(weight_parts)), GRID, scatter_dimension=0, tiled=False
    )
    turned_summed = lax.psum_scatter(
        owner_rows(jnp.stack(turned_parts)), GRID, scatter_dimension=0, tiled=False
    )

    grad_input = jnp.swapaxes(grad_lin, 0, 1).reshape(tokens, width).astype(bf16)
    grad_project_w = outer_sum(top_rows, grad_input)
    grad_project_b = column_sum(grad_input)
    grad_top = transposed(grad_input, project_full).astype(bf16)
    grad_top = swap_team(grad_top.reshape(tokens, team, part).transpose(1, 0, 2))
    grad_hidden = grad_top.reshape(team * tokens, part).astype(f32)
    highway_parts, highway_bias_parts = [None, None], [None, None]
    for level in (1, 0):
        operand, hidden_in, mixed = operands[level], hiddens[level], mixes[level]
        carry_gate = jax.nn.sigmoid(mixed[:, part:])
        pre_act = mixed[:, :part]
        act_sig = jax.nn.sigmoid(pre_act)
        grad_act = grad_hidden * (1.0 - carry_gate) * act_sig * (1.0 + pre_act * (1.0 - act_sig))
        grad_carry = grad_hidden * (hidden_in - pre_act * act_sig) * carry_gate * (1.0 - carry_gate)
        grad_mixed = jnp.concatenate([grad_act, grad_carry], axis=1).astype(bf16)
        highway_parts[level] = outer_sum(operand, grad_mixed).astype(bf16)
        highway_bias_parts[level] = column_sum(grad_mixed)
        direct = grad_hidden * carry_gate
        spread = transposed(grad_mixed, highway_own[level])
        if level == 1:
            spread = spread.astype(bf16).reshape(team * tokens, team, part).transpose(1, 0, 2)
            grad_hidden = direct + swap_team(spread).astype(f32).sum(axis=0)
        else:
            held = lax.dynamic_slice_in_dim(spread, place * part, part, axis=1)
            spread = lax.dynamic_update_slice_in_dim(spread, held + direct, place * part, axis=1)
            spread = spread.astype(bf16).reshape(team, tokens, features_all)
            grad_features = swap_team(spread).astype(f32).sum(axis=0).astype(bf16)

    highway_summed = lax.psum_scatter(
        owner_rows(jnp.stack(highway_parts)), GRID, scatter_dimension=0, tiled=False
    )
    project_grad = lax.psum_scatter(
        grad_project_w.astype(bf16), EVERY, scatter_dimension=0, tiled=True
    ).astype(f32)

    grad_filters, grad_table = pool_grads(
        padded_ids,
        tiled,
        filters,
        counts,
        pooled_lse,
        grad_features,
        char_table.shape[0],
        tight_from,
    )
    lstm_weight_grad = whole_columns(swap_team(lstm_summed), 4).astype(f32)
    turned_grad = whole_columns(swap_team(turned_summed), 1).astype(f32)
    lstm_proj_grad = jnp.swapaxes(turned_grad, 1, 2)
    highway_weight_grad = whole_columns(swap_team(highway_summed), 2).astype(f32)

    def own_place(values, parts):
        lanes = values.shape[-1] // parts
        split = values.reshape(2, parts, 1, lanes)
        full = jnp.zeros((2, parts, team, lanes), f32)
        return lax.dynamic_update_slice(full, split, (0, 0, place, 0)).reshape(2, -1)

    lstm_bias_parts = own_place(jnp.stack(bias_parts), 4)
    highway_bias_parts = own_place(jnp.stack(highway_bias_parts), 2)
    pieces = [
        lstm_bias_parts.reshape(2, devices, -1).transpose(1, 0, 2).reshape(devices, -1),
        highway_bias_parts.reshape(2, devices, -1).transpose(1, 0, 2).reshape(devices, -1),
        grad_project_b.reshape(devices, -1),
    ]
    lengths = [piece.shape[1] for piece in pieces]
    mine = lax.all_to_all(
        jnp.concatenate(pieces, axis=1), EVERY, split_axis=0, concat_axis=0, tiled=True
    ).sum(axis=0)
    lstm_bias_grad = mine[: lengths[0]].reshape(2, -1)
    highway_bias_grad = mine[lengths[0] : lengths[0] + lengths[1]].reshape(2, -1)
    proj_bias_grad = mine[lengths[0] + lengths[1] :]

    grad_kernel, grad_bias = split_banks(grad_filters, bank_cols)
    grad_kernel = lax.psum(
        lax.psum_scatter(grad_kernel, ("x", "c"), scatter_dimension=0, tiled=True), ("g", "t", "y")
    )
    grad_bias = lax.psum(
        lax.psum_scatter(grad_bias, ("x", "c"), scatter_dimension=0, tiled=True), ("g", "t", "y")
    )
    grad_table = lax.psum(grad_table, EVERY)
    return (
        grad_table,
        grad_kernel,
        grad_bias,
        highway_weight_grad,
        highway_bias_grad,
        project_grad,
        proj_bias_grad,
        lstm_weight_grad,
        lstm_bias_grad,
        lstm_proj_grad,
    )


def solution(mesh):
    dp, bank = mesh.shape["dp"], mesh.shape["bank"]
    fine = Mesh(mesh.devices.reshape(dp // 4, 2, 2, bank // 2, 2), EVERY)
    rows, banks = ("g", "t", "y"), ("x", "c")
    whole = rows + banks
    placed = (
        P(rows, None, None),
        P(whole, None),
        P(whole, None, None),
        P(),
        P(banks, None, None, None),
        P(banks, None),
        P(None, whole, None),
        P(None, whole),
        P(whole, None),
        P(whole),
        P(None, whole, None),
        P(None, whole),
        P(None, None, whole),
    )
    return jax.shard_map(
        shards,
        mesh=fine,
        in_specs=placed,
        out_specs=(
            P(),
            P(banks, None, None, None),
            P(banks, None),
            P(None, whole, None),
            P(None, whole),
            P(whole, None),
            P(whole),
            P(None, whole, None),
            P(None, whole),
            P(None, None, whole),
        ),
        check_vma=False,
    )
```

time: 2940 us -> 1230 us (0.42)
  waiting for transfers between devices: 2000 us -> 558 us
  matrix products: 384 us -> 58 us
  Pallas kernels: 47.8 us -> 188 us
  other arithmetic: 140 us -> 40.2 us
  starting transfers between devices: 1.11 us -> 59.5 us
  blocking collectives: 229 us -> 182 us
    reduce_scatter x7 -> x5, waiting for transfers between devices: 1560 us -> 220 us  [the longest x1 174 us: shards(): lax.psum_scatter(owner_rows(jnp.stack(weight_parts)), GRID, scatter_dimen...]
    all_gather x6 -> x4, waiting for transfers between devices: 365 us -> 0.03 us  [the longest x1 0.03 us: shards(): lax.all_gather(highway_swapped, GRID, axis=0, tiled=False)]
    unnamed x18 -> x12, waiting for transfers between devices: 2.93 us -> 225 us
    dot_general x21 -> x3, matrix products: 172 us -> 9.12 us  [transposed(): lax.dot_general(former, latter, (((1,), (1,)), ((), ())), preferred_eleme...]
    pallas_call x0 -> x1, Pallas kernels: none -> 140 us  [run_lstm(): pl.pallas_call(partial(lstm_kernel, team), in_specs=[vmem] * 6, out_specs...]
    dot_general x21 -> x3, matrix products: 135 us -> 12 us  [the longest x2 9.74 us: shards(): jnp.dot(operand, highway_own[level], preferred_element_type=f32)]
    all_to_all x0 -> x11, waiting for transfers between devices: none -> 112 us  [the longest x10 103 us: swap_team(): return lax.all_to_all(values, TEAM, split_axis=0, concat_axis=0, tiled=True)]
    all_gather x5 -> x2, blocking collectives: 118 us -> 35.1 us  [the longest x1 29.9 us: shards(): lax.all_gather(conv_weight, ('x', 'c'), axis=0, tiled=True)]
  transfers between devices with their start and end apart: 16 -> 22, of which waited for: 13 -> 9; matrix products, arithmetic and copies ran while one was open for 13% -> 15% of each run, Pallas kernels for 1% -> 4%
where the time goes in v2:
time: 1230 us; the launch traced here: 1220 us
  waiting for transfers between devices  558 us (45%)
  Pallas kernels  188 us (15%)
  blocking collectives  182 us (15%)
  local copies, waits for them, and re-layouts  119 us (10%)
  starting transfers between devices  59.5 us (5%)
  matrix products  58 us (5%)
  other arithmetic  40.2 us (3%)
  between operations  17.6 us (1%)
    unnamed x12, waiting for transfers between devices  225 us
    reduce_scatter x1, waiting for transfers between devices, shards(): lax.psum_scatter(owner_rows(jnp.stack(weight_parts)), GRID, scatter_dimen...  174 us
    pallas_call x1, Pallas kernels, run_lstm(): pl.pallas_call(partial(lstm_kernel, team), in_specs=[vmem] * 6, out_specs...  140 us
    all_to_all x10, waiting for transfers between devices, swap_team(): return lax.all_to_all(values, TEAM, split_axis=0, concat_axis=0, tiled=True)  103 us
    all_to_all x2, blocking collectives, swap_team(): return lax.all_to_all(values, TEAM, split_axis=0, concat_axis=0, tiled=True)  75 us
    all_to_all x10, starting transfers between devices, swap_team(): return lax.all_to_all(values, TEAM, split_axis=0, concat_axis=0, tiled=True)  51.7 us
    psum x1, blocking collectives, shards(): grad_table = lax.psum(grad_table, EVERY)  44.7 us
    dot_general x11, matrix products, outer_sum(): lax.dot_general(former, latter, (((0,), (0,)), ((), ())), preferred_eleme...  30.5 us
  transfers between devices with their start and end apart: 22, of which 9 were waited for; matrix products, arithmetic and copies ran while one was open for 15% of the time, Pallas kernels for 4%

profile of v2, /device:TPU:14, one launch (start us, length us, event | category | flops | bytes accessed | tf_op | source)
XLA Modules:
  0.0 1221.6 jit_solution(2987562695325870440)
XLA Ops:
  17.8 11.6 all-to-all-done.1
  50.5 29.9 %all_gather.30 = bf16[4,7,16,1024]{3,2,1,0:T(8,128)(2,1)S(1)} all-gather(bf16[1,7,16,1024]{3,2,1,0:T(8,128)(2,1)S(1)} %copy-done.38), channel_id=1, replica_groups=mesh['g'=2,'t'=2,'y'=2,'x'=2,'c'=2] {'x','c'}, dimensions={0}, use_global_device_ids=true | all-gather | bytes 1146880 | tf_op jit(solution)/shard_map/all_gather | solution.py:754
  89.6 19.7 %pool_tokens.1 = (bf16[128,2048]{1,0:T(8,128)(2,1)S(1)}, f32[128,2048]{1,0:T(8,128)S(1)}) custom-call(bf16[128,64,128]{2,1,0:T(8,128)(2,1)S(1)} %bitcast.309, bf16[128,2048]{1,0:T(8,128)(2,1)S(1)} %pad_maximum_fusion.8.weight_ref, f32[8,2048]{1,0:T(8,128)S(1)} %copy-done.8), custom_call_target="tpu_custom_call" | custom-call | tf_op jit(solution)/shard_map/pool_tokens/pallas_call | solution.py:205
  119.3 224.2 %all-reduce.28.cloned.1.call-done = bf16[45568]{0:T(1024)(128)(2,1)} async-done(((bf16[45568]{0:T(1024)(128)(2,1)}), bf16[45568]{0:T(1024)(128)(2,1)}) %all-reduce.28.cloned.1.call-update) | async-done | bytes 91152
  369.2 45.3 %all-to-all-done.2 = bf16[8,1024,256]{1,2,0:T(8,128)(2,1)} async-done(((bf16[8,1024,256]{1,2,0:T(8,128)(2,1)}), bf16[8,1024,256]{1,2,0:T(8,128)(2,1)}, u32[]{:S(2)}, u32[]{:S(2)}) %all-to-all-start.2) | async-done | bytes 4194336 | tf_op jit(solution)/shard_map/all_to_all | solution.py:313
  433.0 8.4 copy.187
  444.4 139.9 %lstm_team.1 = (f32[4,32,512]{2,1,0:T(8,128)}, bf16[2,4,256,2048]{3,2,1,0:T(8,128)(2,1)}, bf16[4,256,512]{2,1,0:T(8,128)(2,1)}, bf16[2,4,256,512]{3,2,1,0:T(8,12...) custom-call(bf16[4,32,512]{2,1,0:T(8,128)(2,1)} %bitcast.366, ...), custom_call_target="tpu_custom_call" | custom-call | tf_op jit(solution)/shard_map/lstm_team/pallas_call | solution.py:619
  588.0 13.2 %all_to_all.69 = bf16[8,128,256]{2,1,0:T(8,128)(2,1)S(1)} all-to-all(bf16[8,128,256]{2,1,0:T(8,128)(2,1)S(1)} %bitcast.353), channel_id=1, replica_groups=mesh['g'=2,'t'=2,'y'=2,'x'=2,'c'=2] {'t','x','c'}, dimensions={0} | all-to-all | bytes 1048576 | tf_op jit(solution)/shard_map/all_to_all | solution.py:313
  607.4 5.9 all-to-all-start.7
  624.0 44.5 %all-to-all-done.7 = bf16[8,1024,256]{2,1,0:T(8,128)(2,1)} async-done(((bf16[8,1024,256]{2,1,0:T(8,128)(2,1)}), bf16[8,1024,256]{2,1,0:T(8,128)(2,1)}, u32[]{:S(2)}, u32[]{:S(2)}) %all-to-all-start.7) | async-done | bytes 4194336 | tf_op jit(solution)/shard_map/all_to_all | solution.py:313
  709.7 7.5 pad_maximum_fusion
  717.2 8.4 copy.230
  740.6 7.0 all-to-all-start.10
  754.9 9.3 all-to-all-done.10
  764.2 61.8 %all_to_all.70 = bf16[8,128,2048]{2,1,0:T(8,128)(2,1)} all-to-all(bf16[8,128,2048]{2,1,0:T(8,128)(2,1)} %bitcast.313), channel_id=1, replica_groups=mesh['g'=2,'t'=2,'y'=2,'x'=2,'c'=2] {'t','x','c'}, dimensions={0} | all-to-all | bytes 8388608 | tf_op jit(solution)/shard_map/all_to_all | solution.py:313
  836.3 28.0 %pool_grads.1 = (f32[128,2048]{1,0:T(8,128)S(1)}, f32[128,64,128]{2,1,0:T(8,128)S(1)}) custom-call(bf16[128,64,128]{2,1,0:T(8,128)(2,1)S(1)} %bitcast.310, bf16[128,2048]{1,0:T(8,128)(2,1)S(1)} %pad_maximum_fusion.8.weight_ref, f32[8,2048]{1,0:T(8,128)S(1)} %copy-done.8, f32[128,2048]{1,0:T(8,128)S(1)} %copy-done.6, ...), custom_call_target="tpu_custom_call" | custom-call | tf_op jit(solution)/shard_map/pool_grads/pallas_call | solution.py:235
  869.4 18.2 %reduce-scatter.10.cloned.1.call-done = bf16[64,512]{1,0:T(8,128)(2,1)} async-done(((bf16[2048,512]{1,0:T(8,128)(2,1)}), bf16[64,512]{1,0:T(8,128)(2,1)}) %reduce-scatter.10.cloned.1.call-update) | async-done | bytes 65552 | tf_op jit(solution)/shard_map/reduce_scatter | solution.py:856
  891.9 174.5 %reduce-scatter.12.cloned.1.call-done = bf16[1,8,64,2048]{3,2,1,0:T(8,128)(2,1)} async-done(((bf16[4,8,64,2048]{3,2,1,0:T(8,128)(2,1)}), bf16[1,8,64,2048]{3,2,1,0:T(8,128)(2,1)}) %reduce-scatter.12.cloned.1.call-update) | async-done | bytes 2097168 | tf_op jit(solution)/shard_map/reduce_scatter | solution.py:818
  1066.3 8.2 all-to-all-start.11
  1081.9 27.7 %reduce-scatter.6.cloned.1.call-done = f32[1,7,16,1024]{3,2,1,0:T(8,128)} async-done(((f32[4,7,16,1024]{3,2,1,0:T(8,128)}), f32[1,7,16,1024]{3,2,1,0:T(8,128)}) %reduce-scatter.6.cloned.1.call-update) | async-done | bytes 458768 | tf_op jit(solution)/shard_map/reduce_scatter | solution.py:898
  1112.8 11.5 all-reduce.22
  1125.0 15.8 %psum.23 = f32[1,1024]{1,0:T(1,128)} all-reduce(f32[1,1024]{1,0:T(1,128)S(1)} %constant_dynamic-slice_fusion.3), channel_id=1, replica_groups=mesh['g'=2,'t'=2,'y'=2,'x'=2,'c'=2] {'g','t','y'}, use_global_device_ids=true, to_apply=%region_7.8 | all-reduce | flops 1024 | bytes 8192 | tf_op jit(solution)/shard_map/psum | solution.py:900
  1140.8 44.7 %psum.21 = f32[262,16]{0,1:T(8,128)} all-reduce(f32[262,16]{0,1:T(8,128)S(1)} %reduce_sum.41), channel_id=1, replica_groups=mesh['g'=2,'t'=2,'y'=2,'x'=2,'c'=2] {'g','t','y','x','c'}, use_global_device_ids=true, to_apply=%region_3.4 | all-reduce | flops 4192 | bytes 33536 | tf_op jit(solution)/shard_map/psum | solution.py:903
  1200.1 6.6 copy.208
  (355 shorter events, 232.3 us)
Async XLA Ops:
  8.0 79.2 %copy-start = (s32[128,4,50]{0,1,2:T(4,128)S(1)}, s32[128,4,50]{0,1,2:T(4,128)}, u32[]{:S(2)}) copy-start(s32[128,4,50]{0,1,2:T(4,128)} %param.13) | copy-start | bytes 307204
  12.1 17.3 %all-to-all-start.1 = ((bf16[8,128,512]{2,1,0:T(8,128)(2,1)}), bf16[8,128,512]{2,1,0:T(8,128)(2,1)S(1)}, u32[]{:S(2)}, u32[]{:S(2)}) async-start(bf16[8,128,512]{2,1,0:T(8,128)(2,1)} %reshape.315), calls=%async_computation.1 | async-start | bytes 2097152 | tf_op jit(solution)/shard_map/all_to_all | solution.py:313
  16.4 327.1 %all-reduce.28.cloned.1.call-start = ((), (), s32[]{:S(2)}) async-start(), calls=%async_computation.28 | async-start | bytes 184320
  17.8 326.9 %all-gather.12.cloned.1.call-start = ((), (), s32[]{:S(2)}) async-start(), calls=%async_computation.25 | async-start | bytes 5242880 | tf_op jit(solution)/shard_map/all_gather | solution.py:744
  31.3 14.1 %all-to-all-start.5 = ((bf16[8,32,512]{2,1,0:T(8,128)(2,1)}), bf16[8,32,512]{2,1,0:T(8,128)(2,1)S(1)}, u32[]{:S(2)}, u32[]{:S(2)}) async-start(bf16[8,32,512]{2,1,0:T(8,128)(2,1)} %bitcast.39), calls=%async_computation.5 | async-start | bytes 524288 | tf_op jit(solution)/shard_map/all_to_all | solution.py:313
  46.2 65.4 %all-to-all-start.4 = ((bf16[8,64,2048]{2,1,0:T(8,128)(2,1)}), bf16[8,64,2048]{2,1,0:T(8,128)(2,1)}, u32[]{:S(2)}, u32[]{:S(2)}) async-start(bf16[8,64,2048]{2,1,0:T(8,128)(2,1)} %reshape.328), calls=%async_computation.4 | async-start | bytes 4194304 | tf_op jit(solution)/shard_map/all_to_all | solution.py:313
  50.5 380.2 %all-gather.16.cloned.1.call-start = ((), (), s32[]{:S(2)}) async-start(), calls=%async_computation.27 | async-start | bytes 1310720 | tf_op jit(solution)/shard_map/all_gather | solution.py:750
  114.2 234.7 %all-to-all-start = ((bf16[8,128,2048]{2,1,0:T(8,128)(2,1)}), bf16[8,128,2048]{2,1,0:T(8,128)(2,1)}, u32[]{:S(2)}, u32[]{:S(2)}) async-start(bf16[8,128,2048]{2,1,0:T(8,128)(2,1)} %broadcast_in_dim.65), calls=%async_computation | async-start | bytes 8388608 | tf_op jit(solution)/shard_map/all_to_all | solution.py:313
  118.7 314.3 %all-gather.14.cloned.1.call-start = ((), (), s32[]{:S(2)}) async-start(), calls=%async_computation.26 | async-start | bytes 10485760 | tf_op jit(solution)/shard_map/all_gather | solution.py:747
  359.5 54.9 %all-to-all-start.2 = ((bf16[8,1024,256]{1,2,0:T(8,128)(2,1)}), bf16[8,1024,256]{1,2,0:T(8,128)(2,1)}, u32[]{:S(2)}, u32[]{:S(2)}) async-start(bf16[8,1024,256]{1,2,0:T(8,128)(2,1)} %broadcast_in_dim.67), calls=%async_computation.2 | async-start | bytes 8388608 | tf_op jit(solution)/shard_map/all_to_all | solution.py:313
  364.2 77.2 %all-gather.10.cloned.1.call-start = ((), (), s32[]{:S(2)}) async-start(), calls=%async_computation.18 | async-start | bytes 2162688 | tf_op jit(solution)/shard_map/all_gather | solution.py:752
  422.7 18.7 %all-to-all-start.3 = ((bf16[8,128,256]{1,2,0:T(8,128)(2,1)}), bf16[8,128,256]{1,2,0:T(8,128)(2,1)S(1)}, u32[]{:S(2)}, u32[]{:S(2)}) async-start(bf16[8,128,256]{1,2,0:T(8,128)(2,1)} %copy.182), calls=%async_computation.3 | async-start | bytes 1048576 | tf_op jit(solution)/shard_map/all_to_all | solution.py:313
  441.4 142.9 %copy-start.22 = (bf16[8,128,256]{1,2,0:T(8,128)(2,1)}, bf16[8,128,256]{1,2,0:T(8,128)(2,1)S(1)}, u32[]{:S(2)}) copy-start(bf16[8,128,256]{1,2,0:T(8,128)(2,1)S(1)} %all-to-all-done.3) | copy-start | bytes 1572868
  607.4 61.1 %all-to-all-start.7 = ((bf16[8,1024,256]{2,1,0:T(8,128)(2,1)}), bf16[8,1024,256]{2,1,0:T(8,128)(2,1)}, u32[]{:S(2)}, u32[]{:S(2)}) async-start(bf16[8,1024,256]{2,1,0:T(8,128)(2,1)} %bitcast.315), calls=%async_computation.7 | async-start | bytes 8388608 | tf_op jit(solution)/shard_map/all_to_all | solution.py:313
  613.3 118.1 %reduce-scatter.14.cloned.1.call-start = ((), (), s32[]{:S(2)}) async-start(), calls=%async_computation.24 | async-start | bytes 1310720 | tf_op jit(solution)/shard_map/reduce_scatter | solution.py:821
  618.1 207.9 %reduce-scatter.8.cloned.1.call-start = ((), (), s32[]{:S(2)}) async-start(), calls=%async_computation.21 | async-start | bytes 5242880 | tf_op jit(solution)/shard_map/reduce_scatter | solution.py:853
  682.4 205.3 %reduce-scatter.10.cloned.1.call-start = ((), (), s32[]{:S(2)}) async-start(), calls=%async_computation.22 | async-start | bytes 2162688 | tf_op jit(solution)/shard_map/reduce_scatter | solution.py:856
  685.4 380.9 %reduce-scatter.12.cloned.1.call-start = ((), (), s32[]{:S(2)}) async-start(), calls=%async_computation.23 | async-start | bytes 10485760 | tf_op jit(solution)/shard_map/reduce_scatter | solution.py:818
  731.5 9.1 all-to-all-start.12
  740.6 23.6 %all-to-all-start.10 = ((f32[32,1,1296]{2,1,0:T(1,128)}), f32[32,1,1296]{2,1,0:T(1,128)}, u32[]{:S(2)}, u32[]{:S(2)}) async-start(f32[32,1,1296]{2,1,0:T(1,128)} %copy.203), calls=%async_computation.12 | async-start | bytes 360448 | tf_op jit(solution)/shard_map/all_to_all | solution.py:889
  826.0 240.3 %all-to-all-start.9 = ((bf16[8,128,512]{2,1,0:T(8,128)(2,1)}), bf16[8,128,512]{2,1,0:T(8,128)(2,1)}, u32[]{:S(2)}, u32[]{:S(2)}) async-start(bf16[8,128,512]{2,1,0:T(8,128)(2,1)} %bitcast.361), calls=%async_computation.11 | async-start | bytes 2097152 | tf_op jit(solution)/shard_map/all_to_all | solution.py:313
  831.4 278.2 %reduce-scatter.6.cloned.1.call-start = ((), (), s32[]{:S(2)}) async-start(), calls=%async_computation.19 | async-start | bytes 2293760 | tf_op jit(solution)/shard_map/reduce_scatter | solution.py:898
  1066.3 129.3 %all-to-all-start.11 = ((bf16[8,64,2048]{2,1,0:T(8,128)(2,1)}), bf16[8,64,2048]{2,1,0:T(8,128)(2,1)S(1)}, u32[]{:S(2)}, u32[]{:S(2)}) async-start(bf16[8,64,2048]{2,1,0:T(8,128)(2,1)} %bitcast.352), calls=%async_computation.15 | async-start | bytes 4194304 | tf_op jit(solution)/shard_map/all_to_all | solution.py:313
  1074.5 137.2 %all-reduce.26.cloned.1.call-start = ((), (), s32[]{:S(2)}) async-start(), calls=%async_computation.20 | async-start | bytes 917504 | tf_op jit(solution)/shard_map/psum | solution.py:897
  (52 other events, 387.0 us)
Sparse Core Ops, SparseCore 0:
  23.4 320.0 all-reduce.27
  1109.7 70.7 all-reduce.25
Sparse Core Ops, SparseCore 1:
  30.5 85.3 all-gather.11
  117.6 38.2 all-gather.15
  157.6 151.9 all-gather.13
  367.9 69.1 all-gather.9
  618.2 37.7 reduce-scatter.13
  682.5 88.6 reduce-scatter.7
  773.3 114.3 reduce-scatter.9
  890.9 175.4 reduce-scatter.11
  1069.3 40.2 reduce-scatter.5

commit v3 on v2

--- a/solution.py
+++ b/solution.py
@@ -267,25 +267,6 @@
     return (grad_weight, grad_table)
 
 
-def split_banks(grad_weight, bank_cols):
-    taps = grad_weight[:TAPS].reshape(WIDEST, EMBED, -1)
-    bias_row = grad_weight[TAPS]
-    kernels, biases, at = [], [], 0
-    for bank_specs in bank_plan(bank_cols):
-        pieces, bias_pieces, used = [], [], 0
-        for filter_width, first_col, count in bank_specs:
-            piece = taps[:filter_width, :, at : at + count]
-            pieces.append(jnp.pad(piece, ((0, WIDEST - filter_width), (0, 0), (0, 0))))
-            bias_pieces.append(bias_row[at : at + count])
-            at += count
-            used += count
-        kernels.append(
-            jnp.pad(jnp.concatenate(pieces, axis=2), ((0, 0), (0, 0), (0, bank_cols - used)))
-        )
-        biases.append(jnp.pad(jnp.concatenate(bias_pieces), (0, bank_cols - used)))
-    return (jnp.stack(kernels), jnp.stack(biases))
-
-
 TEAM = ("t", "x", "c")
 GRID = ("g", "y")
 EVERY = ("g", "t", "y", "x", "c")
@@ -328,13 +309,19 @@
 
 def lstm_kernel(
     team,
-    lin_ref,
+    parts_ref,
+    lin_bias_ref,
     out_grad_ref,
+    weight_hbm,
+    turned_hbm,
+    bias_ref,
+    keep_ref,
+    grad_lin_all_ref,
+    grad_weight_hbm,
+    grad_turned_hbm,
+    grad_bias_ref,
     weight_ref,
     proj_ref,
-    bias_ref,
-    keep_ref,
-    grad_lin_ref,
     grad_gates_ref,
     lin_all_ref,
     state_ref,
@@ -350,13 +337,18 @@
     grad_lin_sum,
     stage_lin,
     received_lin,
+    grad_state_own,
+    grad_stage,
+    turned_stage,
+    load_sems,
     lin_sems,
     send_sems,
     sum_sems,
     share_send_sems,
     share_sems,
+    out_sems,
 ):
-    steps, own, width = lin_ref.shape
+    _, steps, own, width = parts_ref.shape
     group = team * own
     cells = proj_ref.shape[2]
     row_block = 32
@@ -364,6 +356,31 @@
     own_rows = pl.ds(pl.multiple_of(place * own, own), own)
     peers = [lax.rem(place + k, team) for k in range(1, team)]
     last = steps - 1
+    others = pl.ds(0, team - 1)
+    other_rows = pl.ds(0, (team - 1) * own)
+    g_size, y_size = lax.axis_size("g"), lax.axis_size("y")
+    t_size = lax.axis_size("t")
+    blocks = [
+        (g * y_size + y, t, (g * t_size + t) * y_size + y)
+        for g in range(g_size)
+        for t in range(t_size)
+        for y in range(y_size)
+    ]
+    run = weight_hbm.shape[3]
+    turned_run = turned_hbm.shape[3]
+
+    for d in range(2):
+        for source, t, at in blocks:
+            pltpu.make_async_copy(
+                weight_hbm.at[source, t, d],
+                weight_ref.at[d, pl.ds(at * run, run)],
+                load_sems.at[0],
+            ).start()
+            pltpu.make_async_copy(
+                turned_hbm.at[source, t, d],
+                proj_ref.at[d, pl.ds(at * turned_run, turned_run)],
+                load_sems.at[1],
+            ).start()
 
     barrier = pltpu.get_barrier_semaphore()
     for peer in peers:
@@ -383,16 +400,28 @@
         ).start()
 
     for peer in peers:
-        send(lin_ref, lin_all_ref.at[:, own_rows], lin_sems.at[0], lin_sems.at[1], peer)
-    lin_all_ref[:, own_rows] = lin_ref[...]
+        send(parts_ref.at[peer], stage_lin.at[place], lin_sems.at[0], lin_sems.at[1], peer)
+    stage_lin[place] = parts_ref[place]
     for d in range(2):
         first = 0 if d == 0 else last
         state_ref[d, first] = jnp.zeros((group, width), jnp.bfloat16)
         cell_start[d, first] = jnp.zeros((group, cells), jnp.float32)
         grad_cell[d] = jnp.zeros((group, cells), jnp.float32)
     grad_lin_sum[...] = jnp.zeros_like(grad_lin_sum)
-    others = pl.ds(0, team - 1)
-    wait_bytes(lin_all_ref.at[:, pl.ds(0, (team - 1) * own)], lin_sems.at[1])
+    wait_bytes(stage_lin.at[others], lin_sems.at[1])
+    lin_own = jnp.sum(stage_lin[...].astype(jnp.float32), axis=0) + lin_bias_ref[...]
+    lin_all_ref[:, own_rows] = lin_own.astype(jnp.bfloat16)
+    for peer in peers:
+        send(
+            lin_all_ref.at[:, own_rows],
+            lin_all_ref.at[:, own_rows],
+            lin_sems.at[2],
+            lin_sems.at[3],
+            peer,
+        )
+    wait_bytes(weight_ref, load_sems.at[0])
+    wait_bytes(proj_ref, load_sems.at[1])
+    wait_bytes(lin_all_ref.at[:, other_rows], lin_sems.at[3])
 
     @pl.loop(0, steps)
     def _(t):
@@ -420,7 +449,7 @@
             @pl.when(s > 0)
             def _():
                 wait_bytes(
-                    state_ref.at[d, t, pl.ds(0, (team - 1) * own)], share_sems.at[0, d, s]
+                    state_ref.at[d, t, other_rows], share_sems.at[0, d, s]
                 )
                 for q in range(4):
                     cols = pl.ds(q * cells, cells)
@@ -480,7 +509,7 @@
             @pl.when(s > 0)
             def _():
                 wait_bytes(
-                    state_ref.at[d, t, pl.ds(0, (team - 1) * own)], share_send_sems.at[0, d]
+                    state_ref.at[d, t, other_rows], share_send_sems.at[0, d]
                 )
 
             @pl.when(s < last)
@@ -508,15 +537,15 @@
                     received_back.at[d, jnp.maximum(s - 1, 0), others],
                     sum_sems.at[1, d, jnp.maximum(s - 1, 0)],
                 )
-                grad_lin_ref[0] = jnp.sum(
+                grad_state_own[...] = jnp.sum(
                     received_back[d, jnp.maximum(s - 1, 0)].astype(jnp.float32), axis=0
                 )
 
             @pl.when(s == 0)
             def _():
-                grad_lin_ref[0] = jnp.zeros((own, width), jnp.float32)
-
-            grad_state = grad_lin_ref[0] + out_grad_ref[d, t].astype(jnp.float32)
+                grad_state_own[...] = jnp.zeros((own, width), jnp.float32)
+
+            grad_state = grad_state_own[...] + out_grad_ref[d, t].astype(jnp.float32)
             squashed = jnp.tanh(projected[d, t] * (1.0 / 3.0))
             grad_proj_ref[d, t, own_rows] = (grad_state * (1.0 - squashed * squashed)).astype(
                 jnp.bfloat16
@@ -531,9 +560,9 @@
                 )
         for d in range(2):
             t = time_of(1 - d, s)
-            wait_bytes(grad_proj_ref.at[d, t, pl.ds(0, (team - 1) * own)], share_sems.at[1, d, s])
+            wait_bytes(grad_proj_ref.at[d, t, other_rows], share_sems.at[1, d, s])
             wait_bytes(
-                grad_proj_ref.at[d, t, pl.ds(0, (team - 1) * own)], share_send_sems.at[1, d]
+                grad_proj_ref.at[d, t, other_rows], share_send_sems.at[1, d]
             )
 
             @pl.loop(0, group // row_block)
@@ -596,39 +625,115 @@
                 preferred_element_type=jnp.float32,
             )
 
+    wait_bytes(parts_ref.at[others], lin_sems.at[0])
+    wait_bytes(lin_all_ref.at[:, other_rows], lin_sems.at[2])
     for t in range(steps):
         stage_lin[:, t] = grad_lin_sum[t].astype(jnp.bfloat16).reshape(team, own, width)
     received_lin[place] = stage_lin[place]
     for peer in peers:
+        send(stage_lin.at[peer], received_lin.at[place], lin_sems.at[4], lin_sems.at[5], peer)
+
+    count = steps * group
+    half_blocks = len(blocks) // 2
+
+    def weight_grads(d):
+        for half in range(2):
+
+            @pl.loop(0, 4)
+            def _(q):
+                cols = pl.ds(pl.multiple_of(q * cells, cells), cells)
+                slot = lax.rem(q, 2)
+                rows_in = (lin_all_ref[...] if half == 0 else state_ref[d]).reshape(count, width)
+                gate_part = grad_gates_ref[d, :, :, cols].reshape(count, cells)
+                part = lax.dot_general(
+                    rows_in,
+                    gate_part,
+                    (((0,), (0,)), ((), ())),
+                    preferred_element_type=jnp.float32,
+                )
+
+                @pl.when(q >= 2)
+                def _():
+                    wait_bytes(grad_stage.at[slot], out_sems.at[slot])
+
+                grad_stage[slot] = part.astype(jnp.bfloat16)
+                for source, t, at in blocks[half * half_blocks : (half + 1) * half_blocks]:
+                    pltpu.make_async_copy(
+                        grad_stage.at[slot, pl.ds((at - half * half_blocks) * run, run)],
+                        grad_weight_hbm.at[source, t, d, :, cols],
+                        out_sems.at[slot],
+                    ).start()
+
+            for slot in range(2):
+                wait_bytes(grad_stage.at[slot], out_sems.at[slot])
+        turned = lax.dot_general(
+            grad_proj_ref[d].reshape(count, width),
+            full_ref[d].reshape(count, cells),
+            (((0,), (0,)), ((), ())),
+            preferred_element_type=jnp.float32,
+        )
+        turned_stage[d] = turned.astype(jnp.bfloat16)
+        for source, t, at in blocks:
+            pltpu.make_async_copy(
+                turned_stage.at[d, pl.ds(at * turned_run, turned_run)],
+                grad_turned_hbm.at[source, t, d],
+                out_sems.at[2 + d],
+            ).start()
+        ones = jnp.ones((8, count), jnp.bfloat16)
+        for q in range(4):
+            cols = pl.ds(q * cells, cells)
+            grad_bias_ref[d, :, cols] = jnp.dot(
+                ones,
+                grad_gates_ref[d, :, :, cols].reshape(count, cells),
+                preferred_element_type=jnp.float32,
+            )
+
+    weight_grads(0)
+    wait_bytes(received_lin.at[others], lin_sems.at[5])
+    grad_lin_all_ref[place] = jnp.sum(received_lin[...].astype(jnp.float32), axis=0).astype(
+        jnp.bfloat16
+    )
+    for peer in peers:
         send(
-            stage_lin.at[peer], received_lin.at[place], lin_sems.at[2], lin_sems.at[3], peer
+            grad_lin_all_ref.at[place],
+            grad_lin_all_ref.at[place],
+            lin_sems.at[6],
+            lin_sems.at[7],
+            peer,
         )
-    wait_bytes(received_lin.at[others], lin_sems.at[3])
-    grad_lin_ref[...] = jnp.sum(received_lin[...].astype(jnp.float32), axis=0)
-    wait_bytes(stage_lin.at[others], lin_sems.at[2])
-    wait_bytes(lin_all_ref.at[:, pl.ds(0, (team - 1) * own)], lin_sems.at[0])
-
-
-def run_lstm(lin_own, out_grad, weights, proj_turned, bias, keep):
-    team = team_size()
-    steps, own, width = lin_own.shape
+    weight_grads(1)
+    wait_bytes(grad_lin_all_ref.at[others], lin_sems.at[7])
+    wait_bytes(stage_lin.at[others], lin_sems.at[4])
+    wait_bytes(grad_lin_all_ref.at[others], lin_sems.at[6])
+    for d in range(2):
+        wait_bytes(turned_stage.at[d], out_sems.at[2 + d])
+
+
+def run_lstm(parts, lin_bias, out_grad, weights, turned, bias, keep):
+    team, steps, own, width = parts.shape
     group = team * own
-    cells = proj_turned.shape[2]
+    cells = turned.shape[4]
     bf16, f32 = jnp.bfloat16, jnp.float32
     vmem = pl.BlockSpec(memory_space=pltpu.VMEM)
+    hbm = pl.BlockSpec(memory_space=pl.ANY)
     return pl.pallas_call(
         partial(lstm_kernel, team),
-        in_specs=[vmem] * 6,
-        out_specs=[vmem] * 6,
+        in_specs=[vmem, vmem, vmem, hbm, hbm, vmem, vmem],
+        out_specs=[vmem, hbm, hbm, vmem],
         out_shape=[
-            jax.ShapeDtypeStruct((steps, own, width), f32),
-            jax.ShapeDtypeStruct((2, steps, group, 4 * cells), bf16),
-            jax.ShapeDtypeStruct((steps, group, width), bf16),
-            jax.ShapeDtypeStruct((2, steps, group, width), bf16),
-            jax.ShapeDtypeStruct((2, steps, group, cells), bf16),
-            jax.ShapeDtypeStruct((2, steps, group, width), bf16),
+            jax.ShapeDtypeStruct(parts.shape, bf16),
+            jax.ShapeDtypeStruct(weights.shape, bf16),
+            jax.ShapeDtypeStruct(turned.shape, bf16),
+            jax.ShapeDtypeStruct((2, 8, 4 * cells), f32),
         ],
         scratch_shapes=[
+            pltpu.VMEM((2, 2 * width, 4 * cells), bf16),
+            pltpu.VMEM((2, width, cells), bf16),
+            pltpu.VMEM((2, steps, group, 4 * cells), bf16),
+            pltpu.VMEM((steps, group, width), bf16),
+            pltpu.VMEM((2, steps, group, width), bf16),
+            pltpu.VMEM((2, steps, group, cells), bf16),
+            pltpu.VMEM((2, steps, group, width), bf16),
             pltpu.VMEM((2, steps, group, 4 * cells), f32),
             pltpu.VMEM((2, steps, group, cells), f32),
             pltpu.VMEM((2, steps, own, width), f32),
@@ -639,34 +744,53 @@
             pltpu.VMEM((steps, group, width), f32),
             pltpu.VMEM((team, steps, own, width), bf16),
             pltpu.VMEM((team, steps, own, width), bf16),
-            pltpu.SemaphoreType.DMA((4,)),
+            pltpu.VMEM((own, width), f32),
+            pltpu.VMEM((2, width, cells), bf16),
+            pltpu.VMEM((2, width, cells), bf16),
+            pltpu.SemaphoreType.DMA((2,)),
+            pltpu.SemaphoreType.DMA((8,)),
             pltpu.SemaphoreType.DMA((2,)),
             pltpu.SemaphoreType.DMA((2, 2, steps)),
             pltpu.SemaphoreType.DMA((2, 2)),
             pltpu.SemaphoreType.DMA((2, 2, steps)),
+            pltpu.SemaphoreType.DMA((4,)),
         ],
         compiler_params=pltpu.CompilerParams(
-            collective_id=1, has_side_effects=True, vmem_limit_bytes=62 * 1024 * 1024
+            collective_id=1, has_side_effects=True, vmem_limit_bytes=63 * 1024 * 1024
         ),
         name="lstm_team",
-    )(lin_own, out_grad, weights, proj_turned, bias, keep)
-
-
-def natural_rows(gathered, rows):
-    g, y = lax.axis_size("g"), lax.axis_size("y")
-    t, x, c = lax.axis_size("t"), lax.axis_size("x"), lax.axis_size("c")
-    lanes = gathered.shape[-1]
-    split = gathered.reshape(g, y, t, x, c, 2, rows, lanes)
-    return split.transpose(5, 0, 2, 1, 3, 4, 6, 7).reshape(2, g * y * t * x * c * rows, lanes)
-
-
-def owner_rows(values):
-    g, y = lax.axis_size("g"), lax.axis_size("y")
-    t, x, c = lax.axis_size("t"), lax.axis_size("x"), lax.axis_size("c")
-    rows = values.shape[1] // (g * y * t * x * c)
+    )(parts, lin_bias, out_grad, weights, turned, bias, keep)
+
+
+def axis_sizes():
+    return tuple(lax.axis_size(name) for name in EVERY)
+
+
+def run_rows(received):
+    g, t, y, x, c = axis_sizes()
+    lanes = received.shape[-1]
+    split = received.reshape(t, x * c, 2, -1, lanes).transpose(0, 2, 1, 3, 4)
+    return split.reshape(t, 2, -1, lanes)
+
+
+def member_rows(runs):
+    g, t, y, x, c = axis_sizes()
+    lanes = runs.shape[-1]
+    split = runs.reshape(t, 2, x * c, -1, lanes).transpose(0, 2, 1, 3, 4)
+    return split.reshape(t * x * c, -1, lanes)
+
+
+def team_rows(gathered):
+    grid, team, two_rows, lanes = gathered.shape
+    split = gathered.reshape(grid, team, 2, two_rows // 2, lanes)
+    return split.transpose(2, 1, 0, 3, 4).reshape(2, -1, lanes)
+
+
+def owner_team_rows(values):
+    g, t, y, x, c = axis_sizes()
     lanes = values.shape[2]
-    split = values.reshape(2, g, t, y, x, c, rows, lanes).transpose(1, 3, 2, 4, 5, 0, 6, 7)
-    return split.reshape(g * y, t * x * c, 2 * rows, lanes)
+    split = values.reshape(2, t * x * c, g * y, -1, lanes).transpose(2, 1, 0, 3, 4)
+    return split.reshape(g * y, t * x * c, -1, lanes)
 
 
 def team_slices(values, parts):
@@ -681,6 +805,67 @@
     team, two_rows, lanes = received.shape
     split = received.reshape(team, 2, two_rows // 2, parts, lanes // parts)
     return split.transpose(1, 2, 3, 0, 4).reshape(2, two_rows // 2, team * lanes)
+
+
+def team_first(values):
+    g, t, y, x, c = axis_sizes()
+    rows = values.shape[0]
+    split = values.reshape(rows, -1, g, t, y, x, c, values.shape[1] // (2 * g * t * y * x * c))
+    return split.transpose(3, 5, 6, 0, 1, 2, 4, 7)
+
+
+def permuted_columns(values):
+    g, t, y, x, c = axis_sizes()
+    split = values.reshape(values.shape[0], g, t, y, x, c, -1)
+    return split.transpose(0, 2, 4, 5, 1, 3, 6).reshape(values.shape)
+
+
+def restored_columns(values):
+    g, t, y, x, c = axis_sizes()
+    split = values.reshape(values.shape[0], t, x, c, g, y, -1)
+    return split.transpose(0, 4, 1, 5, 2, 3, 6).reshape(values.shape)
+
+
+def padded_rows(values, rows):
+    blocks = values.shape[0]
+    flat = values.reshape(blocks, -1)
+    return jnp.pad(flat, ((0, 0), (0, rows * LANES - flat.shape[1]))).reshape(blocks, rows, LANES)
+
+
+def row_count(items):
+    return -(-items // LANES)
+
+
+def bank_blocks(grad_filters, bank_cols, groups):
+    turned = grad_filters.T
+    blocks, at = [], 0
+    for bank_specs in bank_plan(bank_cols):
+        used = sum(count for width, first, count in bank_specs)
+        piece = turned[at : at + used].reshape(groups, used // groups, LANES)
+        blocks.append(jnp.pad(piece, ((0, 0), (0, (bank_cols - used) // groups), (0, 0))))
+        at += used
+    return jnp.stack(blocks, axis=1).reshape(groups * len(blocks), bank_cols // groups, LANES)
+
+
+def bank_filters(blocks, bank, bank_cols, groups):
+    taps = [
+        [width * EMBED for width, first, count in bank_specs for _ in range(count)]
+        for bank_specs in bank_plan(bank_cols)
+    ]
+    taps = [row + [0] * (bank_cols - len(row)) for row in taps]
+    limit = lax.dynamic_index_in_dim(jnp.asarray(taps, jnp.int32), bank, 0, False)
+    used = [sum(count for width, first, count in specs) for specs in bank_plan(bank_cols)]
+    choices = [
+        lambda value, each=count // groups: jnp.pad(
+            value[:, :each].reshape(groups * each, LANES), ((0, bank_cols - groups * each), (0, 0))
+        )
+        for count in used
+    ]
+    turned = lax.switch(bank, choices, blocks).T
+    row = lax.broadcasted_iota(jnp.int32, (TAPS, 1), 0)
+    kernel = jnp.where(row < limit[None, :], turned[:TAPS], 0.0)
+    bias = jnp.where(limit > 0, turned[TAPS], 0.0)
+    return (kernel.reshape(1, WIDEST, EMBED, bank_cols), bias[None])
 
 
 def shards(
@@ -712,6 +897,17 @@
     cells_all = lstm_proj.shape[1]
     cells = cells_all // team
 
+    highway_slices = team_first(highway_weight.reshape(2 * highway_rows, -1))
+    highway_swapped = swap_team(highway_slices.reshape(team, 2 * highway_rows, 2 * part))
+    first_all = lax.all_gather(
+        jnp.concatenate([highway_swapped.reshape(-1, 2 * part), proj_weight], axis=0),
+        GRID,
+        axis=0,
+        tiled=False,
+    )
+    highway_bias, proj_bias, lstm_bias, highway_swapped = lax.optimization_barrier(
+        (highway_bias, proj_bias, lstm_bias, highway_swapped)
+    )
     sizes = [highway_bias.size, proj_bias.size, lstm_bias.size, resets.size]
     small = jnp.concatenate(
         [
@@ -721,10 +917,17 @@
             resets.astype(bf16).reshape(-1),
         ]
     )
-    small_all = lax.all_gather(small[None], EVERY, axis=0, tiled=True)
+    small_all = lax.all_to_all(
+        jnp.broadcast_to(small[None], (devices, small.size)),
+        EVERY,
+        split_axis=0,
+        concat_axis=0,
+        tiled=True,
+    )
     cut = [sum(sizes[:k]) for k in range(5)]
     highway_bias_all = small_all[:, cut[0] : cut[1]].reshape(devices, 2, -1)
-    highway_bias_all = highway_bias_all.transpose(1, 0, 2).reshape(2, 2, team, part)
+    highway_bias_all = highway_bias_all.transpose(1, 0, 2).reshape(2, 2 * features_all)
+    highway_bias_all = team_first(highway_bias_all).reshape(team, 2, 2 * part)
     proj_bias_all = small_all[:, cut[1] : cut[2]].reshape(-1).astype(f32)
     lstm_bias_all = small_all[:, cut[2] : cut[3]].reshape(devices, 2, -1)
     lstm_bias_all = lstm_bias_all.transpose(1, 0, 2).reshape(2, 4, team, cells)
@@ -734,29 +937,38 @@
     resets_team = lax.dynamic_index_in_dim(resets_all, lax.axis_index("g"), 0, False)
     resets_team = lax.dynamic_index_in_dim(resets_team, lax.axis_index("y"), 1, False)
     resets_team = resets_team.reshape(team * own, steps).astype(f32)
-    highway_bias_own = lax.dynamic_index_in_dim(highway_bias_all, place, 2, False)
-    highway_bias_own = highway_bias_own.reshape(2, 2 * part).astype(f32)
+    highway_bias_own = lax.dynamic_index_in_dim(highway_bias_all, place, 0, False).astype(f32)
     lstm_bias_own = lax.dynamic_index_in_dim(lstm_bias_all, place, 2, False)
     lstm_bias_own = lstm_bias_own.reshape(2, 1, 4 * cells).astype(f32)
 
-    highway_swapped = swap_team(team_slices(highway_weight, 2))
-    highway_own = natural_rows(
-        lax.all_gather(highway_swapped, GRID, axis=0, tiled=False), highway_rows
-    )
+    cut_rows = team * 2 * highway_rows
+    grid = first_all.shape[0]
+    highway_own = team_rows(first_all[:, :cut_rows].reshape(-1, team, 2 * highway_rows, 2 * part))
+    project_own = first_all[:, cut_rows:].reshape(part, width)
+    lstm_weight, lstm_proj, highway_swapped = lax.optimization_barrier(
+        (lstm_weight, lstm_proj, highway_swapped)
+    )
+    turned_rows = lstm_proj.shape[2]
+    turned_slices = team_slices(jnp.swapaxes(lstm_proj, 1, 2), 1)
     lstm_swapped = swap_team(team_slices(lstm_weight, 4))
-    lstm_own = natural_rows(lax.all_gather(lstm_swapped, GRID, axis=0, tiled=False), lstm_rows)
-    turned_swapped = swap_team(team_slices(jnp.swapaxes(lstm_proj, 1, 2), 1))
-    turned_own = natural_rows(
-        lax.all_gather(turned_swapped, GRID, axis=0, tiled=False), lstm_proj.shape[2]
-    )
-    project_full = lax.all_gather(proj_weight, EVERY, axis=0, tiled=True)
-
-    conv_weight_all = lax.all_gather(conv_weight, ("x", "c"), axis=0, tiled=True)
-    conv_bias_all = lax.all_gather(conv_bias, ("x", "c"), axis=0, tiled=True)
+    turned_swapped = swap_team(turned_slices)
+    lstm_own = lax.all_gather(run_rows(lstm_swapped), GRID, axis=0, tiled=False)
+    turned_own = lax.all_gather(run_rows(turned_swapped), GRID, axis=0, tiled=False)
+
+    conv_own = jnp.concatenate([conv_weight.reshape(-1, bank_cols), conv_bias], axis=0)
+    banks = lax.axis_size("x") * lax.axis_size("c")
+    conv_all = lax.all_to_all(
+        jnp.broadcast_to(conv_own[None], (banks,) + conv_own.shape),
+        ("x", "c"),
+        split_axis=0,
+        concat_axis=0,
+        tiled=True,
+    )
+    conv_weight_all = conv_all[:, :-1].reshape((banks,) + conv_weight.shape[1:])
+    conv_bias_all = conv_all[:, -1]
     bank = lax.axis_index("x") * lax.axis_size("c") + lax.axis_index("c")
-    own_ids = lax.dynamic_slice_in_dim(char_ids, bank * own, own, axis=0).reshape(
-        own * steps, char_ids.shape[2]
-    )
+    own_ids = lax.dynamic_slice_in_dim(char_ids, bank * own, own, axis=0)
+    own_ids = jnp.swapaxes(own_ids, 0, 1).reshape(own * steps, char_ids.shape[2])
     filters, counts = filter_matrix(conv_weight_all, conv_bias_all)
     tight_from = wide_columns(bank_cols)
     padded_ids, tiled, features, pooled_lse = pool_tokens(
@@ -765,7 +977,7 @@
 
     tokens = own * steps
     operands, hiddens, mixes = [], [], []
-    operand = share_team(features).reshape(team * tokens, features_all)
+    operand = share_team(permuted_columns(features)).reshape(team * tokens, features_all)
     hidden = lax.dynamic_slice_in_dim(operand, place * part, part, axis=1).astype(f32)
     for level in range(2):
         mixed = (
@@ -780,54 +992,31 @@
         if level == 0:
             operand = share_team(hidden.astype(bf16)).transpose(1, 0, 2)
             operand = operand.reshape(team * tokens, features_all)
-    top = swap_team(hidden.astype(bf16).reshape(team, tokens, part))
-    top_rows = top.transpose(1, 0, 2).reshape(tokens, features_all)
-    lin = (jnp.dot(top_rows, project_full, preferred_element_type=f32) + proj_bias_all).astype(bf16)
-
+    top_own = hidden.astype(bf16)
+    lin_parts = jnp.dot(top_own, project_own, preferred_element_type=f32).astype(bf16)
     keep_forward = 1.0 - resets_team
     keep_backward = 1.0 - jnp.concatenate(
         [resets_team[:, 1:], jnp.zeros((team * own, 1), f32)], axis=1
     )
     keep = jnp.stack([keep_forward.T, keep_backward.T])[..., None]
-    lin_own = jnp.swapaxes(lin.reshape(own, steps, width), 0, 1)
     grad_time = out_grad.reshape(own, steps, 2, width).transpose(2, 1, 0, 3)
-    grad_lin, grad_gates, lin_all, states, fulls, grad_projected = run_lstm(
-        lin_own, grad_time, lstm_own, turned_own, lstm_bias_own, keep
-    )
-
-    count = steps * team * own
-    flat_lin = lin_all.reshape(count, width)
-    weight_parts, turned_parts, bias_parts = [], [], []
-    for d in range(2):
-        flat_gates = grad_gates[d].reshape(count, 4 * cells)
-        weight_parts.append(
-            jnp.concatenate(
-                [
-                    outer_sum(flat_lin, flat_gates).astype(bf16),
-                    outer_sum(states[d].reshape(count, width), flat_gates).astype(bf16),
-                ],
-                axis=0,
-            )
-        )
-        turned_parts.append(
-            outer_sum(
-                grad_projected[d].reshape(count, width), fulls[d].reshape(count, cells)
-            ).astype(bf16)
-        )
-        bias_parts.append(column_sum(flat_gates))
-    lstm_summed = lax.psum_scatter(
-        owner_rows(jnp.stack(weight_parts)), GRID, scatter_dimension=0, tiled=False
-    )
-    turned_summed = lax.psum_scatter(
-        owner_rows(jnp.stack(turned_parts)), GRID, scatter_dimension=0, tiled=False
-    )
-
-    grad_input = jnp.swapaxes(grad_lin, 0, 1).reshape(tokens, width).astype(bf16)
-    grad_project_w = outer_sum(top_rows, grad_input)
+    grad_lin_all, lstm_grads, turned_grads, bias_sums = run_lstm(
+        lin_parts.reshape(team, steps, own, width),
+        proj_bias_all[None],
+        grad_time,
+        lstm_own,
+        turned_own,
+        lstm_bias_own,
+        keep,
+    )
+    lstm_summed = lax.psum_scatter(lstm_grads, GRID, scatter_dimension=0, tiled=False)
+    turned_summed = lax.all_to_all(turned_grads, GRID, split_axis=0, concat_axis=0, tiled=True)
+    turned_summed = turned_summed.astype(f32).sum(axis=0).astype(bf16)
+    grad_input_team = grad_lin_all.reshape(team * tokens, width)
+    grad_input = lax.dynamic_index_in_dim(grad_lin_all, place, 0, False).reshape(tokens, width)
     grad_project_b = column_sum(grad_input)
-    grad_top = transposed(grad_input, project_full).astype(bf16)
-    grad_top = swap_team(grad_top.reshape(tokens, team, part).transpose(1, 0, 2))
-    grad_hidden = grad_top.reshape(team * tokens, part).astype(f32)
+    grad_project_w = outer_sum(top_own, grad_input_team).astype(bf16)
+    grad_hidden = transposed(grad_input_team, project_own)
     highway_parts, highway_bias_parts = [None, None], [None, None]
     for level in (1, 0):
         operand, hidden_in, mixed = operands[level], hiddens[level], mixes[level]
@@ -848,14 +1037,25 @@
             held = lax.dynamic_slice_in_dim(spread, place * part, part, axis=1)
             spread = lax.dynamic_update_slice_in_dim(spread, held + direct, place * part, axis=1)
             spread = spread.astype(bf16).reshape(team, tokens, features_all)
-            grad_features = swap_team(spread).astype(f32).sum(axis=0).astype(bf16)
-
-    highway_summed = lax.psum_scatter(
-        owner_rows(jnp.stack(highway_parts)), GRID, scatter_dimension=0, tiled=False
-    )
-    project_grad = lax.psum_scatter(
-        grad_project_w.astype(bf16), EVERY, scatter_dimension=0, tiled=True
-    ).astype(f32)
+            grad_features = restored_columns(
+                swap_team(spread).astype(f32).sum(axis=0).astype(bf16)
+            )
+
+    first_parts = jnp.concatenate(
+        [
+            owner_team_rows(jnp.stack(highway_parts)).reshape(grid, cut_rows, 2 * part),
+            grad_project_w.reshape(grid, -1, width),
+        ],
+        axis=1,
+    )
+    first_parts, lstm_summed = lax.optimization_barrier((first_parts, lstm_summed))
+    first_summed = lax.psum_scatter(
+        first_parts,
+        GRID,
+        scatter_dimension=0,
+        tiled=False,
+    )
+    project_grad = first_summed[cut_rows:].astype(f32)
 
     grad_filters, grad_table = pool_grads(
         padded_ids,
@@ -867,10 +1067,18 @@
         char_table.shape[0],
         tight_from,
     )
-    lstm_weight_grad = whole_columns(swap_team(lstm_summed), 4).astype(f32)
-    turned_grad = whole_columns(swap_team(turned_summed), 1).astype(f32)
+    lstm_returned = swap_team(member_rows(lstm_summed))
+    lstm_weight_grad = whole_columns(lstm_returned, 4).astype(f32)
+    turned_grad = whole_columns(swap_team(member_rows(turned_summed)), 1).astype(f32)
     lstm_proj_grad = jnp.swapaxes(turned_grad, 1, 2)
-    highway_weight_grad = whole_columns(swap_team(highway_summed), 2).astype(f32)
+    highway_returned = swap_team(first_summed[:cut_rows].reshape(team, 2 * highway_rows, 2 * part))
+    g, t, y, x, c = axis_sizes()
+    highway_weight_grad = (
+        highway_returned.reshape(t, x, c, 2 * highway_rows, 2, g, y, -1)
+        .transpose(3, 4, 5, 0, 6, 1, 2, 7)
+        .reshape(2, highway_rows, 2 * features_all)
+        .astype(f32)
+    )
 
     def own_place(values, parts):
         lanes = values.shape[-1] // parts
@@ -878,29 +1086,57 @@
         full = jnp.zeros((2, parts, team, lanes), f32)
         return lax.dynamic_update_slice(full, split, (0, 0, place, 0)).reshape(2, -1)
 
-    lstm_bias_parts = own_place(jnp.stack(bias_parts), 4)
+    lstm_bias_parts = own_place(bias_sums[:, 0], 4)
     highway_bias_parts = own_place(jnp.stack(highway_bias_parts), 2)
-    pieces = [
-        lstm_bias_parts.reshape(2, devices, -1).transpose(1, 0, 2).reshape(devices, -1),
-        highway_bias_parts.reshape(2, devices, -1).transpose(1, 0, 2).reshape(devices, -1),
-        grad_project_b.reshape(devices, -1),
-    ]
-    lengths = [piece.shape[1] for piece in pieces]
+    highway_bias_parts = (
+        highway_bias_parts.reshape(2, 2, t, x, c, g, y, -1)
+        .transpose(0, 1, 5, 2, 6, 3, 4, 7)
+        .reshape(2, 2 * features_all)
+    )
+    biases = jnp.concatenate(
+        [
+            lstm_bias_parts.reshape(2, devices, -1).transpose(1, 0, 2).reshape(devices, -1),
+            highway_bias_parts.reshape(2, devices, -1).transpose(1, 0, 2).reshape(devices, -1),
+            grad_project_b.reshape(devices, -1),
+        ],
+        axis=1,
+    )
+    groups = g * t * y
+    table_items = -(-grad_table.size // groups)
+    table_flat = jnp.pad(grad_table.reshape(-1), (0, groups * table_items - grad_table.size))
+    table_blocks = jnp.broadcast_to(
+        padded_rows(table_flat.reshape(groups, table_items), row_count(table_items))[:, None],
+        (groups, x * c, row_count(table_items), LANES),
+    ).reshape(devices, -1, LANES)
+    filter_blocks = bank_blocks(grad_filters, bank_cols, groups)
     mine = lax.all_to_all(
-        jnp.concatenate(pieces, axis=1), EVERY, split_axis=0, concat_axis=0, tiled=True
-    ).sum(axis=0)
-    lstm_bias_grad = mine[: lengths[0]].reshape(2, -1)
-    highway_bias_grad = mine[lengths[0] : lengths[0] + lengths[1]].reshape(2, -1)
-    proj_bias_grad = mine[lengths[0] + lengths[1] :]
-
-    grad_kernel, grad_bias = split_banks(grad_filters, bank_cols)
-    grad_kernel = lax.psum(
-        lax.psum_scatter(grad_kernel, ("x", "c"), scatter_dimension=0, tiled=True), ("g", "t", "y")
-    )
-    grad_bias = lax.psum(
-        lax.psum_scatter(grad_bias, ("x", "c"), scatter_dimension=0, tiled=True), ("g", "t", "y")
-    )
-    grad_table = lax.psum(grad_table, EVERY)
+        jnp.concatenate(
+            [filter_blocks, table_blocks, padded_rows(biases, row_count(biases.shape[1]))], axis=1
+        ).astype(bf16),
+        EVERY,
+        split_axis=0,
+        concat_axis=0,
+        tiled=True,
+    )
+    mine = mine.astype(f32).sum(axis=0)
+    shared = filter_blocks.shape[1] + table_blocks.shape[1]
+    mine_biases = mine[shared:].reshape(-1)
+    ends = [2 * lstm_bias.shape[1], 2 * lstm_bias.shape[1] + 2 * highway_bias.shape[1]]
+    lstm_bias_grad = mine_biases[: ends[0]].reshape(2, -1)
+    highway_bias_grad = mine_biases[ends[0] : ends[1]].reshape(2, -1)
+    proj_bias_grad = mine_biases[ends[1] : ends[1] + proj_bias.size]
+    both = lax.all_to_all(
+        jnp.broadcast_to(mine[None, :shared], (groups, shared, LANES)),
+        ("g", "t", "y"),
+        split_axis=0,
+        concat_axis=0,
+        tiled=True,
+    )
+    grad_kernel, grad_bias = bank_filters(
+        both[:, : filter_blocks.shape[1]], bank, bank_cols, groups
+    )
+    grad_table = both[:, filter_blocks.shape[1] :].reshape(groups, -1)[:, :table_items]
+    grad_table = grad_table.reshape(-1)[: char_table.size].reshape(char_table.shape)
     return (
         grad_table,
         grad_kernel,

time: 1230 us -> 952 us (0.77)
  blocking collectives: 182 us -> 0 us
  waiting for transfers between devices: 558 us -> 441 us
  starting transfers between devices: 59.5 us -> 88.7 us
  matrix products: 58 us -> 37.2 us
  Pallas kernels: 188 us -> 208 us
    unnamed x12 -> x5, waiting for transfers between devices: 225 us -> 0.62 us
    reduce_scatter x5 -> x2, waiting for transfers between devices: 220 us -> 0.02 us  [the longest x1 0.02 us: shards(): lax.psum_scatter(lstm_grads, GRID, scatter_dimension=0, tiled=False)]
    all_to_all x10, waiting for transfers between devices: 103 us -> 292 us  [swap_team(): return lax.all_to_all(values, TEAM, split_axis=0, concat_axis=0, tiled=True)]
    all_to_all x1 -> x5, waiting for transfers between devices: 9.26 us -> 86.3 us  [the longest x1 52.8 us: shards(): lax.all_to_all(jnp.concatenate([filter_blocks, table_blocks, padded_rows(...]
    all_to_all x2 -> x0, blocking collectives: 75 us -> none  [swap_team(): return lax.all_to_all(values, TEAM, split_axis=0, concat_axis=0, tiled=True)]
    all_gather x4 -> x3, waiting for transfers between devices: 0.03 us -> 62 us  [the longest x1 36.3 us: shards(): lstm_own = lax.all_gather(run_rows(lstm_swapped), GRID, axis=0, tiled=False)]
    psum x2 -> x0, blocking collectives: 60.5 us -> none  [the longest x1 44.7 us: shards(): grad_table = lax.psum(grad_table, EVERY)]
    all_gather x2 -> x0, blocking collectives: 35.1 us -> none  [the longest x1 29.9 us: shards(): lax.all_gather(conv_weight, ('x', 'c'), axis=0, tiled=True)]
  transfers between devices with their start and end apart: 22 -> 20, of which waited for: 9 -> 13; matrix products, arithmetic and copies ran while one was open for 15% -> 17% of each run, Pallas kernels for 4% -> 5%
where the time goes in v3:
time: 952 us; the launch traced here: 944 us
  waiting for transfers between devices  441 us (46%)
  Pallas kernels  208 us (22%)
  local copies, waits for them, and re-layouts  117 us (12%)
  starting transfers between devices  88.7 us (9%)
  matrix products  37.2 us (4%)
  other arithmetic  35.7 us (4%)
  between operations  15.2 us (2%)
    all_to_all x10, waiting for transfers between devices, swap_team(): return lax.all_to_all(values, TEAM, split_axis=0, concat_axis=0, tiled=True)  292 us
    pallas_call x1, Pallas kernels, run_lstm(): pl.pallas_call(partial(lstm_kernel, team), in_specs=[vmem, vmem, vmem, hb...  160 us
    all_to_all x10, starting transfers between devices, swap_team(): return lax.all_to_all(values, TEAM, split_axis=0, concat_axis=0, tiled=True)  60.8 us
    all_to_all x1, waiting for transfers between devices, shards(): lax.all_to_all(jnp.concatenate([filter_blocks, table_blocks, padded_rows(...  52.8 us
    all_gather x1, waiting for transfers between devices, shards(): lstm_own = lax.all_gather(run_rows(lstm_swapped), GRID, axis=0, tiled=False)  36.3 us
    pallas_call x1, Pallas kernels, pool_grads(): pl.pallas_call(partial(pool_grad_kernel, tight_from), grid=(tokens // blo...  28 us
    all_gather x1, waiting for transfers between devices, shards(): lax.all_gather(jnp.concatenate([highway_swapped.reshape(-1, 2 * part), pr...  25.7 us
    all_to_all x1, waiting for transfers between devices, shards(): lax.all_to_all(jnp.broadcast_to(mine[None, :shared], (groups, shared, LAN...  25 us
  transfers between devices with their start and end apart: 20, of which 13 were waited for; matrix products, arithmetic and copies ran while one was open for 17% of the time, Pallas kernels for 5%

profile of v3, /device:TPU:14, one launch (start us, length us, event | category | flops | bytes accessed | tf_op | source)
XLA Modules:
  0.0 943.5 jit_solution(11462451784741721293)
XLA Ops:
  24.3 12.9 %all-to-all-done.2 = bf16[8,128,512]{1,2,0:T(8,128)(2,1)S(1)} async-done(((bf16[8,128,512]{1,2,0:T(8,128)(2,1)}), bf16[8,128,512]{1,2,0:T(8,128)(2,1)S(1)}, u32[]{:S(2)}, u32[]{:S(2)}) %all-to-all-start.2) | async-done | bytes 1048608 | tf_op jit(solution)/shard_map/all_to_all | solution.py:294
  46.9 8.5 all-to-all-done
  55.4 6.2 all-to-all-start.3
  86.0 19.7 %pool_tokens.1 = (bf16[128,2048]{1,0:T(8,128)(2,1)S(1)}, f32[128,2048]{1,0:T(8,128)S(1)}) custom-call(bf16[128,64,128]{2,1,0:T(8,128)(2,1)S(1)} %bitcast.251, bf16[128,2048]{1,0:T(8,128)(2,1)S(1)} %pad_maximum_fusion.6.weight_ref, f32[8,2048]{1,0:T(8,128)S(1)} %copy-done.8), custom_call_target="tpu_custom_call" | custom-call | tf_op jit(solution)/shard_map/pool_tokens/pallas_call | solution.py:205
  115.7 7.1 all-to-all-start.1
  128.2 25.7 %all-gather.9.cloned.1.call-done = bf16[4352,512]{1,0:T(8,128)(2,1)} async-done(((bf16[1088,512]{1,0:T(8,128)(2,1)}), bf16[4352,512]{1,0:T(8,128)(2,1)}) %all-gather.9.cloned.1.call-update) | async-done | bytes 4456464 | tf_op jit(solution)/shard_map/all_gather | solution.py:902
  158.1 38.9 %all-to-all-done.1 = bf16[8,128,2048]{2,1,0:T(8,128)(2,1)} async-done(((bf16[8,128,2048]{2,1,0:T(8,128)(2,1)}), bf16[8,128,2048]{2,1,0:T(8,128)(2,1)}, u32[]{:S(2)}, u32[]{:S(2)}) %all-to-all-start.1) | async-done | bytes 4194336 | tf_op jit(solution)/shard_map/all_to_all | solution.py:294
  211.3 7.6 all-to-all-start.4
  225.9 76.0 %all-to-all-done.4 = bf16[8,1024,256]{1,2,0:T(8,128)(2,1)} async-done(((bf16[8,1024,256]{1,2,0:T(8,128)(2,1)}), bf16[8,1024,256]{1,2,0:T(8,128)(2,1)}, u32[]{:S(2)}, u32[]{:S(2)}) %all-to-all-start.4) | async-done | bytes 4194336 | tf_op jit(solution)/shard_map/all_to_all | solution.py:294
  311.4 36.3 %all-gather.5.cloned.1.call-done.weight_hbm = bf16[4,2,2,128,2048]{4,3,2,1,0:T(8,128)(2,1)} async-done(((bf16[1,2,2,128,2048]{4,3,2,1,0:T(8,128)(2,1)}), bf16[4,2,2,128,2048]{4,3,2,1,0:T(8,128)(2,1)}) %all-gather.5.cloned.1.call-update) | async-done | bytes 8388624 | tf_op jit(solution)/shard_map/all_gather | solution.py:955
  347.7 160.1 %lstm_team.1 = (bf16[8,4,32,512]{3,2,1,0:T(8,128)(2,1)}, bf16[4,2,2,128,2048]{4,3,2,1,0:T(8,128)(2,1)}, bf16[4,2,2,64,512]{4,3,2,1,0:T(8,128)(2,1)}, f32[2,8,2048]{2,1,0:T(8,128)}) custom-call(bf16[8,4,32,512]{3,2,1,0:T(8,128)(2,1)} %bitcast.269, f32[1,512]{1,0:T(1,128)} %reshape.382.lin_bias_ref, bf16[2,4,32,512]{3,2,1,0:T(8,128)(2,1)} %bitcast.293, ...), custom_call_target="tpu_custom_call" | custom-call | tf_op jit(solution)/shard_map/lstm_team/pallas_call | solution.py:719
  522.4 81.9 %all-to-all-done.7 = bf16[8,1024,256]{2,1,0:T(8,128)(2,1)} async-done(((bf16[8,1024,256]{2,1,0:T(8,128)(2,1)}), bf16[8,1024,256]{2,1,0:T(8,128)(2,1)}, u32[]{:S(2)}, u32[]{:S(2)}) %all-to-all-start.7) | async-done | bytes 4194336 | tf_op jit(solution)/shard_map/all_to_all | solution.py:294
  615.8 6.4 all-to-all-start.8
  644.9 46.5 %all-to-all-done.8 = bf16[8,128,2048]{2,1,0:T(8,128)(2,1)} async-done(((bf16[8,128,2048]{2,1,0:T(8,128)(2,1)}), bf16[8,128,2048]{2,1,0:T(8,128)(2,1)}, u32[]{:S(2)}, u32[]{:S(2)}) %all-to-all-start.8) | async-done | bytes 4194336 | tf_op jit(solution)/shard_map/all_to_all | solution.py:294
  708.4 28.0 %pool_grads.1 = (f32[128,2048]{1,0:T(8,128)S(1)}, f32[128,64,128]{2,1,0:T(8,128)S(1)}) custom-call(bf16[128,64,128]{2,1,0:T(8,128)(2,1)S(1)} %bitcast.252, bf16[128,2048]{1,0:T(8,128)(2,1)S(1)} %pad_maximum_fusion.6.weight_ref, f32[8,2048]{1,0:T(8,128)S(1)} %copy-done.8, f32[128,2048]{1,0:T(8,128)S(1)} %copy-done.6, bf16[128,2048]{1,0:T(8,128)(2,1)S(1)} %copy-done.4), custom_call_target="tpu_custom_call" | custom-call | tf_op jit(solution)/shard_map/pool_grads/pallas_call | solution.py:235
  753.0 52.8 %all-to-all-done.9 = bf16[32,144,128]{2,1,0:T(8,128)(2,1)S(1)} async-done(((bf16[32,144,128]{2,1,0:T(8,128)(2,1)}), bf16[32,144,128]{2,1,0:T(8,128)(2,1)S(1)}, u32[]{:S(2)}, u32[]{:S(2)}) %all-to-all-start.9) | async-done | bytes 1179680 | tf_op jit(solution)/shard_map/all_to_all | solution.py:1112
  805.7 7.6 all-to-all-start.14
  813.5 10.1 %all-to-all-done.14 = bf16[8,32,512]{2,1,0:T(8,128)(2,1)S(1)} async-done(((bf16[8,32,512]{2,1,0:T(8,128)(2,1)}), bf16[8,32,512]{2,1,0:T(8,128)(2,1)S(1)}, u32[]{:S(2)}, u32[]{:S(2)}) %all-to-all-start.14) | async-done | bytes 262176 | tf_op jit(solution)/shard_map/all_to_all | solution.py:294
  824.5 6.0 all-to-all-start.10
  833.6 25.0 %all-to-all-done.10 = f32[8,133,128]{2,1,0:T(8,128)S(1)} async-done(((f32[8,133,128]{2,1,0:T(8,128)}), f32[8,133,128]{2,1,0:T(8,128)S(1)}, u32[]{:S(2)}, u32[]{:S(2)}) %all-to-all-start.10) | async-done | bytes 544800 | tf_op jit(solution)/shard_map/all_to_all | solution.py:1128
  858.6 7.8 all-to-all-start.12
  868.7 21.9 %all-to-all-done.12 = bf16[8,64,2048]{2,1,0:T(8,128)(2,1)S(1)} async-done(((bf16[8,64,2048]{2,1,0:T(8,128)(2,1)}), bf16[8,64,2048]{2,1,0:T(8,128)(2,1)S(1)}, u32[]{:S(2)}, u32[]{:S(2)}) %all-to-all-start.12) | async-done | bytes 2097184 | tf_op jit(solution)/shard_map/all_to_all | solution.py:294
  911.6 6.6 copy.254
  930.6 6.2 reshape.386
  (318 shorter events, 222.5 us)
Async XLA Ops:
  7.2 67.3 %copy-start = (s32[128,4,50]{0,1,2:T(4,128)S(1)}, s32[128,4,50]{0,1,2:T(4,128)}, u32[]{:S(2)}) copy-start(s32[128,4,50]{0,1,2:T(4,128)} %param.18) | copy-start | bytes 307204
  9.1 10.9 %all-to-all-start.6 = ((bf16[8,32,512]{2,1,0:T(8,128)(2,1)}), bf16[8,32,512]{2,1,0:T(8,128)(2,1)S(1)}, u32[]{:S(2)}, u32[]{:S(2)}) async-start(bf16[8,32,512]{2,1,0:T(8,128)(2,1)} %bitcast.50), calls=%async_computation.6 | async-start | bytes 524288 | tf_op jit(solution)/shard_map/all_to_all | solution.py:294
  20.0 17.2 %all-to-all-start.2 = ((bf16[8,128,512]{1,2,0:T(8,128)(2,1)}), bf16[8,128,512]{1,2,0:T(8,128)(2,1)S(1)}, u32[]{:S(2)}, u32[]{:S(2)}) async-start(bf16[8,128,512]{1,2,0:T(8,128)(2,1)} %bitcast.26), calls=%async_computation.2 | async-start | bytes 2097152 | tf_op jit(solution)/shard_map/all_to_all | solution.py:294
  24.2 19.4 %copy-start.39 = (bf16[16]{0:T(256)(128)(2,1)S(1)}, bf16[16]{0:T(256)(128)(2,1)}, u32[]{:S(2)}) copy-start(bf16[16]{0:T(256)(128)(2,1)} %param.27) | copy-start | bytes 100
  38.3 23.5 %copy-start.31 = (bf16[64,512]{1,0:T(8,128)(2,1)S(1)}, bf16[64,512]{1,0:T(8,128)(2,1)}, u32[]{:S(2)}) copy-start(bf16[64,512]{1,0:T(8,128)(2,1)} %param.26) | copy-start | bytes 196612
  38.3 17.2 %all-to-all-start = ((bf16[4,113,1024]{2,1,0:T(8,128)(2,1)}), bf16[4,113,1024]{2,1,0:T(8,128)(2,1)S(1)}, u32[]{:S(2)}, u32[]{:S(2)}) async-start(bf16[4,113,1024]{2,1,0:T(8,128)(2,1)} %broadcast_in_dim.95), calls=%async_computation | async-start | bytes 1966080 | tf_op jit(solution)/shard_map/all_to_all | solution.py:960
  55.4 13.7 %all-to-all-start.3 = ((bf16[32,2,712]{2,1,0:T(2,128)(2,1)}), bf16[32,2,712]{2,1,0:T(2,128)(2,1)}, u32[]{:S(2)}, u32[]{:S(2)}) async-start(bf16[32,2,712]{2,1,0:T(2,128)(2,1)} %reshape.404), calls=%async_computation.3 | async-start | bytes 196608 | tf_op jit(solution)/shard_map/all_to_all | solution.py:920
  61.7 92.2 %all-gather.9.cloned.1.call-start = ((), (), s32[]{:S(2)}) async-start(), calls=%async_computation.21 | async-start | bytes 5570560 | tf_op jit(solution)/shard_map/all_gather | solution.py:902
  69.1 44.0 %all-to-all-start.5 = ((bf16[8,64,2048]{2,1,0:T(8,128)(2,1)}), bf16[8,64,2048]{2,1,0:T(8,128)(2,1)}, u32[]{:S(2)}, u32[]{:S(2)}) async-start(bf16[8,64,2048]{2,1,0:T(8,128)(2,1)} %reshape.345), calls=%async_computation.5 | async-start | bytes 4194304 | tf_op jit(solution)/shard_map/all_to_all | solution.py:294
  115.7 81.3 %all-to-all-start.1 = ((bf16[8,128,2048]{2,1,0:T(8,128)(2,1)}), bf16[8,128,2048]{2,1,0:T(8,128)(2,1)}, u32[]{:S(2)}, u32[]{:S(2)}) async-start(bf16[8,128,2048]{2,1,0:T(8,128)(2,1)} %broadcast_in_dim.100), calls=%async_computation.1 | async-start | bytes 8388608 | tf_op jit(solution)/shard_map/all_to_all | solution.py:294
  122.8 188.6 %all-gather.7.cloned.1.call-start = ((), (), s32[]{:S(2)}) async-start(), calls=%async_computation.18 | async-start | bytes 1310720 | tf_op jit(solution)/shard_map/all_gather | solution.py:956
  123.5 224.2 %all-gather.5.cloned.1.call-start = ((), (), s32[]{:S(2)}) async-start(), calls=%async_computation.17 | async-start | bytes 10485760 | tf_op jit(solution)/shard_map/all_gather | solution.py:955
  211.3 90.6 %all-to-all-start.4 = ((bf16[8,1024,256]{1,2,0:T(8,128)(2,1)}), bf16[8,1024,256]{1,2,0:T(8,128)(2,1)}, u32[]{:S(2)}, u32[]{:S(2)}) async-start(bf16[8,1024,256]{1,2,0:T(8,128)(2,1)} %broadcast_in_dim.102), calls=%async_computation.4 | async-start | bytes 8388608 | tf_op jit(solution)/shard_map/all_to_all | solution.py:294
  516.8 87.5 %all-to-all-start.7 = ((bf16[8,1024,256]{2,1,0:T(8,128)(2,1)}), bf16[8,1024,256]{2,1,0:T(8,128)(2,1)}, u32[]{:S(2)}, u32[]{:S(2)}) async-start(bf16[8,1024,256]{2,1,0:T(8,128)(2,1)} %bitcast.255), calls=%async_computation.7 | async-start | bytes 8388608 | tf_op jit(solution)/shard_map/all_to_all | solution.py:294
  521.8 217.2 %reduce-scatter.3.cloned.1.call-start = ((), (), s32[]{:S(2)}) async-start(), calls=%async_computation.19 | async-start | bytes 10485760 | tf_op jit(solution)/shard_map/reduce_scatter | solution.py:1012
  522.4 85.0 %copy-start.10 = (f32[1024,512]{1,0:T(8,128)S(1)}, f32[1024,512]{1,0:T(8,128)}, u32[]{:S(2)}) copy-start(f32[1024,512]{1,0:T(8,128)} %copy-done.9) | copy-start | bytes 6291460
  615.8 75.6 %all-to-all-start.8 = ((bf16[8,128,2048]{2,1,0:T(8,128)(2,1)}), bf16[8,128,2048]{2,1,0:T(8,128)(2,1)}, u32[]{:S(2)}, u32[]{:S(2)}) async-start(bf16[8,128,2048]{2,1,0:T(8,128)(2,1)} %bitcast.253), calls=%async_computation.8 | async-start | bytes 8388608 | tf_op jit(solution)/shard_map/all_to_all | solution.py:294
  691.5 53.6 %all-to-all-start.13 = ((bf16[4,2,2,64,512]{4,3,2,1,0:T(8,128)(2,1)}), bf16[4,2,2,64,512]{4,3,2,1,0:T(8,128)(2,1)}, u32[]{:S(2)}, u32[]{:S(2)}) async-start(bf16[4,2,2,64,512]{4,3,2,1,0:T(8,128)(2,1)} %get-tuple-element.48), calls=%async_computation.15 | async-start | bytes 2097152 | tf_op jit(solution)/shard_map/all_to_all | solution.py:1013
  696.2 170.2 %reduce-scatter.5.cloned.1.call-start = ((), (), s32[]{:S(2)}) async-start(), calls=%async_computation.20 | async-start | bytes 5570560 | tf_op jit(solution)/shard_map/reduce_scatter | solution.py:1052
  745.0 60.7 %all-to-all-start.9 = ((bf16[32,144,128]{2,1,0:T(8,128)(2,1)}), bf16[32,144,128]{2,1,0:T(8,128)(2,1)S(1)}, u32[]{:S(2)}, u32[]{:S(2)}) async-start(bf16[32,144,128]{2,1,0:T(8,128)(2,1)} %pad_maximum_fusion.1), calls=%async_computation.9 | async-start | bytes 2359296 | tf_op jit(solution)/shard_map/all_to_all | solution.py:1112
  805.7 17.9 %all-to-all-start.14 = ((bf16[8,32,512]{2,1,0:T(8,128)(2,1)}), bf16[8,32,512]{2,1,0:T(8,128)(2,1)S(1)}, u32[]{:S(2)}, u32[]{:S(2)}) async-start(bf16[8,32,512]{2,1,0:T(8,128)(2,1)} %bitcast.119), calls=%async_computation.16 | async-start | bytes 524288 | tf_op jit(solution)/shard_map/all_to_all | solution.py:294
  824.5 34.2 %all-to-all-start.10 = ((f32[8,133,128]{2,1,0:T(8,128)}), f32[8,133,128]{2,1,0:T(8,128)S(1)}, u32[]{:S(2)}, u32[]{:S(2)}) async-start(f32[8,133,128]{2,1,0:T(8,128)} %broadcast_in_dim.109), calls=%async_computation.10 | async-start | bytes 1114112 | tf_op jit(solution)/shard_map/all_to_all | solution.py:1128
  858.6 32.0 %all-to-all-start.12 = ((bf16[8,64,2048]{2,1,0:T(8,128)(2,1)}), bf16[8,64,2048]{2,1,0:T(8,128)(2,1)S(1)}, u32[]{:S(2)}, u32[]{:S(2)}) async-start(bf16[8,64,2048]{2,1,0:T(8,128)(2,1)} %bitcast.261), calls=%async_computation.14 | async-start | bytes 4194304 | tf_op jit(solution)/shard_map/all_to_all | solution.py:294
  890.6 34.0 %all-to-all-start.11 = ((bf16[8,128,512]{2,1,0:T(8,128)(2,1)}), bf16[8,128,512]{2,1,0:T(8,128)(2,1)}, u32[]{:S(2)}, u32[]{:S(2)}) async-start(bf16[8,128,512]{2,1,0:T(8,128)(2,1)} %bitcast.108), calls=%async_computation.13 | async-start | bytes 2097152 | tf_op jit(solution)/shard_map/all_to_all | solution.py:294
  (36 other events, 198.1 us)
Sparse Core Ops, SparseCore 0:
  64.3 89.4 all-gather.8
  155.7 35.1 all-gather.6
  192.7 154.9 all-gather.4
  525.4 154.6 reduce-scatter.2
  739.2 125.3 reduce-scatter.4

commit v4 on v3

--- a/solution.py
+++ b/solution.py
@@ -193,39 +193,14 @@
     return token_ids.reshape(-1)[:, None] == lax.broadcasted_iota(jnp.int32, (1, vocab_size), 1)
 
 
-def pool_tokens(token_ids, char_table, weights, counts, tight_from):
+def embed_tokens(token_ids, char_table):
     tokens = token_ids.shape[0]
     padded = jnp.pad(token_ids, ((0, 0), (0, PLACES - token_ids.shape[1])), constant_values=-1)
     table_tiled = jnp.pad(jnp.tile(char_table, (1, WIDEST)), ((0, 0), (0, LANES - TAPS)))
     selector = char_selector(padded, char_table.shape[0]).astype(jnp.bfloat16)
     tiled = jnp.dot(selector, table_tiled, preferred_element_type=jnp.float32)
     tiled = tiled.astype(jnp.bfloat16).reshape(tokens, PLACES, LANES)
-    block = math.gcd(tokens, TOKEN_BLOCK)
-    total = weights.shape[1]
-    features, pooled_lse = pl.pallas_call(
-        partial(pool_kernel, tight_from),
-        grid=(tokens // block,),
-        in_specs=[
-            pl.BlockSpec((block, PLACES, LANES), lambda i: (i, 0, 0)),
-            pl.BlockSpec((LANES, total), lambda i: (0, 0)),
-            pl.BlockSpec((8, total), lambda i: (0, 0)),
-        ],
-        out_specs=[
-            pl.BlockSpec((block, total), lambda i: (i, 0)),
-            pl.BlockSpec((block, total), lambda i: (i, 0)),
-        ],
-        out_shape=[
-            jax.ShapeDtypeStruct((tokens, total), jnp.bfloat16),
-            jax.ShapeDtypeStruct((tokens, total), jnp.float32),
-        ],
-        scratch_shapes=[
-            pltpu.VMEM((block * PLACES, LANES), jnp.bfloat16),
-            pltpu.VMEM((block * TIGHT, LANES), jnp.bfloat16),
-        ],
-        compiler_params=pltpu.CompilerParams(vmem_limit_bytes=40 * 1024 * 1024),
-        name="pool_tokens",
-    )(tiled, weights, counts)
-    return (padded, tiled, features, pooled_lse)
+    return (padded, tiled)
 
 
 def pool_grads(padded, tiled, weights, counts, pooled_lse, upstream, vocab_size, tight_from):
@@ -366,16 +341,17 @@
         for t in range(t_size)
         for y in range(y_size)
     ]
-    run = weight_hbm.shape[3]
+    run = weight_hbm.shape[4]
     turned_run = turned_hbm.shape[3]
 
     for d in range(2):
         for source, t, at in blocks:
-            pltpu.make_async_copy(
-                weight_hbm.at[source, t, d],
-                weight_ref.at[d, pl.ds(at * run, run)],
-                load_sems.at[0],
-            ).start()
+            for q in range(4):
+                pltpu.make_async_copy(
+                    weight_hbm.at[source, t, d, q],
+                    weight_ref.at[d, pl.ds(at * run, run), pl.ds(q * cells, cells)],
+                    load_sems.at[0],
+                ).start()
             pltpu.make_async_copy(
                 turned_hbm.at[source, t, d],
                 proj_ref.at[d, pl.ds(at * turned_run, turned_run)],
@@ -722,7 +698,7 @@
         out_specs=[vmem, hbm, hbm, vmem],
         out_shape=[
             jax.ShapeDtypeStruct(parts.shape, bf16),
-            jax.ShapeDtypeStruct(weights.shape, bf16),
+            jax.ShapeDtypeStruct(weights.shape[:3] + (weights.shape[4], 4 * cells), bf16),
             jax.ShapeDtypeStruct(turned.shape, bf16),
             jax.ShapeDtypeStruct((2, 8, 4 * cells), f32),
         ],
@@ -762,6 +738,905 @@
     )(parts, lin_bias, out_grad, weights, turned, bias, keep)
 
 
+def member_at(offset):
+    t_size, x_size, c_size = lax.axis_size("t"), lax.axis_size("x"), lax.axis_size("c")
+    dt, dx, dc = offset // (x_size * c_size), lax.rem(offset // c_size, x_size), lax.rem(offset, c_size)
+    t = lax.rem(lax.axis_index("t") + dt, t_size)
+    x = lax.rem(lax.axis_index("x") + dx, x_size)
+    c = lax.rem(lax.axis_index("c") + dc, c_size)
+    return (t * x_size + x) * c_size + c
+
+
+def opposite(offset):
+    t_size, x_size, c_size = lax.axis_size("t"), lax.axis_size("x"), lax.axis_size("c")
+    dt, dx, dc = offset // (x_size * c_size), offset // c_size % x_size, offset % c_size
+    return (-dt % t_size * x_size + -dx % x_size) * c_size + -dc % c_size
+
+
+def send_block(source, target, send_sem, recv_sem, peer):
+    pltpu.make_async_remote_copy(
+        src_ref=source,
+        dst_ref=target,
+        send_sem=send_sem,
+        recv_sem=recv_sem,
+        device_id=team_coords(peer),
+        device_id_type=pl.DeviceIdType.MESH,
+    ).start()
+
+
+def greet(offsets, with_grid=False):
+    barrier = pltpu.get_barrier_semaphore()
+    for offset in offsets:
+        pl.semaphore_signal(
+            barrier,
+            inc=1,
+            device_id=team_coords(member_at(offset)),
+            device_id_type=pl.DeviceIdType.MESH,
+        )
+    extra = greet_grid(barrier) if with_grid else 0
+    pl.semaphore_wait(barrier, len(offsets) + extra)
+
+
+def load_highway(first_hbm, weights, project, sems):
+    grid = first_hbm.shape[0]
+    team = team_size()
+    run = project.shape[0] // grid
+
+    @pl.loop(0, team)
+    def _(member):
+        for block in range(grid):
+            for level in range(2):
+                pltpu.make_async_copy(
+                    first_hbm.at[
+                        block, pl.ds(pl.multiple_of((member * 2 + level) * run, run), run)
+                    ],
+                    weights.at[
+                        level, pl.ds(pl.multiple_of((member * grid + block) * run, run), run)
+                    ],
+                    sems.at[0],
+                ).start()
+
+    for block in range(grid):
+        pltpu.make_async_copy(
+            first_hbm.at[block, pl.ds(team * 2 * run, run)],
+            project.at[pl.ds(block * run, run)],
+            sems.at[1],
+        ).start()
+
+
+def grid_coords(dg, dy):
+    g_size, y_size = lax.axis_size("g"), lax.axis_size("y")
+    return {
+        "g": lax.rem(lax.axis_index("g") + dg, g_size),
+        "y": lax.rem(lax.axis_index("y") + dy, y_size),
+    }
+
+
+def grid_block(dg, dy):
+    coords = grid_coords(dg, dy)
+    return coords["g"] * lax.axis_size("y") + coords["y"]
+
+
+def send_grid(source, target, send_sem, recv_sem, dg, dy):
+    pltpu.make_async_remote_copy(
+        src_ref=source,
+        dst_ref=target,
+        send_sem=send_sem,
+        recv_sem=recv_sem,
+        device_id=grid_coords(dg, dy),
+        device_id_type=pl.DeviceIdType.MESH,
+    ).start()
+
+
+def greet_grid(barrier):
+    for dg in range(1, lax.axis_size("g")):
+        pl.semaphore_signal(
+            barrier, inc=1, device_id=grid_coords(dg, 0), device_id_type=pl.DeviceIdType.MESH
+        )
+    pl.semaphore_signal(
+        barrier, inc=1, device_id=grid_coords(0, 1), device_id_type=pl.DeviceIdType.MESH
+    )
+    return lax.axis_size("g")
+
+
+class Gather:
+    def __init__(self, blocks, targets, send_sem, recv_sems):
+        self.blocks = blocks
+        self.targets = targets
+        self.send_sem = send_sem
+        self.recv_sems = recv_sems
+
+    def start(self, pieces):
+        home = grid_block(0, 0)
+        g_size = lax.axis_size("g")
+        for piece in pieces:
+            source = self.blocks[piece]
+            target = self.targets[piece](home)
+            for dg in range(1, g_size):
+                send_grid(
+                    source, target, self.send_sem, self.recv_sems.at[piece, g_size - dg, 0], dg, 0
+                )
+            send_grid(source, target, self.send_sem, self.recv_sems.at[piece, 0, 1], 0, 1)
+
+    def forward(self, pieces):
+        for piece in pieces:
+            for dg in range(1, lax.axis_size("g")):
+                target = self.targets[piece](grid_block(dg, 0))
+                wait_bytes(target, self.recv_sems.at[piece, dg, 0])
+                send_grid(target, target, self.send_sem, self.recv_sems.at[piece, dg, 1], 0, 1)
+
+    def finish(self, pieces):
+        for piece in pieces:
+            for dg in range(lax.axis_size("g")):
+                wait_bytes(self.targets[piece](grid_block(dg, 1)), self.recv_sems.at[piece, dg, 1])
+
+    def sent(self, pieces):
+        for piece in pieces:
+            for _ in range(2 * lax.axis_size("g") - 1):
+                wait_bytes(self.blocks[piece], self.send_sem)
+
+
+def row_pieces(total, parts):
+    step = -(-total // (parts * 16)) * 16
+    return [(start, min(step, total - start)) for start in range(0, total, step)]
+
+
+def highway_kernel(
+    tight_from,
+    tiled_ref,
+    filter_ref,
+    count_ref,
+    block_hbm,
+    lstm_block_hbm,
+    turned_block_hbm,
+    bias_ref,
+    lse_ref,
+    first_hbm,
+    lstm_hbm,
+    turned_hbm,
+    first_ref,
+    second_ref,
+    mixed_ref,
+    hidden_ref,
+    top_ref,
+    parts_ref,
+    features_own,
+    wide,
+    tight,
+    weights,
+    project,
+    load_sems,
+    send_sems,
+    first_sems,
+    second_sems,
+    gather_send_sems,
+    block_sems,
+    turned_sems,
+    lstm_sems,
+):
+    team, tokens, features = first_ref.shape
+    part = features // team
+    cores = lax.axis_size("c")
+    g_size, y_size = lax.axis_size("g"), lax.axis_size("y")
+    place = team_place()
+    sibling = member_at(1)
+    near = list(range(cores, team, cores))
+    chunks = lstm_block_hbm.shape[0]
+    greet([1] + near, True)
+    home = grid_block(0, 0)
+    places = [pl.ds(start, size) for start, size in row_pieces(block_hbm.shape[0], 8)]
+    block_gather = Gather(
+        [block_hbm.at[rows] for rows in places],
+        [lambda at, rows=rows: first_hbm.at[at, rows] for rows in places],
+        gather_send_sems.at[0],
+        block_sems,
+    )
+    turned_gather = Gather(
+        [turned_block_hbm],
+        [lambda at: turned_hbm.at[at]],
+        gather_send_sems.at[1],
+        turned_sems,
+    )
+    all_places = list(range(len(places)))
+    block_gather.start(all_places)
+    pltpu.make_async_copy(block_hbm, first_hbm.at[home], load_sems.at[2]).start()
+    pltpu.make_async_copy(turned_block_hbm, turned_hbm.at[home], load_sems.at[3]).start()
+    pltpu.make_async_copy(lstm_block_hbm, lstm_hbm.at[home], load_sems.at[4]).start()
+
+    def columns(member):
+        return pl.ds(pl.multiple_of(member * part, part), part)
+
+    token_block = wide.shape[0] // tiled_ref.shape[1]
+
+    @pl.loop(0, tokens // token_block)
+    def _(step):
+        rows = pl.ds(pl.multiple_of(step * token_block, token_block), token_block)
+        pool_kernel(
+            tight_from,
+            tiled_ref.at[rows],
+            filter_ref,
+            count_ref,
+            features_own.at[rows],
+            lse_ref.at[rows],
+            wide,
+            tight,
+        )
+
+    g, t, y, x, c = axis_sizes()
+    run = part // (g * y)
+    natural = features_own[...]
+    starts = [
+        ((((gi * t + ti) * y + yi) * x + xi) * c + ci) * run
+        for ti in range(t)
+        for xi in range(x)
+        for ci in range(c)
+        for gi in range(g)
+        for yi in range(y)
+    ]
+    features_own[...] = jnp.concatenate([natural[:, at : at + run] for at in starts], axis=1)
+
+    for offset in near + [1]:
+        send_block(
+            features_own,
+            first_ref.at[place],
+            send_sems.at[0],
+            first_sems.at[opposite(offset)],
+            member_at(offset),
+        )
+    first_ref[place] = features_own[...]
+    block_gather.forward(all_places)
+
+    def lstm_start(chunk):
+        for dg in range(1, g_size):
+            send_grid(
+                lstm_block_hbm.at[chunk],
+                lstm_hbm.at[home, chunk],
+                gather_send_sems.at[2],
+                lstm_sems.at[chunk, g_size - dg, 0],
+                dg,
+                0,
+            )
+
+    def lstm_forward(chunk):
+        for dg in range(1, g_size):
+            target = lstm_hbm.at[grid_block(dg, 0), chunk]
+            wait_bytes(target, lstm_sems.at[chunk, dg, 0])
+            send_grid(
+                target, target, gather_send_sems.at[3], lstm_sems.at[chunk, dg, 1], 0, 1
+            )
+
+    def pump(chunk):
+        @pl.when(chunk < chunks)
+        def _():
+            lstm_forward(jnp.minimum(chunk, chunks - 1))
+
+            @pl.when(chunk + 2 < chunks)
+            def _():
+                lstm_start(jnp.minimum(chunk + 2, chunks - 1))
+
+    turned_gather.start([0])
+    lstm_start(0)
+    lstm_start(1)
+    for offset in near:
+        member = member_at(offset)
+        wait_bytes(first_ref.at[member], first_sems.at[offset])
+        send_block(
+            first_ref.at[member],
+            first_ref.at[member],
+            send_sems.at[0],
+            first_sems.at[offset + 1],
+            sibling,
+        )
+    block_gather.finish(all_places)
+    wait_bytes(block_hbm, load_sems.at[2])
+    load_highway(first_hbm, weights, project, load_sems)
+
+    @pl.loop(0, chunks)
+    def _(chunk):
+        send_grid(
+            lstm_block_hbm.at[chunk],
+            lstm_hbm.at[home, chunk],
+            gather_send_sems.at[4],
+            lstm_sems.at[chunk, 0, 1],
+            0,
+            1,
+        )
+
+    wait_bytes(weights, load_sems.at[0])
+    wait_bytes(project, load_sems.at[1])
+
+    def mix(level, member, operand):
+        mixed = (
+            jnp.dot(operand, weights[level], preferred_element_type=jnp.float32)
+            + bias_ref[level : level + 1]
+        )
+        mixed_ref[level, member] = mixed
+        gate = sigmoid(mixed[:, part:])
+        pre_act = mixed[:, :part]
+        return (gate, pre_act * sigmoid(pre_act))
+
+    @pl.loop(0, team)
+    def _(offset):
+        member = member_at(offset)
+
+        @pl.when(lax.rem(offset, cores) == 1)
+        def _():
+            wait_bytes(first_ref.at[member], first_sems.at[offset])
+
+        gate, act = mix(0, member, first_ref[member])
+        carried = first_ref[member, :, columns(place)].astype(jnp.float32)
+        hidden = gate * carried + (1.0 - gate) * act
+        hidden_ref[member] = hidden
+        mine = second_ref.at[member, :, columns(place)]
+        mine[...] = hidden.astype(jnp.bfloat16)
+        for to in near + [1]:
+            send_block(
+                mine,
+                mine,
+                send_sems.at[1],
+                second_sems.at[member, opposite(to)],
+                member_at(to),
+            )
+        pump(offset)
+
+    @pl.loop(0, team + 1)
+    def _(step):
+        @pl.when(step < team)
+        def _():
+            member = member_at(jnp.minimum(step, team - 1))
+            for origin in near:
+                piece = second_ref.at[member, :, columns(member_at(origin))]
+                wait_bytes(piece, second_sems.at[member, origin])
+                send_block(
+                    piece,
+                    piece,
+                    send_sems.at[1],
+                    second_sems.at[member, origin + 1],
+                    sibling,
+                )
+
+        @pl.when(step > 0)
+        def _():
+            member = member_at(jnp.maximum(step - 1, 0))
+            for origin in [0] + near:
+                piece = second_ref.at[member, :, columns(member_at(origin + 1))]
+                wait_bytes(piece, second_sems.at[member, origin + 1])
+            gate, act = mix(1, member, second_ref[member])
+            top = (gate * hidden_ref[member] + (1.0 - gate) * act).astype(jnp.bfloat16)
+            top_ref[member] = top
+            parts_ref[member] = jnp.dot(
+                top, project[...], preferred_element_type=jnp.float32
+            ).astype(jnp.bfloat16)
+
+        pump(team + step)
+
+    @pl.loop(2 * team + 1, max(chunks, 2 * team + 1))
+    def _(chunk):
+        pump(chunk)
+
+    turned_gather.forward([0])
+    turned_gather.finish([0])
+
+    @pl.loop(0, chunks)
+    def _(chunk):
+        for dg in range(g_size):
+            wait_bytes(lstm_hbm.at[grid_block(dg, 1), chunk], lstm_sems.at[chunk, dg, 1])
+
+    wait_bytes(first_ref.at[pl.ds(0, team - 1)], send_sems.at[0])
+    wait_bytes(second_ref.at[pl.ds(0, team - 1)], send_sems.at[1])
+    block_gather.sent(all_places)
+    turned_gather.sent([0])
+    for _ in range(g_size - 1):
+        wait_bytes(lstm_block_hbm, gather_send_sems.at[2])
+        wait_bytes(lstm_block_hbm, gather_send_sems.at[3])
+    wait_bytes(lstm_block_hbm, gather_send_sems.at[4])
+    wait_bytes(turned_block_hbm, load_sems.at[3])
+    wait_bytes(lstm_block_hbm, load_sems.at[4])
+
+
+def run_highway(tight_from, tiled, filters, counts, block, lstm_block, turned_block, bias):
+    team = team_size()
+    tokens, features = tiled.shape[0], filters.shape[1]
+    part = features // team
+    g_size, y_size = lax.axis_size("g"), lax.axis_size("y")
+    grid = g_size * y_size
+    width = block.shape[1]
+    bf16, f32 = jnp.bfloat16, jnp.float32
+    vmem = pl.BlockSpec(memory_space=pltpu.VMEM)
+    hbm = pl.BlockSpec(memory_space=pl.ANY)
+    pieces = len(row_pieces(block.shape[0], 8))
+    token_block = math.gcd(tokens, TOKEN_BLOCK)
+    return pl.pallas_call(
+        partial(highway_kernel, tight_from),
+        in_specs=[vmem] * 3 + [hbm] * 3 + [vmem],
+        out_specs=[vmem] + [hbm] * 3 + [vmem] * 6,
+        out_shape=[
+            jax.ShapeDtypeStruct((tokens, features), f32),
+            jax.ShapeDtypeStruct((grid,) + block.shape, bf16),
+            jax.ShapeDtypeStruct((grid,) + lstm_block.shape, bf16),
+            jax.ShapeDtypeStruct((grid,) + turned_block.shape, bf16),
+            jax.ShapeDtypeStruct((team, tokens, features), bf16),
+            jax.ShapeDtypeStruct((team, tokens, features), bf16),
+            jax.ShapeDtypeStruct((2, team, tokens, 2 * part), f32),
+            jax.ShapeDtypeStruct((team, tokens, part), f32),
+            jax.ShapeDtypeStruct((team, tokens, part), bf16),
+            jax.ShapeDtypeStruct((team, tokens, width), bf16),
+        ],
+        scratch_shapes=[
+            pltpu.VMEM((tokens, features), bf16),
+            pltpu.VMEM((token_block * PLACES, LANES), bf16),
+            pltpu.VMEM((token_block * TIGHT, LANES), bf16),
+            pltpu.VMEM((2, features, 2 * part), bf16),
+            pltpu.VMEM((part, width), bf16),
+            pltpu.SemaphoreType.DMA((5,)),
+            pltpu.SemaphoreType.DMA((2,)),
+            pltpu.SemaphoreType.DMA((team,)),
+            pltpu.SemaphoreType.DMA((team, team)),
+            pltpu.SemaphoreType.DMA((5,)),
+            pltpu.SemaphoreType.DMA((pieces, g_size, y_size)),
+            pltpu.SemaphoreType.DMA((1, g_size, y_size)),
+            pltpu.SemaphoreType.DMA((lstm_block.shape[0], g_size, y_size)),
+        ],
+        compiler_params=pltpu.CompilerParams(
+            collective_id=2, has_side_effects=True, vmem_limit_bytes=60 * 1024 * 1024
+        ),
+        name="highway_team",
+    )(tiled, filters, counts, block, lstm_block, turned_block, bias)
+
+
+def highway_back_kernel(
+    grad_lin_ref,
+    first_hbm,
+    first_ref,
+    second_ref,
+    mixed_ref,
+    hidden_ref,
+    top_ref,
+    features_ref,
+    grads_hbm,
+    bias_ref,
+    weights,
+    project,
+    grad_mixed,
+    direct,
+    column_parts,
+    column_sibling,
+    column_send,
+    column_recv,
+    column_sum_own,
+    row_part,
+    row_keep,
+    row_give,
+    row_sibling,
+    row_send,
+    row_recv,
+    row_sum_own,
+    grad_stage,
+    load_sems,
+    send_sems,
+    column_sib_sems,
+    column_sems,
+    row_sib_sems,
+    row_sems,
+    out_sems,
+):
+    team, tokens, features = first_ref.shape
+    part = features // team
+    grid = first_hbm.shape[0]
+    run = part // grid
+    cores = lax.axis_size("c")
+    chips = team // cores
+    place = team_place()
+    sibling = member_at(1)
+    near = list(range(1, chips))
+    load_highway(first_hbm, weights, project, load_sems)
+    greet([1] + [chip * cores for chip in near])
+    f32, bf16 = jnp.float32, jnp.bfloat16
+
+    def columns(member):
+        return pl.ds(pl.multiple_of(member * part, part), part)
+
+    def opposite_chip(chip):
+        return opposite(chip * cores) // cores
+
+    wait_bytes(weights, load_sems.at[0])
+    wait_bytes(project, load_sems.at[1])
+
+    def mix_grads(level, member, grad, carried):
+        pre_act = mixed_ref[level, member, :, pl.ds(0, part)]
+        gate = sigmoid(mixed_ref[level, member, :, pl.ds(part, part)])
+        act_sig = sigmoid(pre_act)
+        grad_mixed[level, member, :, pl.ds(0, part)] = (
+            grad * (1.0 - gate) * act_sig * (1.0 + pre_act * (1.0 - act_sig))
+        ).astype(bf16)
+        grad_mixed[level, member, :, pl.ds(part, part)] = (
+            grad * (carried - pre_act * act_sig) * gate * (1.0 - gate)
+        ).astype(bf16)
+        return grad * gate
+
+    def spread(level, member):
+        return lax.dot_general(
+            grad_mixed[level, member],
+            weights[level],
+            (((1,), (1,)), ((), ())),
+            preferred_element_type=f32,
+        )
+
+    @pl.loop(0, team)
+    def _(member):
+        grad = lax.dot_general(
+            grad_lin_ref[member], project[...], (((1,), (1,)), ((), ())), preferred_element_type=f32
+        )
+        direct[member] = mix_grads(1, member, grad, hidden_ref[member])
+        column_parts[member] = spread(1, member).astype(bf16)
+        for chip in range(chips):
+            send_block(
+                column_parts.at[member, :, columns(member_at(chip * cores + 1))],
+                column_sibling.at[member, chip],
+                send_sems.at[0],
+                column_sib_sems.at[member],
+                sibling,
+            )
+
+    @pl.loop(0, team)
+    def _(member):
+        wait_bytes(column_sibling.at[member], column_sib_sems.at[member])
+        for chip in near + [0]:
+            target = member_at(chip * cores)
+            both = column_parts[member, :, columns(target)].astype(f32) + column_sibling[
+                member, chip
+            ].astype(f32)
+            if chip == 0:
+                column_sum_own[member] = both
+            else:
+                column_send[chip - 1, member] = both.astype(bf16)
+                send_block(
+                    column_send.at[chip - 1, member],
+                    column_recv.at[opposite_chip(chip) - 1, member],
+                    send_sems.at[1],
+                    column_sems.at[member, opposite_chip(chip) - 1],
+                    target,
+                )
+
+    def weight_grads(level, source_ref):
+        @pl.loop(0, team)
+        def _(member):
+            slot = lax.rem(member, 2)
+
+            @pl.when(member >= 2)
+            def _():
+                wait_bytes(grad_stage.at[slot], out_sems.at[slot])
+
+            grad_stage[slot] = lax.dot_general(
+                source_ref[:, :, columns(member)].reshape(team * tokens, part),
+                grad_mixed[level].reshape(team * tokens, 2 * part),
+                (((0,), (0,)), ((), ())),
+                preferred_element_type=f32,
+            ).astype(bf16)
+            for block in range(grid):
+                pltpu.make_async_copy(
+                    grad_stage.at[slot, pl.ds(block * run, run)],
+                    grads_hbm.at[
+                        block, pl.ds(pl.multiple_of((member * 2 + level) * run, run), run)
+                    ],
+                    out_sems.at[slot],
+                ).start()
+
+        for slot in range(2):
+            wait_bytes(grad_stage.at[slot], out_sems.at[slot])
+        bias_ref[level] = jnp.dot(
+            jnp.ones((8, team * tokens), bf16),
+            grad_mixed[level].reshape(team * tokens, 2 * part),
+            preferred_element_type=f32,
+        )
+
+    weight_grads(1, second_ref)
+
+    @pl.loop(0, team)
+    def _(step):
+        offset = team - 1 - step
+        member = member_at(offset)
+        chip = offset // cores
+        grad = column_sum_own[member] + direct[member]
+        for other in near:
+            wait_bytes(column_recv.at[other - 1, member], column_sems.at[member, other - 1])
+            grad = grad + column_recv[other - 1, member].astype(f32)
+        carried = first_ref[member, :, columns(place)].astype(f32)
+        straight = mix_grads(0, member, grad, carried)
+        row_part[...] = spread(0, member)
+        row_part[:, columns(place)] += straight
+
+        @pl.when(lax.rem(offset, cores) == 1)
+        def _():
+            row_give[chip] = row_part[...].astype(bf16)
+            send_block(
+                row_give.at[chip],
+                row_sibling.at[chip],
+                send_sems.at[2],
+                row_sib_sems.at[chip],
+                sibling,
+            )
+
+        @pl.when(lax.rem(offset, cores) == 0)
+        def _():
+            row_keep[chip] = row_part[...].astype(bf16)
+
+    for chip in near[::-1] + [0]:
+        wait_bytes(row_sibling.at[chip], row_sib_sems.at[chip])
+        both = row_keep[chip].astype(f32) + row_sibling[chip].astype(f32)
+        if chip == 0:
+            row_sum_own[...] = both
+        else:
+            row_send[chip - 1] = both.astype(bf16)
+            send_block(
+                row_send.at[chip - 1],
+                row_recv.at[opposite_chip(chip) - 1],
+                send_sems.at[3],
+                row_sems.at[opposite_chip(chip) - 1],
+                member_at(chip * cores),
+            )
+
+    weight_grads(0, first_ref)
+    grad_stage[0] = lax.dot_general(
+        top_ref[...].reshape(team * tokens, part),
+        grad_lin_ref[...].reshape(team * tokens, 2 * part),
+        (((0,), (0,)), ((), ())),
+        preferred_element_type=f32,
+    ).astype(bf16)
+    for block in range(grid):
+        pltpu.make_async_copy(
+            grad_stage.at[0, pl.ds(block * run, run)],
+            grads_hbm.at[block, pl.ds(team * 2 * run, run)],
+            out_sems.at[0],
+        ).start()
+    total = row_sum_own[...]
+    for other in near:
+        wait_bytes(row_recv.at[other - 1], row_sems.at[other - 1])
+        total = total + row_recv[other - 1].astype(f32)
+    features_ref[...] = total.astype(bf16)
+    wait_bytes(grad_stage.at[0], out_sems.at[0])
+    wait_bytes(column_sibling, send_sems.at[0])
+    wait_bytes(column_send, send_sems.at[1])
+    wait_bytes(row_give, send_sems.at[2])
+    wait_bytes(row_send, send_sems.at[3])
+
+
+def run_highway_back(grad_lin, first_all, first, second, mixed, hidden, top):
+    team, tokens, features = first.shape
+    part = features // team
+    chips = team // lax.axis_size("c")
+    width = first_all.shape[2]
+    bf16, f32 = jnp.bfloat16, jnp.float32
+    vmem = pl.BlockSpec(memory_space=pltpu.VMEM)
+    hbm = pl.BlockSpec(memory_space=pl.ANY)
+    return pl.pallas_call(
+        highway_back_kernel,
+        in_specs=[vmem, hbm] + [vmem] * 5,
+        out_specs=[vmem, hbm, vmem],
+        out_shape=[
+            jax.ShapeDtypeStruct((tokens, features), bf16),
+            jax.ShapeDtypeStruct(first_all.shape, bf16),
+            jax.ShapeDtypeStruct((2, 8, 2 * part), f32),
+        ],
+        scratch_shapes=[
+            pltpu.VMEM((2, features, 2 * part), bf16),
+            pltpu.VMEM((part, width), bf16),
+            pltpu.VMEM((2, team, tokens, 2 * part), bf16),
+            pltpu.VMEM((team, tokens, part), f32),
+            pltpu.VMEM((team, tokens, features), bf16),
+            pltpu.VMEM((team, chips, tokens, part), bf16),
+            pltpu.VMEM((chips - 1, team, tokens, part), bf16),
+            pltpu.VMEM((chips - 1, team, tokens, part), bf16),
+            pltpu.VMEM((team, tokens, part), f32),
+            pltpu.VMEM((tokens, features), f32),
+            pltpu.VMEM((chips, tokens, features), bf16),
+            pltpu.VMEM((chips, tokens, features), bf16),
+            pltpu.VMEM((chips, tokens, features), bf16),
+            pltpu.VMEM((chips - 1, tokens, features), bf16),
+            pltpu.VMEM((chips - 1, tokens, features), bf16),
+            pltpu.VMEM((tokens, features), f32),
+            pltpu.VMEM((2, part, width), bf16),
+            pltpu.SemaphoreType.DMA((2,)),
+            pltpu.SemaphoreType.DMA((4,)),
+            pltpu.SemaphoreType.DMA((team,)),
+            pltpu.SemaphoreType.DMA((team, chips - 1)),
+            pltpu.SemaphoreType.DMA((chips,)),
+            pltpu.SemaphoreType.DMA((chips - 1,)),
+            pltpu.SemaphoreType.DMA((2,)),
+        ],
+        compiler_params=pltpu.CompilerParams(
+            collective_id=3, has_side_effects=True, vmem_limit_bytes=60 * 1024 * 1024
+        ),
+        name="highway_team_back",
+    )(grad_lin, first_all, first, second, mixed, hidden, top)
+
+
+def every_coords(shift):
+    g, t, y, x, c = axis_sizes()
+    sizes = (g, t, y, x, c)
+    coords, rest = {}, shift
+    for name, size in list(zip(EVERY, sizes))[::-1]:
+        coords[name] = lax.rem(lax.axis_index(name) + lax.rem(rest, size), size)
+        rest = rest // size
+    return coords
+
+
+def every_place(coords):
+    place = 0
+    for name in EVERY:
+        place = place * lax.axis_size(name) + coords[name]
+    return place
+
+
+def return_kernel(
+    shared,
+    grads_ref,
+    small_ref,
+    team_ref,
+    project_ref,
+    sums_ref,
+    shared_ref,
+    y_recv,
+    g_send,
+    g_recv,
+    kept,
+    team_send,
+    small_recv,
+    y_sems,
+    g_sems,
+    team_sems,
+    small_sems,
+    send_sems,
+):
+    grid, rows, lanes = grads_ref.shape
+    team = team_size()
+    g_size, y_size = lax.axis_size("g"), lax.axis_size("y")
+    devices = small_ref.shape[0]
+    groups = shared_ref.shape[0]
+    cut = team_ref.shape[1] * team
+    step = team_ref.shape[1]
+    f32, bf16 = jnp.float32, jnp.bfloat16
+    here = every_place({name: lax.axis_index(name) for name in EVERY})
+    place = team_place()
+    barrier = pltpu.get_barrier_semaphore()
+
+    @pl.loop(1, devices)
+    def _(shift):
+        pl.semaphore_signal(
+            barrier, inc=1, device_id=every_coords(shift), device_id_type=pl.DeviceIdType.MESH
+        )
+
+    pl.semaphore_wait(barrier, devices - 1)
+    pieces = [pl.ds(k * step, step) for k in range(team)] + [pl.ds(cut, rows - cut)]
+    g_index, y_index = lax.axis_index("g"), lax.axis_index("y")
+    other_y = lax.rem(y_index + 1, y_size)
+    for k, piece in enumerate(pieces):
+        for dg in list(range(1, g_size)) + [0]:
+            g = lax.rem(g_index + dg, g_size)
+            send_grid(
+                grads_ref.at[g * y_size + other_y, piece],
+                y_recv.at[dg, piece],
+                send_sems.at[0],
+                y_sems.at[k, dg],
+                0,
+                1,
+            )
+
+    @pl.loop(1, devices)
+    def _(shift):
+        coords = every_coords(shift)
+        pltpu.make_async_remote_copy(
+            src_ref=small_ref.at[every_place(coords)],
+            dst_ref=small_recv.at[here],
+            send_sem=send_sems.at[3],
+            recv_sem=small_sems.at[0],
+            device_id=coords,
+            device_id_type=pl.DeviceIdType.MESH,
+        ).start()
+
+    small_recv[here] = small_ref[here]
+    for k, piece in enumerate(pieces):
+        for dg in list(range(1, g_size)) + [0]:
+            g = lax.rem(g_index + dg, g_size)
+            wait_bytes(y_recv.at[dg, piece], y_sems.at[k, dg])
+            both = grads_ref[g * y_size + y_index, piece].astype(f32) + y_recv[dg, piece].astype(f32)
+            if dg == 0:
+                kept[piece] = both
+            else:
+                g_send[dg - 1, piece] = both.astype(bf16)
+                send_grid(
+                    g_send.at[dg - 1, piece],
+                    g_recv.at[g_size - dg - 1, piece],
+                    send_sems.at[1],
+                    g_sems.at[k, g_size - dg - 1],
+                    dg,
+                    0,
+                )
+
+    wait_bytes(small_recv.at[pl.ds(0, devices - 1)], small_sems.at[0])
+    sums_ref[...] = jnp.sum(small_recv[...].astype(f32), axis=0)
+    group = (g_index * lax.axis_size("t") + lax.axis_index("t")) * y_size + y_index
+    banks = devices // groups
+
+    @pl.loop(1, groups)
+    def _(shift):
+        coords = every_coords(shift * banks)
+        pltpu.make_async_remote_copy(
+            src_ref=sums_ref.at[pl.ds(0, shared)],
+            dst_ref=shared_ref.at[group],
+            send_sem=send_sems.at[4],
+            recv_sem=small_sems.at[1],
+            device_id=coords,
+            device_id_type=pl.DeviceIdType.MESH,
+        ).start()
+
+    shared_ref[group] = sums_ref[pl.ds(0, shared)]
+    for k, piece in enumerate(pieces):
+        total = kept[piece]
+        for dg in range(1, g_size):
+            wait_bytes(g_recv.at[dg - 1, piece], g_sems.at[k, dg - 1])
+            total = total + g_recv[dg - 1, piece].astype(f32)
+        if k == team:
+            project_ref[...] = total
+        else:
+            team_send[piece] = total.astype(bf16)
+
+            @pl.when(place == k)
+            def _():
+                team_ref[k] = team_send[piece]
+
+            @pl.when(place != k)
+            def _():
+                send_block(
+                    team_send.at[piece], team_ref.at[place], send_sems.at[2], team_sems.at[0], k
+                )
+
+    wait_bytes(team_ref.at[pl.ds(0, team - 1)], team_sems.at[0])
+    wait_bytes(shared_ref.at[pl.ds(0, groups - 1)], small_sems.at[1])
+    wait_bytes(y_recv, send_sems.at[0])
+    wait_bytes(g_recv, send_sems.at[1])
+    wait_bytes(team_ref.at[pl.ds(0, team - 1)], send_sems.at[2])
+    wait_bytes(small_recv.at[pl.ds(0, devices - 1)], send_sems.at[3])
+    wait_bytes(shared_ref.at[pl.ds(0, groups - 1)], send_sems.at[4])
+
+
+def run_return(grads, small, step, shared, groups):
+    grid, rows, lanes = grads.shape
+    team = team_size()
+    g_size = lax.axis_size("g")
+    bf16, f32 = jnp.bfloat16, jnp.float32
+    vmem = pl.BlockSpec(memory_space=pltpu.VMEM)
+    small_rows = small.shape[1]
+    return pl.pallas_call(
+        partial(return_kernel, shared),
+        in_specs=[vmem, vmem],
+        out_specs=[vmem] * 4,
+        out_shape=[
+            jax.ShapeDtypeStruct((team, step, lanes), bf16),
+            jax.ShapeDtypeStruct((rows - team * step, lanes), f32),
+            jax.ShapeDtypeStruct((small_rows, LANES), f32),
+            jax.ShapeDtypeStruct((groups, shared, LANES), f32),
+        ],
+        scratch_shapes=[
+            pltpu.VMEM((g_size, rows, lanes), bf16),
+            pltpu.VMEM((g_size - 1, rows, lanes), bf16),
+            pltpu.VMEM((g_size - 1, rows, lanes), bf16),
+            pltpu.VMEM((rows, lanes), f32),
+            pltpu.VMEM((rows, lanes), bf16),
+            pltpu.VMEM(small.shape, bf16),
+            pltpu.SemaphoreType.DMA((team + 1, g_size)),
+            pltpu.SemaphoreType.DMA((team + 1, g_size - 1)),
+            pltpu.SemaphoreType.DMA((1,)),
+            pltpu.SemaphoreType.DMA((2,)),
+            pltpu.SemaphoreType.DMA((5,)),
+        ],
+        compiler_params=pltpu.CompilerParams(
+            collective_id=4, has_side_effects=True, vmem_limit_bytes=56 * 1024 * 1024
+        ),
+        name="return_sums",
+    )(grads, small)
+
+
 def axis_sizes():
     return tuple(lax.axis_size(name) for name in EVERY)
 
@@ -778,19 +1653,6 @@
     lanes = runs.shape[-1]
     split = runs.reshape(t, 2, x * c, -1, lanes).transpose(0, 2, 1, 3, 4)
     return split.reshape(t * x * c, -1, lanes)
-
-
-def team_rows(gathered):
-    grid, team, two_rows, lanes = gathered.shape
-    split = gathered.reshape(grid, team, 2, two_rows // 2, lanes)
-    return split.transpose(2, 1, 0, 3, 4).reshape(2, -1, lanes)
-
-
-def owner_team_rows(values):
-    g, t, y, x, c = axis_sizes()
-    lanes = values.shape[2]
-    split = values.reshape(2, t * x * c, g * y, -1, lanes).transpose(2, 1, 0, 3, 4)
-    return split.reshape(g * y, t * x * c, -1, lanes)
 
 
 def team_slices(values, parts):
@@ -897,17 +1759,17 @@
     cells_all = lstm_proj.shape[1]
     cells = cells_all // team
 
-    highway_slices = team_first(highway_weight.reshape(2 * highway_rows, -1))
-    highway_swapped = swap_team(highway_slices.reshape(team, 2 * highway_rows, 2 * part))
-    first_all = lax.all_gather(
-        jnp.concatenate([highway_swapped.reshape(-1, 2 * part), proj_weight], axis=0),
-        GRID,
-        axis=0,
-        tiled=False,
-    )
-    highway_bias, proj_bias, lstm_bias, highway_swapped = lax.optimization_barrier(
-        (highway_bias, proj_bias, lstm_bias, highway_swapped)
-    )
+    conv_own = jnp.concatenate([conv_weight.reshape(-1, bank_cols), conv_bias], axis=0)
+    banks = lax.axis_size("x") * lax.axis_size("c")
+    conv_all = lax.all_to_all(
+        jnp.broadcast_to(conv_own[None], (banks,) + conv_own.shape),
+        ("x", "c"),
+        split_axis=0,
+        concat_axis=0,
+        tiled=True,
+    )
+    conv_weight_all = conv_all[:, :-1].reshape((banks,) + conv_weight.shape[1:])
+    conv_bias_all = conv_all[:, -1]
     sizes = [highway_bias.size, proj_bias.size, lstm_bias.size, resets.size]
     small = jnp.concatenate(
         [
@@ -941,59 +1803,55 @@
     lstm_bias_own = lax.dynamic_index_in_dim(lstm_bias_all, place, 2, False)
     lstm_bias_own = lstm_bias_own.reshape(2, 1, 4 * cells).astype(f32)
 
+    highway_slices = team_first(highway_weight.reshape(2 * highway_rows, -1))
+    turned_rows = lstm_proj.shape[2]
+    gate_slices = lstm_weight.reshape(2, lstm_rows, 4, team, cells).transpose(3, 0, 2, 1, 4)
+    swapped = swap_team(
+        jnp.concatenate(
+            [
+                highway_slices.reshape(team, 2 * highway_rows, 2 * part),
+                gate_slices.reshape(team, 8 * lstm_rows, cells),
+                team_slices(jnp.swapaxes(lstm_proj, 1, 2), 1),
+            ],
+            axis=1,
+        )
+    )
+    ends = [2 * highway_rows, 2 * highway_rows + 8 * lstm_rows]
+    block = jnp.concatenate([swapped[:, : ends[0]].reshape(-1, 2 * part), proj_weight], axis=0)
+    t, x, c = lax.axis_size("t"), lax.axis_size("x"), lax.axis_size("c")
+    lstm_block = (
+        swapped[:, ends[0] : ends[1]]
+        .reshape(t, x * c, 8, lstm_rows, cells)
+        .transpose(0, 2, 1, 3, 4)
+        .reshape(t * 8, x * c * lstm_rows, cells)
+    )
+    turned_block = run_rows(swapped[:, ends[1] :])
     cut_rows = team * 2 * highway_rows
-    grid = first_all.shape[0]
-    highway_own = team_rows(first_all[:, :cut_rows].reshape(-1, team, 2 * highway_rows, 2 * part))
-    project_own = first_all[:, cut_rows:].reshape(part, width)
-    lstm_weight, lstm_proj, highway_swapped = lax.optimization_barrier(
-        (lstm_weight, lstm_proj, highway_swapped)
-    )
-    turned_rows = lstm_proj.shape[2]
-    turned_slices = team_slices(jnp.swapaxes(lstm_proj, 1, 2), 1)
-    lstm_swapped = swap_team(team_slices(lstm_weight, 4))
-    turned_swapped = swap_team(turned_slices)
-    lstm_own = lax.all_gather(run_rows(lstm_swapped), GRID, axis=0, tiled=False)
-    turned_own = lax.all_gather(run_rows(turned_swapped), GRID, axis=0, tiled=False)
-
-    conv_own = jnp.concatenate([conv_weight.reshape(-1, bank_cols), conv_bias], axis=0)
-    banks = lax.axis_size("x") * lax.axis_size("c")
-    conv_all = lax.all_to_all(
-        jnp.broadcast_to(conv_own[None], (banks,) + conv_own.shape),
-        ("x", "c"),
-        split_axis=0,
-        concat_axis=0,
-        tiled=True,
-    )
-    conv_weight_all = conv_all[:, :-1].reshape((banks,) + conv_weight.shape[1:])
-    conv_bias_all = conv_all[:, -1]
+    grid = lax.axis_size("g") * lax.axis_size("y")
     bank = lax.axis_index("x") * lax.axis_size("c") + lax.axis_index("c")
     own_ids = lax.dynamic_slice_in_dim(char_ids, bank * own, own, axis=0)
     own_ids = jnp.swapaxes(own_ids, 0, 1).reshape(own * steps, char_ids.shape[2])
     filters, counts = filter_matrix(conv_weight_all, conv_bias_all)
     tight_from = wide_columns(bank_cols)
-    padded_ids, tiled, features, pooled_lse = pool_tokens(
-        own_ids, char_table, filters, counts, tight_from
-    )
+    padded_ids, tiled = embed_tokens(own_ids, char_table)
 
     tokens = own * steps
-    operands, hiddens, mixes = [], [], []
-    operand = share_team(permuted_columns(features)).reshape(team * tokens, features_all)
-    hidden = lax.dynamic_slice_in_dim(operand, place * part, part, axis=1).astype(f32)
-    for level in range(2):
-        mixed = (
-            jnp.dot(operand, highway_own[level], preferred_element_type=f32)
-            + highway_bias_own[level]
-        )
-        operands.append(operand)
-        hiddens.append(hidden)
-        mixes.append(mixed)
-        carry_gate = jax.nn.sigmoid(mixed[:, part:])
-        hidden = carry_gate * hidden + (1.0 - carry_gate) * jax.nn.silu(mixed[:, :part])
-        if level == 0:
-            operand = share_team(hidden.astype(bf16)).transpose(1, 0, 2)
-            operand = operand.reshape(team * tokens, features_all)
-    top_own = hidden.astype(bf16)
-    lin_parts = jnp.dot(top_own, project_own, preferred_element_type=f32).astype(bf16)
+    (
+        pooled_lse,
+        first_all,
+        lstm_own,
+        turned_own,
+        first,
+        second,
+        mixed,
+        hidden,
+        top_own,
+        lin_parts,
+    ) = run_highway(
+        tight_from, tiled, filters, counts, block, lstm_block, turned_block, highway_bias_own
+    )
+    lstm_own = lstm_own.reshape(grid, t, 2, 4, x * c * lstm_rows, cells)
+
     keep_forward = 1.0 - resets_team
     keep_backward = 1.0 - jnp.concatenate(
         [resets_team[:, 1:], jnp.zeros((team * own, 1), f32)], axis=1
@@ -1012,51 +1870,18 @@
     lstm_summed = lax.psum_scatter(lstm_grads, GRID, scatter_dimension=0, tiled=False)
     turned_summed = lax.all_to_all(turned_grads, GRID, split_axis=0, concat_axis=0, tiled=True)
     turned_summed = turned_summed.astype(f32).sum(axis=0).astype(bf16)
-    grad_input_team = grad_lin_all.reshape(team * tokens, width)
     grad_input = lax.dynamic_index_in_dim(grad_lin_all, place, 0, False).reshape(tokens, width)
     grad_project_b = column_sum(grad_input)
-    grad_project_w = outer_sum(top_own, grad_input_team).astype(bf16)
-    grad_hidden = transposed(grad_input_team, project_own)
-    highway_parts, highway_bias_parts = [None, None], [None, None]
-    for level in (1, 0):
-        operand, hidden_in, mixed = operands[level], hiddens[level], mixes[level]
-        carry_gate = jax.nn.sigmoid(mixed[:, part:])
-        pre_act = mixed[:, :part]
-        act_sig = jax.nn.sigmoid(pre_act)
-        grad_act = grad_hidden * (1.0 - carry_gate) * act_sig * (1.0 + pre_act * (1.0 - act_sig))
-        grad_carry = grad_hidden * (hidden_in - pre_act * act_sig) * carry_gate * (1.0 - carry_gate)
-        grad_mixed = jnp.concatenate([grad_act, grad_carry], axis=1).astype(bf16)
-        highway_parts[level] = outer_sum(operand, grad_mixed).astype(bf16)
-        highway_bias_parts[level] = column_sum(grad_mixed)
-        direct = grad_hidden * carry_gate
-        spread = transposed(grad_mixed, highway_own[level])
-        if level == 1:
-            spread = spread.astype(bf16).reshape(team * tokens, team, part).transpose(1, 0, 2)
-            grad_hidden = direct + swap_team(spread).astype(f32).sum(axis=0)
-        else:
-            held = lax.dynamic_slice_in_dim(spread, place * part, part, axis=1)
-            spread = lax.dynamic_update_slice_in_dim(spread, held + direct, place * part, axis=1)
-            spread = spread.astype(bf16).reshape(team, tokens, features_all)
-            grad_features = restored_columns(
-                swap_team(spread).astype(f32).sum(axis=0).astype(bf16)
-            )
-
-    first_parts = jnp.concatenate(
-        [
-            owner_team_rows(jnp.stack(highway_parts)).reshape(grid, cut_rows, 2 * part),
-            grad_project_w.reshape(grid, -1, width),
-        ],
-        axis=1,
-    )
-    first_parts, lstm_summed = lax.optimization_barrier((first_parts, lstm_summed))
-    first_summed = lax.psum_scatter(
-        first_parts,
-        GRID,
-        scatter_dimension=0,
-        tiled=False,
-    )
-    project_grad = first_summed[cut_rows:].astype(f32)
-
+    grad_features, first_parts, highway_bias_sums = run_highway_back(
+        grad_lin_all.reshape(team, tokens, width),
+        first_all,
+        first,
+        second,
+        mixed,
+        hidden,
+        top_own,
+    )
+    grad_features = restored_columns(grad_features)
     grad_filters, grad_table = pool_grads(
         padded_ids,
         tiled,
@@ -1071,14 +1896,7 @@
     lstm_weight_grad = whole_columns(lstm_returned, 4).astype(f32)
     turned_grad = whole_columns(swap_team(member_rows(turned_summed)), 1).astype(f32)
     lstm_proj_grad = jnp.swapaxes(turned_grad, 1, 2)
-    highway_returned = swap_team(first_summed[:cut_rows].reshape(team, 2 * highway_rows, 2 * part))
     g, t, y, x, c = axis_sizes()
-    highway_weight_grad = (
-        highway_returned.reshape(t, x, c, 2 * highway_rows, 2, g, y, -1)
-        .transpose(3, 4, 5, 0, 6, 1, 2, 7)
-        .reshape(2, highway_rows, 2 * features_all)
-        .astype(f32)
-    )
 
     def own_place(values, parts):
         lanes = values.shape[-1] // parts
@@ -1087,7 +1905,7 @@
         return lax.dynamic_update_slice(full, split, (0, 0, place, 0)).reshape(2, -1)
 
     lstm_bias_parts = own_place(bias_sums[:, 0], 4)
-    highway_bias_parts = own_place(jnp.stack(highway_bias_parts), 2)
+    highway_bias_parts = own_place(highway_bias_sums[:, 0], 2)
     highway_bias_parts = (
         highway_bias_parts.reshape(2, 2, t, x, c, g, y, -1)
         .transpose(0, 1, 5, 2, 6, 3, 4, 7)
@@ -1109,33 +1927,37 @@
         (groups, x * c, row_count(table_items), LANES),
     ).reshape(devices, -1, LANES)
     filter_blocks = bank_blocks(grad_filters, bank_cols, groups)
-    mine = lax.all_to_all(
-        jnp.concatenate(
-            [filter_blocks, table_blocks, padded_rows(biases, row_count(biases.shape[1]))], axis=1
-        ).astype(bf16),
-        EVERY,
-        split_axis=0,
-        concat_axis=0,
-        tiled=True,
-    )
-    mine = mine.astype(f32).sum(axis=0)
-    shared = filter_blocks.shape[1] + table_blocks.shape[1]
+    shared = -(-(filter_blocks.shape[1] + table_blocks.shape[1]) // 8) * 8
+    fill = shared - filter_blocks.shape[1] - table_blocks.shape[1]
+    bias_rows = -(-(shared + row_count(biases.shape[1])) // 16) * 16 - shared
+    small = jnp.concatenate(
+        [
+            filter_blocks,
+            jnp.pad(table_blocks, ((0, 0), (0, fill), (0, 0))),
+            padded_rows(biases, bias_rows),
+        ],
+        axis=1,
+    ).astype(bf16)
+    highway_returned, project_grad, mine, both = run_return(
+        first_parts, small, 2 * highway_rows, shared, groups
+    )
+    highway_weight_grad = (
+        highway_returned.reshape(t, x, c, 2 * highway_rows, 2, g, y, -1)
+        .transpose(3, 4, 5, 0, 6, 1, 2, 7)
+        .reshape(2, highway_rows, 2 * features_all)
+        .astype(f32)
+    )
+
     mine_biases = mine[shared:].reshape(-1)
     ends = [2 * lstm_bias.shape[1], 2 * lstm_bias.shape[1] + 2 * highway_bias.shape[1]]
     lstm_bias_grad = mine_biases[: ends[0]].reshape(2, -1)
     highway_bias_grad = mine_biases[ends[0] : ends[1]].reshape(2, -1)
     proj_bias_grad = mine_biases[ends[1] : ends[1] + proj_bias.size]
-    both = lax.all_to_all(
-        jnp.broadcast_to(mine[None, :shared], (groups, shared, LANES)),
-        ("g", "t", "y"),
-        split_axis=0,
-        concat_axis=0,
-        tiled=True,
-    )
     grad_kernel, grad_bias = bank_filters(
         both[:, : filter_blocks.shape[1]], bank, bank_cols, groups
     )
-    grad_table = both[:, filter_blocks.shape[1] :].reshape(groups, -1)[:, :table_items]
+    table_end = filter_blocks.shape[1] + table_blocks.shape[1]
+    grad_table = both[:, filter_blocks.shape[1] : table_end].reshape(groups, -1)[:, :table_items]
     grad_table = grad_table.reshape(-1)[: char_table.size].reshape(char_table.shape)
     return (
         grad_table,

time: 952 us -> 808 us (0.85)
  waiting for transfers between devices: 441 us -> 7.52 us
  Pallas kernels: 208 us -> 601 us
  starting transfers between devices: 88.7 us -> 33.1 us
  matrix products: 37.2 us -> 6.27 us
  other arithmetic: 35.7 us -> 20.5 us
    pallas_call x1 -> x3, Pallas kernels: 19.7 us -> 404 us  [the longest x1 182 us: run_highway(): pl.pallas_call(partial(highway_kernel, tight_from), in_specs=[vmem] * 3 +...]
    all_to_all x10 -> x3, waiting for transfers between devices: 292 us -> 1.65 us  [swap_team(): return lax.all_to_all(values, TEAM, split_axis=0, concat_axis=0, tiled=True)]
    all_to_all x2 -> x0, waiting for transfers between devices: 77.8 us -> none  [the longest x1 52.8 us: shards(): lax.all_to_all(jnp.concatenate([filter_blocks, table_blocks, padded_rows(...]
    all_gather x3 -> x0, waiting for transfers between devices: 62 us -> none  [the longest x1 36.3 us: shards(): lstm_own = lax.all_gather(run_rows(lstm_swapped), GRID, axis=0, tiled=False)]
    all_to_all x10 -> x3, starting transfers between devices: 60.8 us -> 17.5 us  [swap_team(): return lax.all_to_all(values, TEAM, split_axis=0, concat_axis=0, tiled=True)]
    dot_general x7 -> x1, matrix products: 22.8 us -> 3.27 us  [embed_tokens(): tiled = jnp.dot(selector, table_tiled, preferred_element_type=jnp.float32)]
    all_to_all x2 -> x0, starting transfers between devices: 11.7 us -> none  [the longest x1 5.96 us: shards(): lax.all_to_all(jnp.broadcast_to(mine[None, :shared], (groups, shared, LAN...]
    dot_general x5 -> x2, matrix products: 13.5 us -> 2.59 us  [outer_sum(): lax.dot_general(former, latter, (((0,), (0,)), ((), ())), preferred_eleme...]
  transfers between devices with their start and end apart: 20 -> 7, of which waited for: 13 -> 4; matrix products, arithmetic and copies ran while one was open for 17% -> 13% of each run, Pallas kernels for 5% -> 32%
where the time goes in v4:
time: 808 us; the launch traced here: 794 us
  Pallas kernels  601 us (74%)
  local copies, waits for them, and re-layouts  110 us (14%)
  starting transfers between devices  33.1 us (4%)
  other arithmetic  20.5 us (3%)
  between operations  15.2 us (2%)
    pallas_call x1, Pallas kernels, run_highway(): pl.pallas_call(partial(highway_kernel, tight_from), in_specs=[vmem] * 3 +...  182 us
    pallas_call x1, Pallas kernels, run_lstm(): pl.pallas_call(partial(lstm_kernel, team), in_specs=[vmem, vmem, vmem, hb...  169 us
    pallas_call x1, Pallas kernels, run_highway_back(): pl.pallas_call(highway_back_kernel, in_specs=[vmem, hbm] + [vmem] * 5, ou...  120 us
    pallas_call x1, Pallas kernels, run_return(): pl.pallas_call(partial(return_kernel, shared), in_specs=[vmem, vmem], out...  103 us
    pallas_call x1, Pallas kernels, pool_grads(): pl.pallas_call(partial(pool_grad_kernel, tight_from), grid=(tokens // blo...  28 us
    all_to_all x3, starting transfers between devices, swap_team(): return lax.all_to_all(values, TEAM, split_axis=0, concat_axis=0, tiled=True)  17.5 us
  transfers between devices with their start and end apart: 7, of which 4 were waited for; matrix products, arithmetic and copies ran while one was open for 13% of the time, Pallas kernels for 32%

profile of v4, /device:TPU:14, one launch (start us, length us, event | category | flops | bytes accessed | tf_op | source)
XLA Modules:
  0.0 794.3 jit_solution(9905280393669744821)
XLA Ops:
  13.0 6.0 all-to-all-start.2
  20.0 4.2 all-to-all-done.2
  25.2 4.7 all-to-all-start
  33.2 4.4 reshape_reshape.21
  37.7 4.4 copy.227
  44.7 3.0 pad_maximum_fusion
  48.6 4.5 all-to-all-start.1
  61.2 3.3 convolution_convert_fusion
  95.1 181.5 %highway_team.1 = (f32[128,2048]{1,0:T(8,128)}, bf16[4,1088,512]{2,1,0:T(8,128)(2,1)}, bf16[4,16,128,512]{3,2,1,0:T(8,128)(2,1)}, bf16[4,2,2,64,512]{4,3,2,1,0:T...) custom-call(bf16[128,64,128]{2,1,0:T(8,128)(2,1)} %bitcast.191, ...), custom_call_target="tpu_custom_call" | custom-call | tf_op jit(solution)/shard_map/highway_team/pallas_call | solution.py:1149
  276.6 168.7 %lstm_team.1 = (bf16[8,4,32,512]{3,2,1,0:T(8,128)(2,1)}, bf16[4,2,2,128,2048]{4,3,2,1,0:T(8,128)(2,1)}, bf16[4,2,2,64,512]{4,3,2,1,0:T(8,128)(2,1)}, f32[2,8,2048]{2,1,0:T(8,128)}) custom-call(bf16[8,4,32,512]{3,2,1,0:T(8,128)(2,1)} %bitcast.219, f32[1,512]{1,0:T(1,128)} %reshape.315.lin_bias_ref, bf16[2,4,32,512]{3,2,1,0:T(8,128)(2,1)} %bitcast.220, ...), custom_call_target="tpu_custom_call" | custom-call | tf_op jit(solution)/shard_map/lstm_team/pallas_call | solution.py:695
  445.3 4.9 all-to-all-start.4
  450.2 119.5 %highway_team_back.1 = (bf16[128,2048]{1,0:T(8,128)(2,1)}, bf16[4,1088,512]{2,1,0:T(8,128)(2,1)}, f32[2,8,512]{2,1,0:T(8,128)}) custom-call(bf16[8,128,512]{2,1,0:T(8,128)(2,1)} %bitcast.212, bf16[4,1088,512]{2,1,0:T(8,128)(2,1)} %get-tuple-element.46.first_hbm, bf16[8,128,2048]{2,1,0:T(8,128)(2,1)} %get-tuple-element.47.first_ref, ...), custom_call_target="tpu_custom_call" | custom-call | tf_op jit(solution)/shard_map/highway_team_back/pallas_call | solution.py:1412
  574.8 28.0 %pool_grads.1 = (f32[128,2048]{1,0:T(8,128)S(1)}, f32[128,64,128]{2,1,0:T(8,128)S(1)}) custom-call(bf16[128,64,128]{2,1,0:T(8,128)(2,1)S(1)} %bitcast.192, bf16[128,2048]{1,0:T(8,128)(2,1)S(1)} %copy-done.3, f32[8,2048]{1,0:T(8,128)S(1)} %copy-done.6, f32[128,2048]{1,0:T(8,128)S(1)} %copy-done.5, bf16[128,2048]{1,0:T(8,128)(2,1)S(1)} %copy.244.upstream_ref), custom_call_target="tpu_custom_call" | custom-call | tf_op jit(solution)/shard_map/pool_grads/pallas_call | solution.py:210
  609.4 5.2 all-to-all-start.5
  619.4 3.2 copy.261
  623.0 7.8 all-to-all-start.3
  630.9 2.7 fusion.7
  642.0 103.2 %return_sums.1 = (bf16[8,128,512]{2,1,0:T(8,128)(2,1)}, f32[64,512]{1,0:T(8,128)}, f32[160,128]{1,0:T(8,128)}, f32[8,136,128]{2,1,0:T(8,128)}) custom-call(bf16[4,1088,512]{2,1,0:T(8,128)(2,1)} %get-tuple-element.52.grads_ref, bf16[32,160,128]{2,1,0:T(8,128)(2,1)} %fusion.11.small_ref), custom_call_target="tpu_custom_call" | custom-call | tf_op jit(solution)/shard_map/return_sums/pallas_call | solution.py:1610
  747.1 2.6 copy.259
  749.7 6.7 copy.260
  756.3 6.2 reshape.319
  770.3 4.5 reshape.323
  774.8 6.6 copy.262
  781.4 5.0 reshape.320
  (206 shorter events, 88.5 us)
Async XLA Ops:
  7.2 45.9 %copy-start = (s32[128,4,50]{0,1,2:T(4,128)S(1)}, s32[128,4,50]{0,1,2:T(4,128)}, u32[]{:S(2)}) copy-start(s32[128,4,50]{0,1,2:T(4,128)} %param.18) | copy-start | bytes 307204
  7.2 22.8 %copy-start.9 = (bf16[2,32,16384]{2,1,0:T(8,128)(2,1)S(1)}, bf16[2,32,16384]{2,1,0:T(8,128)(2,1)}, u32[]{:S(2)}) copy-start(bf16[2,32,16384]{2,1,0:T(8,128)(2,1)} %param.28) | copy-start | bytes 6291460
  13.0 11.1 %all-to-all-start.2 = ((bf16[32,2,712]{2,1,0:T(2,128)(2,1)}), bf16[32,2,712]{2,1,0:T(2,128)(2,1)S(1)}, u32[]{:S(2)}, u32[]{:S(2)}) async-start(bf16[32,2,712]{2,1,0:T(2,128)(2,1)} %reshape.332), calls=%async_computation.2 | async-start | bytes 196608 | tf_op jit(solution)/shard_map/all_to_all | solution.py:1782
  24.1 1.1 copy-start.10
  25.2 22.4 %all-to-all-start = ((bf16[4,113,1024]{2,1,0:T(8,128)(2,1)}), bf16[4,113,1024]{2,1,0:T(8,128)(2,1)S(1)}, u32[]{:S(2)}, u32[]{:S(2)}) async-start(bf16[4,113,1024]{2,1,0:T(8,128)(2,1)} %broadcast_in_dim.76), calls=%async_computation | async-start | bytes 1966080 | tf_op jit(solution)/shard_map/all_to_all | solution.py:1764
  37.7 6.8 copy-start.12
  42.1 2.6 copy-start.7
  47.7 13.6 %copy-start.17 = (bf16[262,16]{0,1:T(8,128)(2,1)S(1)}, bf16[262,16]{0,1:T(8,128)(2,1)}, u32[]{:S(2)}) copy-start(bf16[262,16]{0,1:T(8,128)(2,1)} %param.21) | copy-start | bytes 25156
  48.6 42.7 %all-to-all-start.1 = ((bf16[8,416,512]{2,1,0:T(8,128)(2,1)}), bf16[8,416,512]{2,1,0:T(8,128)(2,1)S(1)}, u32[]{:S(2)}, u32[]{:S(2)}) async-start(bf16[8,416,512]{2,1,0:T(8,128)(2,1)} %pad_maximum_fusion), calls=%async_computation.1 | async-start | bytes 6815744 | tf_op jit(solution)/shard_map/all_to_all | solution.py:269
  53.1 566.3 %reduce-scatter.2.cloned.1.call-start = ((), (), s32[]{:S(2)}) async-start(), calls=%async_computation.7 | async-start | bytes 10485760 | tf_op jit(solution)/shard_map/reduce_scatter | solution.py:1870
  56.4 8.1 %copy-start.15 = (s32[8192]{0:T(1024)}, s32[8192]{0:T(1024)S(1)}, u32[]{:S(2)}) copy-start(s32[8192]{0:T(1024)S(1)} %eq.71) | copy-start | bytes 98308
  61.2 3.3 copy-start.11
  445.3 4.9 copy-start.18
  445.3 161.9 %all-to-all-start.4 = ((bf16[4,2,2,64,512]{4,3,2,1,0:T(8,128)(2,1)}), bf16[4,2,2,64,512]{4,3,2,1,0:T(8,128)(2,1)}, u32[]{:S(2)}, u32[]{:S(2)}) async-start(bf16[4,2,2,64,512]{4,3,2,1,0:T(8,128)(2,1)} %get-tuple-element.64), calls=%async_computation.5 | async-start | bytes 2097152 | tf_op jit(solution)/shard_map/all_to_all | solution.py:1871
  569.8 3.6 copy-start.2
  569.8 3.6 copy-start.3
  569.8 3.6 copy-start.6
  573.4 1.4 copy-start.5
  602.8 2.0 copy-start.4
  609.4 13.6 %all-to-all-start.5 = ((bf16[8,32,512]{2,1,0:T(8,128)(2,1)}), bf16[8,32,512]{2,1,0:T(8,128)(2,1)S(1)}, u32[]{:S(2)}, u32[]{:S(2)}) async-start(bf16[8,32,512]{2,1,0:T(8,128)(2,1)} %bitcast.91), calls=%async_computation.6 | async-start | bytes 524288 | tf_op jit(solution)/shard_map/all_to_all | solution.py:269
  623.0 147.3 %all-to-all-start.3 = ((bf16[8,64,2048]{2,1,0:T(8,128)(2,1)}), bf16[8,64,2048]{2,1,0:T(8,128)(2,1)S(1)}, u32[]{:S(2)}, u32[]{:S(2)}) async-start(bf16[8,64,2048]{2,1,0:T(8,128)(2,1)} %bitcast.197), calls=%async_computation.4 | async-start | bytes 4194304 | tf_op jit(solution)/shard_map/all_to_all | solution.py:269
  630.9 2.7 copy-start.16
  774.8 12.2 %copy-start.1 = (s32[128,4,50]{0,1,2:T(4,128)S(1)}, s32[128,4,50]{0,1,2:T(4,128)}, u32[]{:S(2)}) copy-start(s32[128,4,50]{0,1,2:T(4,128)} %param.18) | copy-start | bytes 307204
  781.4 5.0 copy-start.13
  (2 other events, 1.8 us)
Sparse Core Ops, SparseCore 0:
  445.5 173.8 reduce-scatter.1

commit v5 on v4

--- a/solution.py
+++ b/solution.py
@@ -9,6 +9,7 @@
 from jax.sharding import Mesh, PartitionSpec as P
 
 CHAR_COUNT = 50
+VOCAB = 262
 EMBED = 16
 WIDEST = 7
 TAPS = WIDEST * EMBED
@@ -17,6 +18,7 @@
 TIGHT = 48
 CHUNK = 256
 TOKEN_BLOCK = 16
+AHEAD = 6
 
 
 def bank_plan(bank_cols):
@@ -106,26 +108,22 @@
         features_ref[:, cols] = (pooled_pre * jax.nn.sigmoid(pooled_pre)).astype(jnp.bfloat16)
 
 
-def pool_grad_kernel(
+def pool_grad_block(
     tight_from,
     tiled_ref,
+    ids_row,
     weight_ref,
     count_ref,
     lse_ref,
     upstream_ref,
     grad_weight_ref,
-    aligned_ref,
+    table_ref,
     wide,
     tight,
     spread,
 ):
     tokens, places, lanes = tiled_ref.shape
     block_windows(tiled_ref, wide, tight)
-
-    @pl.when(pl.program_id(0) == 0)
-    def _():
-        grad_weight_ref[...] = jnp.zeros_like(grad_weight_ref)
-
     spread[...] = jnp.zeros_like(spread)
     wide_turned = wide[...].T
     tight_turned = tight[...].T
@@ -159,7 +157,15 @@
     aligned = jnp.where(lane < EMBED, flat, 0.0)
     for offset in range(1, WIDEST):
         aligned = jnp.where(lane // EMBED == offset, shift_rows(flat, offset), aligned)
-    aligned_ref[...] = aligned.reshape(tokens, places, lanes)
+    high = aligned.astype(jnp.bfloat16)
+    low = (aligned - high.astype(jnp.float32)).astype(jnp.bfloat16)
+    vocab = table_ref.shape[0]
+    selector = jnp.where(
+        lax.broadcasted_iota(jnp.int32, (vocab, rows), 0) == ids_row, 1.0, 0.0
+    ).astype(jnp.bfloat16)
+    table_ref[...] += jnp.dot(selector, high, preferred_element_type=jnp.float32) + jnp.dot(
+        selector, low, preferred_element_type=jnp.float32
+    )
 
 
 def filter_matrix(conv_weight, conv_bias):
@@ -203,45 +209,6 @@
     return (padded, tiled)
 
 
-def pool_grads(padded, tiled, weights, counts, pooled_lse, upstream, vocab_size, tight_from):
-    tokens = tiled.shape[0]
-    block = math.gcd(tokens, TOKEN_BLOCK)
-    total = weights.shape[1]
-    grad_weight, aligned = pl.pallas_call(
-        partial(pool_grad_kernel, tight_from),
-        grid=(tokens // block,),
-        in_specs=[
-            pl.BlockSpec((block, PLACES, LANES), lambda i: (i, 0, 0)),
-            pl.BlockSpec((LANES, total), lambda i: (0, 0)),
-            pl.BlockSpec((8, total), lambda i: (0, 0)),
-            pl.BlockSpec((block, total), lambda i: (i, 0)),
-            pl.BlockSpec((block, total), lambda i: (i, 0)),
-        ],
-        out_specs=[
-            pl.BlockSpec((LANES, total), lambda i: (0, 0)),
-            pl.BlockSpec((block, PLACES, LANES), lambda i: (i, 0, 0)),
-        ],
-        out_shape=[
-            jax.ShapeDtypeStruct((LANES, total), jnp.float32),
-            jax.ShapeDtypeStruct((tokens, PLACES, LANES), jnp.float32),
-        ],
-        scratch_shapes=[
-            pltpu.VMEM((block * PLACES, LANES), jnp.bfloat16),
-            pltpu.VMEM((block * TIGHT, LANES), jnp.bfloat16),
-            pltpu.VMEM((block, PLACES, LANES), jnp.float32),
-        ],
-        compiler_params=pltpu.CompilerParams(vmem_limit_bytes=40 * 1024 * 1024),
-        name="pool_grads",
-    )(tiled, weights, counts, pooled_lse, upstream)
-    aligned = aligned.reshape(tokens * PLACES, LANES)
-    selector = char_selector(padded, vocab_size).astype(jnp.bfloat16)
-    high = aligned.astype(jnp.bfloat16)
-    low = (aligned - high.astype(jnp.float32)).astype(jnp.bfloat16)
-    by_tap = outer_sum(selector, high) + outer_sum(selector, low)
-    grad_table = by_tap[:, :TAPS].reshape(vocab_size, WIDEST, EMBED).sum(axis=1)
-    return (grad_weight, grad_table)
-
-
 TEAM = ("t", "x", "c")
 GRID = ("g", "y")
 EVERY = ("g", "t", "y", "x", "c")
@@ -284,8 +251,7 @@
 
 def lstm_kernel(
     team,
-    parts_ref,
-    lin_bias_ref,
+    lin_ref,
     out_grad_ref,
     weight_hbm,
     turned_hbm,
@@ -323,7 +289,7 @@
     share_sems,
     out_sems,
 ):
-    _, steps, own, width = parts_ref.shape
+    _, steps, own, width = lin_ref.shape
     group = team * own
     cells = proj_ref.shape[2]
     row_block = 32
@@ -375,29 +341,16 @@
             device_id_type=pl.DeviceIdType.MESH,
         ).start()
 
-    for peer in peers:
-        send(parts_ref.at[peer], stage_lin.at[place], lin_sems.at[0], lin_sems.at[1], peer)
-    stage_lin[place] = parts_ref[place]
+    for t in range(steps):
+        lin_all_ref[t] = lin_ref[:, t].reshape(group, width)
     for d in range(2):
         first = 0 if d == 0 else last
         state_ref[d, first] = jnp.zeros((group, width), jnp.bfloat16)
         cell_start[d, first] = jnp.zeros((group, cells), jnp.float32)
         grad_cell[d] = jnp.zeros((group, cells), jnp.float32)
     grad_lin_sum[...] = jnp.zeros_like(grad_lin_sum)
-    wait_bytes(stage_lin.at[others], lin_sems.at[1])
-    lin_own = jnp.sum(stage_lin[...].astype(jnp.float32), axis=0) + lin_bias_ref[...]
-    lin_all_ref[:, own_rows] = lin_own.astype(jnp.bfloat16)
-    for peer in peers:
-        send(
-            lin_all_ref.at[:, own_rows],
-            lin_all_ref.at[:, own_rows],
-            lin_sems.at[2],
-            lin_sems.at[3],
-            peer,
-        )
     wait_bytes(weight_ref, load_sems.at[0])
     wait_bytes(proj_ref, load_sems.at[1])
-    wait_bytes(lin_all_ref.at[:, other_rows], lin_sems.at[3])
 
     @pl.loop(0, steps)
     def _(t):
@@ -601,8 +554,6 @@
                 preferred_element_type=jnp.float32,
             )
 
-    wait_bytes(parts_ref.at[others], lin_sems.at[0])
-    wait_bytes(lin_all_ref.at[:, other_rows], lin_sems.at[2])
     for t in range(steps):
         stage_lin[:, t] = grad_lin_sum[t].astype(jnp.bfloat16).reshape(team, own, width)
     received_lin[place] = stage_lin[place]
@@ -685,8 +636,8 @@
         wait_bytes(turned_stage.at[d], out_sems.at[2 + d])
 
 
-def run_lstm(parts, lin_bias, out_grad, weights, turned, bias, keep):
-    team, steps, own, width = parts.shape
+def run_lstm(lin, out_grad, weights, turned, bias, keep):
+    team, steps, own, width = lin.shape
     group = team * own
     cells = turned.shape[4]
     bf16, f32 = jnp.bfloat16, jnp.float32
@@ -694,10 +645,10 @@
     hbm = pl.BlockSpec(memory_space=pl.ANY)
     return pl.pallas_call(
         partial(lstm_kernel, team),
-        in_specs=[vmem, vmem, vmem, hbm, hbm, vmem, vmem],
+        in_specs=[vmem, vmem, hbm, hbm, vmem, vmem],
         out_specs=[vmem, hbm, hbm, vmem],
         out_shape=[
-            jax.ShapeDtypeStruct(parts.shape, bf16),
+            jax.ShapeDtypeStruct(lin.shape, bf16),
             jax.ShapeDtypeStruct(weights.shape[:3] + (weights.shape[4], 4 * cells), bf16),
             jax.ShapeDtypeStruct(turned.shape, bf16),
             jax.ShapeDtypeStruct((2, 8, 4 * cells), f32),
@@ -735,7 +686,7 @@
             collective_id=1, has_side_effects=True, vmem_limit_bytes=63 * 1024 * 1024
         ),
         name="lstm_team",
-    )(parts, lin_bias, out_grad, weights, turned, bias, keep)
+    )(lin, out_grad, weights, turned, bias, keep)
 
 
 def member_at(offset):
@@ -890,6 +841,7 @@
     lstm_block_hbm,
     turned_block_hbm,
     bias_ref,
+    lin_bias_ref,
     lse_ref,
     first_hbm,
     lstm_hbm,
@@ -899,7 +851,9 @@
     mixed_ref,
     hidden_ref,
     top_ref,
-    parts_ref,
+    lin_ref,
+    parts,
+    parts_recv,
     features_own,
     wide,
     tight,
@@ -913,6 +867,7 @@
     block_sems,
     turned_sems,
     lstm_sems,
+    lin_sems,
 ):
     team, tokens, features = first_ref.shape
     part = features // team
@@ -1010,13 +965,13 @@
         def _():
             lstm_forward(jnp.minimum(chunk, chunks - 1))
 
-            @pl.when(chunk + 2 < chunks)
+            @pl.when(chunk + AHEAD < chunks)
             def _():
-                lstm_start(jnp.minimum(chunk + 2, chunks - 1))
+                lstm_start(jnp.minimum(chunk + AHEAD, chunks - 1))
 
     turned_gather.start([0])
-    lstm_start(0)
-    lstm_start(1)
+    for chunk in range(AHEAD):
+        lstm_start(chunk)
     for offset in near:
         member = member_at(offset)
         wait_bytes(first_ref.at[member], first_sems.at[offset])
@@ -1077,6 +1032,7 @@
                 second_sems.at[member, opposite(to)],
                 member_at(to),
             )
+
         pump(offset)
 
     @pl.loop(0, team + 1)
@@ -1104,15 +1060,43 @@
             gate, act = mix(1, member, second_ref[member])
             top = (gate * hidden_ref[member] + (1.0 - gate) * act).astype(jnp.bfloat16)
             top_ref[member] = top
-            parts_ref[member] = jnp.dot(
+            parts[member] = jnp.dot(
                 top, project[...], preferred_element_type=jnp.float32
             ).astype(jnp.bfloat16)
 
+            @pl.when(step > 1)
+            def _():
+                send_block(
+                    parts.at[member],
+                    parts_recv.at[place],
+                    lin_sems.at[0],
+                    lin_sems.at[1],
+                    member,
+                )
+
         pump(team + step)
+
+    parts_recv[place] = parts[place]
+    others = pl.ds(0, team - 1)
+    wait_bytes(parts_recv.at[others], lin_sems.at[1])
+    lin = jnp.sum(parts_recv[...].astype(jnp.float32), axis=0) + lin_bias_ref[...]
+    lin_ref[place] = lin.astype(jnp.bfloat16)
+    for offset in range(1, team):
+        send_block(
+            lin_ref.at[place],
+            lin_ref.at[place],
+            lin_sems.at[2],
+            lin_sems.at[3],
+            member_at(offset),
+        )
 
     @pl.loop(2 * team + 1, max(chunks, 2 * team + 1))
     def _(chunk):
         pump(chunk)
+
+    wait_bytes(lin_ref.at[others], lin_sems.at[3])
+    wait_bytes(lin_ref.at[others], lin_sems.at[2])
+    wait_bytes(parts.at[others], lin_sems.at[0])
 
     turned_gather.forward([0])
     turned_gather.finish([0])
@@ -1134,7 +1118,9 @@
     wait_bytes(lstm_block_hbm, load_sems.at[4])
 
 
-def run_highway(tight_from, tiled, filters, counts, block, lstm_block, turned_block, bias):
+def run_highway(
+    tight_from, tiled, filters, counts, block, lstm_block, turned_block, bias, lin_bias
+):
     team = team_size()
     tokens, features = tiled.shape[0], filters.shape[1]
     part = features // team
@@ -1148,7 +1134,7 @@
     token_block = math.gcd(tokens, TOKEN_BLOCK)
     return pl.pallas_call(
         partial(highway_kernel, tight_from),
-        in_specs=[vmem] * 3 + [hbm] * 3 + [vmem],
+        in_specs=[vmem] * 3 + [hbm] * 3 + [vmem] * 2,
         out_specs=[vmem] + [hbm] * 3 + [vmem] * 6,
         out_shape=[
             jax.ShapeDtypeStruct((tokens, features), f32),
@@ -1163,6 +1149,8 @@
             jax.ShapeDtypeStruct((team, tokens, width), bf16),
         ],
         scratch_shapes=[
+            pltpu.VMEM((team, tokens, width), bf16),
+            pltpu.VMEM((team, tokens, width), bf16),
             pltpu.VMEM((tokens, features), bf16),
             pltpu.VMEM((token_block * PLACES, LANES), bf16),
             pltpu.VMEM((token_block * TIGHT, LANES), bf16),
@@ -1176,12 +1164,13 @@
             pltpu.SemaphoreType.DMA((pieces, g_size, y_size)),
             pltpu.SemaphoreType.DMA((1, g_size, y_size)),
             pltpu.SemaphoreType.DMA((lstm_block.shape[0], g_size, y_size)),
+            pltpu.SemaphoreType.DMA((4,)),
         ],
         compiler_params=pltpu.CompilerParams(
             collective_id=2, has_side_effects=True, vmem_limit_bytes=60 * 1024 * 1024
         ),
         name="highway_team",
-    )(tiled, filters, counts, block, lstm_block, turned_block, bias)
+    )(tiled, filters, counts, block, lstm_block, turned_block, bias, lin_bias)
 
 
 def highway_back_kernel(
@@ -1468,20 +1457,39 @@
     return place
 
 
-def return_kernel(
-    shared,
+def final_kernel(
+    tight_from,
+    bank_counts,
     grads_ref,
-    small_ref,
-    team_ref,
+    tiled_ref,
+    ids_ref,
+    filter_ref,
+    count_ref,
+    lse_ref,
+    upstream_ref,
+    bias_ref,
+    highway_ref,
     project_ref,
     sums_ref,
-    shared_ref,
+    conv_ref,
+    table_ref,
+    natural,
+    grad_filters,
+    table_sum,
+    wide,
+    tight,
+    spread,
     y_recv,
     g_send,
     g_recv,
     kept,
     team_send,
-    small_recv,
+    team_recv,
+    bias_recv,
+    small,
+    small_team,
+    small_send,
+    small_grid,
     y_sems,
     g_sems,
     team_sems,
@@ -1490,14 +1498,16 @@
 ):
     grid, rows, lanes = grads_ref.shape
     team = team_size()
-    g_size, y_size = lax.axis_size("g"), lax.axis_size("y")
-    devices = small_ref.shape[0]
-    groups = shared_ref.shape[0]
-    cut = team_ref.shape[1] * team
-    step = team_ref.shape[1]
+    g, t, y, x, c = axis_sizes()
+    devices = bias_ref.shape[0]
+    step = team_recv.shape[1]
+    cut = step * team
+    table_rows = table_ref.shape[0] // team
     f32, bf16 = jnp.float32, jnp.bfloat16
     here = every_place({name: lax.axis_index(name) for name in EVERY})
     place = team_place()
+    bank = lax.rem(place, x * c)
+    conv_ref[...] = jnp.zeros_like(conv_ref)
     barrier = pltpu.get_barrier_semaphore()
 
     @pl.loop(1, devices)
@@ -1509,12 +1519,11 @@
     pl.semaphore_wait(barrier, devices - 1)
     pieces = [pl.ds(k * step, step) for k in range(team)] + [pl.ds(cut, rows - cut)]
     g_index, y_index = lax.axis_index("g"), lax.axis_index("y")
-    other_y = lax.rem(y_index + 1, y_size)
+    other_y = lax.rem(y_index + 1, y)
     for k, piece in enumerate(pieces):
-        for dg in list(range(1, g_size)) + [0]:
-            g = lax.rem(g_index + dg, g_size)
+        for dg in list(range(1, g)) + [0]:
             send_grid(
-                grads_ref.at[g * y_size + other_y, piece],
+                grads_ref.at[lax.rem(g_index + dg, g) * y + other_y, piece],
                 y_recv.at[dg, piece],
                 send_sems.at[0],
                 y_sems.at[k, dg],
@@ -1526,54 +1535,184 @@
     def _(shift):
         coords = every_coords(shift)
         pltpu.make_async_remote_copy(
-            src_ref=small_ref.at[every_place(coords)],
-            dst_ref=small_recv.at[here],
+            src_ref=bias_ref.at[every_place(coords)],
+            dst_ref=bias_recv.at[here],
             send_sem=send_sems.at[3],
             recv_sem=small_sems.at[0],
             device_id=coords,
             device_id_type=pl.DeviceIdType.MESH,
         ).start()
 
-    small_recv[here] = small_ref[here]
-    for k, piece in enumerate(pieces):
-        for dg in list(range(1, g_size)) + [0]:
-            g = lax.rem(g_index + dg, g_size)
+    bias_recv[here] = bias_ref[here]
+    run = upstream_ref.shape[1] // devices
+    order = [
+        (((ti * x + xi) * c + ci) * g + gi) * y + yi
+        for gi in range(g)
+        for ti in range(t)
+        for yi in range(y)
+        for xi in range(x)
+        for ci in range(c)
+    ]
+    permuted = upstream_ref[...]
+    natural[...] = jnp.concatenate([permuted[:, at * run : (at + 1) * run] for at in order], axis=1)
+    grad_filters[...] = jnp.zeros_like(grad_filters)
+    table_sum[...] = jnp.zeros_like(table_sum)
+
+    def pass_on(k):
+        piece = pieces[k]
+        for dg in list(range(1, g)) + [0]:
             wait_bytes(y_recv.at[dg, piece], y_sems.at[k, dg])
-            both = grads_ref[g * y_size + y_index, piece].astype(f32) + y_recv[dg, piece].astype(f32)
+            both = grads_ref[lax.rem(g_index + dg, g) * y + y_index, piece].astype(f32)
+            both = both + y_recv[dg, piece].astype(f32)
             if dg == 0:
                 kept[piece] = both
             else:
                 g_send[dg - 1, piece] = both.astype(bf16)
                 send_grid(
                     g_send.at[dg - 1, piece],
-                    g_recv.at[g_size - dg - 1, piece],
+                    g_recv.at[g - dg - 1, piece],
                     send_sems.at[1],
-                    g_sems.at[k, g_size - dg - 1],
+                    g_sems.at[k, g - dg - 1],
                     dg,
                     0,
                 )
 
-    wait_bytes(small_recv.at[pl.ds(0, devices - 1)], small_sems.at[0])
-    sums_ref[...] = jnp.sum(small_recv[...].astype(f32), axis=0)
-    group = (g_index * lax.axis_size("t") + lax.axis_index("t")) * y_size + y_index
-    banks = devices // groups
-
-    @pl.loop(1, groups)
-    def _(shift):
-        coords = every_coords(shift * banks)
-        pltpu.make_async_remote_copy(
-            src_ref=sums_ref.at[pl.ds(0, shared)],
-            dst_ref=shared_ref.at[group],
-            send_sem=send_sems.at[4],
-            recv_sem=small_sems.at[1],
-            device_id=coords,
-            device_id_type=pl.DeviceIdType.MESH,
-        ).start()
-
-    shared_ref[group] = sums_ref[pl.ds(0, shared)]
+    token_block = spread.shape[0]
+    blocks = tiled_ref.shape[0] // token_block
+    early = min(4, team)
+
+    def pool_block(at):
+        picked = pl.ds(pl.multiple_of(at * token_block, token_block), token_block)
+        pool_grad_block(
+            tight_from,
+            tiled_ref.at[picked],
+            ids_ref[pl.ds(at, 1)],
+            filter_ref,
+            count_ref,
+            lse_ref.at[picked],
+            natural.at[picked],
+            grad_filters,
+            table_sum,
+            wide,
+            tight,
+            spread,
+        )
+
+    for k in range(early):
+
+        @pl.loop(blocks * k // early, blocks * (k + 1) // early)
+        def _(at):
+            pool_block(at)
+
+        pass_on(k)
+
+    lane = lax.broadcasted_iota(jnp.int32, (LANES, LANES), 0)
+    fold = jnp.where(
+        (lane < TAPS)
+        & (lax.rem(lane, EMBED) == lax.broadcasted_iota(jnp.int32, (LANES, LANES), 1)),
+        1.0,
+        0.0,
+    ).astype(bf16)
+    by_tap = table_sum[...]
+    high = by_tap.astype(bf16)
+    low = (by_tap - high.astype(f32)).astype(bf16)
+    table = jnp.dot(high, fold, preferred_element_type=f32)
+    table = (table + jnp.dot(low, fold, preferred_element_type=f32)).astype(bf16)
+    starts, halves, at, column = [], [], 0, 0
+    for half in range(t):
+        for b, count in enumerate(bank_counts):
+            starts.append(at)
+            halves.append(count // t)
+            at += count // t + table_rows
+    for b, count in enumerate(bank_counts):
+        for half in range(t):
+            member = half * len(bank_counts) + b
+            each = count // t
+            turned = grad_filters[:, pl.ds(column, each)].T.astype(bf16)
+            small[pl.ds(starts[member], each)] = turned
+            column += each
+    vocab = table_sum.shape[0]
+    for member in range(team):
+        top = min(table_rows, vocab - member * table_rows)
+        begin = starts[member] + halves[member]
+        if top > 0:
+            small[pl.ds(begin, top)] = table[member * table_rows : member * table_rows + top]
+        if top < table_rows:
+            low_row = max(top, 0)
+            small[pl.ds(begin + low_row, table_rows - low_row)] = jnp.zeros(
+                (table_rows - low_row, LANES), bf16
+            )
+    for member in range(team):
+        size = halves[member] + table_rows
+        source = small.at[pl.ds(starts[member], size)]
+
+        @pl.when(place == member)
+        def _():
+            small_team[member, pl.ds(0, size)] = small[pl.ds(starts[member], size)]
+
+        @pl.when(place != member)
+        def _():
+            send_block(
+                source,
+                small_team.at[place, pl.ds(0, size)],
+                send_sems.at[4],
+                small_sems.at[1],
+                member,
+            )
+
+    for k in range(early, team - 2):
+        pass_on(k)
+    home = grid_block(0, 0)
+    for b, count in enumerate(bank_counts):
+        size = count // t + table_rows
+
+        @pl.when(bank == b)
+        def _():
+            wait_bytes(small_team.at[pl.ds(0, team - 1), pl.ds(0, size)], small_sems.at[1])
+            total = small_team[0, pl.ds(0, size)].astype(f32)
+            for origin in range(1, team):
+                total = total + small_team[origin, pl.ds(0, size)].astype(f32)
+            small_send[pl.ds(0, size)] = total.astype(bf16)
+            small_grid[home, pl.ds(0, size)] = total.astype(bf16)
+            for dg in range(g):
+                for dy in range(y):
+                    if dg or dy:
+                        send_grid(
+                            small_send.at[pl.ds(0, size)],
+                            small_grid.at[home, pl.ds(0, size)],
+                            send_sems.at[5],
+                            small_sems.at[2],
+                            dg,
+                            dy,
+                        )
+
+    for k in range(team - 2, team + 1):
+        pass_on(k)
+    t_index = lax.axis_index("t")
+    for b, count in enumerate(bank_counts):
+        each = count // t
+        size = each + table_rows
+
+        @pl.when(bank == b)
+        def _():
+            wait_bytes(small_grid.at[pl.ds(0, grid - 1), pl.ds(0, size)], small_sems.at[2])
+            total = small_grid[0, pl.ds(0, size)].astype(f32)
+            for origin in range(1, grid):
+                total = total + small_grid[origin, pl.ds(0, size)].astype(f32)
+            mine = conv_ref.at[pl.ds(pl.multiple_of(t_index * each, each), each)]
+            mine[...] = total[:each]
+            for dt in range(1, t):
+                send_block(
+                    mine, mine, send_sems.at[6], small_sems.at[3], member_at(dt * x * c)
+                )
+            piece = table_ref.at[pl.ds(pl.multiple_of(place * table_rows, 16), table_rows)]
+            piece[...] = total[each:]
+            for offset in range(1, team):
+                send_block(piece, piece, send_sems.at[7], small_sems.at[4], member_at(offset))
+
     for k, piece in enumerate(pieces):
         total = kept[piece]
-        for dg in range(1, g_size):
+        for dg in range(1, g):
             wait_bytes(g_recv.at[dg - 1, piece], g_sems.at[k, dg - 1])
             total = total + g_recv[dg - 1, piece].astype(f32)
         if k == team:
@@ -1583,58 +1722,134 @@
 
             @pl.when(place == k)
             def _():
-                team_ref[k] = team_send[piece]
+                team_recv[k] = team_send[piece]
 
             @pl.when(place != k)
             def _():
                 send_block(
-                    team_send.at[piece], team_ref.at[place], send_sems.at[2], team_sems.at[0], k
+                    team_send.at[piece], team_recv.at[place], send_sems.at[2], team_sems.at[0], k
                 )
 
-    wait_bytes(team_ref.at[pl.ds(0, team - 1)], team_sems.at[0])
-    wait_bytes(shared_ref.at[pl.ds(0, groups - 1)], small_sems.at[1])
+    wait_bytes(bias_recv.at[pl.ds(0, devices - 1)], small_sems.at[0])
+    sums_ref[...] = jnp.sum(bias_recv[...].astype(f32), axis=0)
+    wait_bytes(team_recv.at[pl.ds(0, team - 1)], team_sems.at[0])
+    half_lanes = lanes // 2
+    for half in range(2):
+        parts = [
+            team_recv[
+                (ti * x + xi) * c + ci,
+                :,
+                half * half_lanes + (gi * y + yi) * run : half * half_lanes + (gi * y + yi + 1) * run,
+            ]
+            for gi in range(g)
+            for ti in range(t)
+            for yi in range(y)
+            for xi in range(x)
+            for ci in range(c)
+        ]
+        wide_half = half_lanes * team
+        highway_ref[:, pl.ds(half * wide_half, wide_half)] = jnp.concatenate(parts, axis=1).astype(
+            f32
+        )
+    for b, count in enumerate(bank_counts):
+        each = count // t
+        size = each + table_rows
+
+        @pl.when(bank == b)
+        def _():
+            for _ in range(t - 1):
+                wait_bytes(conv_ref.at[pl.ds(0, each)], small_sems.at[3])
+                wait_bytes(conv_ref.at[pl.ds(0, each)], send_sems.at[6])
+            wait_bytes(small_grid.at[pl.ds(0, grid - 1), pl.ds(0, size)], send_sems.at[5])
+
+    wait_bytes(table_ref.at[pl.ds(0, (team - 1) * table_rows)], small_sems.at[4])
+    wait_bytes(table_ref.at[pl.ds(0, (team - 1) * table_rows)], send_sems.at[7])
     wait_bytes(y_recv, send_sems.at[0])
     wait_bytes(g_recv, send_sems.at[1])
-    wait_bytes(team_ref.at[pl.ds(0, team - 1)], send_sems.at[2])
-    wait_bytes(small_recv.at[pl.ds(0, devices - 1)], send_sems.at[3])
-    wait_bytes(shared_ref.at[pl.ds(0, groups - 1)], send_sems.at[4])
-
-
-def run_return(grads, small, step, shared, groups):
+    wait_bytes(team_recv.at[pl.ds(0, team - 1)], send_sems.at[2])
+    wait_bytes(bias_recv.at[pl.ds(0, devices - 1)], send_sems.at[3])
+    for member in range(team):
+
+        @pl.when(place != member)
+        def _():
+            size = halves[member] + table_rows
+            wait_bytes(small.at[pl.ds(starts[member], size)], send_sems.at[4])
+
+
+def run_final(tight_from, bank_counts, grads, tiled, ids, filters, counts, lse, upstream, biases, step):
     grid, rows, lanes = grads.shape
     team = team_size()
-    g_size = lax.axis_size("g")
+    g, t, y, x, c = axis_sizes()
+    tokens, features = upstream.shape
+    devices, bias_rows, _ = biases.shape
     bf16, f32 = jnp.bfloat16, jnp.float32
     vmem = pl.BlockSpec(memory_space=pltpu.VMEM)
-    small_rows = small.shape[1]
+    token_block = math.gcd(tokens, TOKEN_BLOCK)
+    vocab = -(-VOCAB // 16) * 16
+    table_rows = -(-vocab // (16 * team)) * 16
+    most = max(bank_counts) // t + table_rows
     return pl.pallas_call(
-        partial(return_kernel, shared),
-        in_specs=[vmem, vmem],
-        out_specs=[vmem] * 4,
+        partial(final_kernel, tight_from, bank_counts),
+        in_specs=[vmem] * 8,
+        out_specs=[vmem] * 5,
         out_shape=[
-            jax.ShapeDtypeStruct((team, step, lanes), bf16),
+            jax.ShapeDtypeStruct((step, lanes * team), f32),
             jax.ShapeDtypeStruct((rows - team * step, lanes), f32),
-            jax.ShapeDtypeStruct((small_rows, LANES), f32),
-            jax.ShapeDtypeStruct((groups, shared, LANES), f32),
+            jax.ShapeDtypeStruct((bias_rows, LANES), f32),
+            jax.ShapeDtypeStruct((max(bank_counts), LANES), f32),
+            jax.ShapeDtypeStruct((team * table_rows, LANES), f32),
         ],
         scratch_shapes=[
-            pltpu.VMEM((g_size, rows, lanes), bf16),
-            pltpu.VMEM((g_size - 1, rows, lanes), bf16),
-            pltpu.VMEM((g_size - 1, rows, lanes), bf16),
+            pltpu.VMEM((tokens, features), bf16),
+            pltpu.VMEM((LANES, features), f32),
+            pltpu.VMEM((vocab, LANES), f32),
+            pltpu.VMEM((token_block * PLACES, LANES), bf16),
+            pltpu.VMEM((token_block * TIGHT, LANES), bf16),
+            pltpu.VMEM((token_block, PLACES, LANES), f32),
+            pltpu.VMEM((g, rows, lanes), bf16),
+            pltpu.VMEM((g - 1, rows, lanes), bf16),
+            pltpu.VMEM((g - 1, rows, lanes), bf16),
             pltpu.VMEM((rows, lanes), f32),
             pltpu.VMEM((rows, lanes), bf16),
-            pltpu.VMEM(small.shape, bf16),
-            pltpu.SemaphoreType.DMA((team + 1, g_size)),
-            pltpu.SemaphoreType.DMA((team + 1, g_size - 1)),
+            pltpu.VMEM((team, step, lanes), bf16),
+            pltpu.VMEM(biases.shape, bf16),
+            pltpu.VMEM((sum(bank_counts) + team * table_rows, LANES), bf16),
+            pltpu.VMEM((team, most, LANES), bf16),
+            pltpu.VMEM((most, LANES), bf16),
+            pltpu.VMEM((grid, most, LANES), bf16),
+            pltpu.SemaphoreType.DMA((team + 1, g)),
+            pltpu.SemaphoreType.DMA((team + 1, g - 1)),
             pltpu.SemaphoreType.DMA((1,)),
-            pltpu.SemaphoreType.DMA((2,)),
             pltpu.SemaphoreType.DMA((5,)),
+            pltpu.SemaphoreType.DMA((8,)),
         ],
         compiler_params=pltpu.CompilerParams(
-            collective_id=4, has_side_effects=True, vmem_limit_bytes=56 * 1024 * 1024
+            collective_id=4, has_side_effects=True, vmem_limit_bytes=60 * 1024 * 1024
         ),
-        name="return_sums",
-    )(grads, small)
+        name="final_sums",
+    )(grads, tiled, ids, filters, counts, lse, upstream, biases)
+
+
+def pack_kernel(parts, received_ref, out_ref):
+    team, rows, lanes = received_ref.shape
+    each = lanes // parts
+    for member in range(team):
+        for part in range(parts):
+            out_ref[:, pl.ds((part * team + member) * each, each)] = received_ref[
+                member, :, pl.ds(part * each, each)
+            ].astype(jnp.float32)
+
+
+def pack_columns(received, parts):
+    team, rows, lanes = received.shape
+    return pl.pallas_call(
+        partial(pack_kernel, parts),
+        in_specs=[pl.BlockSpec(memory_space=pltpu.VMEM)],
+        out_specs=pl.BlockSpec(memory_space=pltpu.VMEM),
+        out_shape=jax.ShapeDtypeStruct((rows, team * lanes), jnp.float32),
+        compiler_params=pltpu.CompilerParams(vmem_limit_bytes=40 * 1024 * 1024),
+        name="pack_columns",
+    )(received)
 
 
 def axis_sizes():
@@ -1698,32 +1913,14 @@
     return -(-items // LANES)
 
 
-def bank_blocks(grad_filters, bank_cols, groups):
-    turned = grad_filters.T
-    blocks, at = [], 0
-    for bank_specs in bank_plan(bank_cols):
-        used = sum(count for width, first, count in bank_specs)
-        piece = turned[at : at + used].reshape(groups, used // groups, LANES)
-        blocks.append(jnp.pad(piece, ((0, 0), (0, (bank_cols - used) // groups), (0, 0))))
-        at += used
-    return jnp.stack(blocks, axis=1).reshape(groups * len(blocks), bank_cols // groups, LANES)
-
-
-def bank_filters(blocks, bank, bank_cols, groups):
+def bank_filters(turned, bank, bank_cols):
     taps = [
         [width * EMBED for width, first, count in bank_specs for _ in range(count)]
         for bank_specs in bank_plan(bank_cols)
     ]
     taps = [row + [0] * (bank_cols - len(row)) for row in taps]
     limit = lax.dynamic_index_in_dim(jnp.asarray(taps, jnp.int32), bank, 0, False)
-    used = [sum(count for width, first, count in specs) for specs in bank_plan(bank_cols)]
-    choices = [
-        lambda value, each=count // groups: jnp.pad(
-            value[:, :each].reshape(groups * each, LANES), ((0, bank_cols - groups * each), (0, 0))
-        )
-        for count in used
-    ]
-    turned = lax.switch(bank, choices, blocks).T
+    turned = turned.T
     row = lax.broadcasted_iota(jnp.int32, (TAPS, 1), 0)
     kernel = jnp.where(row < limit[None, :], turned[:TAPS], 0.0)
     bias = jnp.where(limit > 0, turned[TAPS], 0.0)
@@ -1846,9 +2043,17 @@
         mixed,
         hidden,
         top_own,
-        lin_parts,
+        lin_all,
     ) = run_highway(
-        tight_from, tiled, filters, counts, block, lstm_block, turned_block, highway_bias_own
+        tight_from,
+        tiled,
+        filters,
+        counts,
+        block,
+        lstm_block,
+        turned_block,
+        highway_bias_own,
+        proj_bias_all[None],
     )
     lstm_own = lstm_own.reshape(grid, t, 2, 4, x * c * lstm_rows, cells)
 
@@ -1859,8 +2064,7 @@
     keep = jnp.stack([keep_forward.T, keep_backward.T])[..., None]
     grad_time = out_grad.reshape(own, steps, 2, width).transpose(2, 1, 0, 3)
     grad_lin_all, lstm_grads, turned_grads, bias_sums = run_lstm(
-        lin_parts.reshape(team, steps, own, width),
-        proj_bias_all[None],
+        lin_all.reshape(team, steps, own, width),
         grad_time,
         lstm_own,
         turned_own,
@@ -1881,19 +2085,7 @@
         hidden,
         top_own,
     )
-    grad_features = restored_columns(grad_features)
-    grad_filters, grad_table = pool_grads(
-        padded_ids,
-        tiled,
-        filters,
-        counts,
-        pooled_lse,
-        grad_features,
-        char_table.shape[0],
-        tight_from,
-    )
-    lstm_returned = swap_team(member_rows(lstm_summed))
-    lstm_weight_grad = whole_columns(lstm_returned, 4).astype(f32)
+    turned_summed, grad_features = lax.optimization_barrier((turned_summed, grad_features))
     turned_grad = whole_columns(swap_team(member_rows(turned_summed)), 1).astype(f32)
     lstm_proj_grad = jnp.swapaxes(turned_grad, 1, 2)
     g, t, y, x, c = axis_sizes()
@@ -1919,46 +2111,32 @@
         ],
         axis=1,
     )
-    groups = g * t * y
-    table_items = -(-grad_table.size // groups)
-    table_flat = jnp.pad(grad_table.reshape(-1), (0, groups * table_items - grad_table.size))
-    table_blocks = jnp.broadcast_to(
-        padded_rows(table_flat.reshape(groups, table_items), row_count(table_items))[:, None],
-        (groups, x * c, row_count(table_items), LANES),
-    ).reshape(devices, -1, LANES)
-    filter_blocks = bank_blocks(grad_filters, bank_cols, groups)
-    shared = -(-(filter_blocks.shape[1] + table_blocks.shape[1]) // 8) * 8
-    fill = shared - filter_blocks.shape[1] - table_blocks.shape[1]
-    bias_rows = -(-(shared + row_count(biases.shape[1])) // 16) * 16 - shared
-    small = jnp.concatenate(
-        [
-            filter_blocks,
-            jnp.pad(table_blocks, ((0, 0), (0, fill), (0, 0))),
-            padded_rows(biases, bias_rows),
-        ],
-        axis=1,
-    ).astype(bf16)
-    highway_returned, project_grad, mine, both = run_return(
-        first_parts, small, 2 * highway_rows, shared, groups
-    )
-    highway_weight_grad = (
-        highway_returned.reshape(t, x, c, 2 * highway_rows, 2, g, y, -1)
-        .transpose(3, 4, 5, 0, 6, 1, 2, 7)
-        .reshape(2, highway_rows, 2 * features_all)
-        .astype(f32)
-    )
-
-    mine_biases = mine[shared:].reshape(-1)
+    bank_counts = [sum(item[2] for item in specs) for specs in bank_plan(bank_cols)]
+    bias_rows = -(-row_count(biases.shape[1]) // 16) * 16
+    highway_weight_grad, project_grad, mine, conv_sums, table_sums = run_final(
+        tight_from,
+        bank_counts,
+        first_parts,
+        tiled,
+        padded_ids.reshape(-1, math.gcd(tokens, TOKEN_BLOCK) * PLACES),
+        filters,
+        counts,
+        pooled_lse,
+        grad_features,
+        padded_rows(biases, bias_rows).astype(bf16),
+        2 * highway_rows,
+    )
+    lstm_summed, highway_weight_grad = lax.optimization_barrier((lstm_summed, highway_weight_grad))
+    lstm_returned = swap_team(member_rows(lstm_summed))
+    lstm_weight_grad = pack_columns(lstm_returned, 4).reshape(2, lstm_rows, -1)
+    highway_weight_grad = highway_weight_grad.reshape(2, highway_rows, -1)
+    mine_biases = mine.reshape(-1)
     ends = [2 * lstm_bias.shape[1], 2 * lstm_bias.shape[1] + 2 * highway_bias.shape[1]]
     lstm_bias_grad = mine_biases[: ends[0]].reshape(2, -1)
     highway_bias_grad = mine_biases[ends[0] : ends[1]].reshape(2, -1)
     proj_bias_grad = mine_biases[ends[1] : ends[1] + proj_bias.size]
-    grad_kernel, grad_bias = bank_filters(
-        both[:, : filter_blocks.shape[1]], bank, bank_cols, groups
-    )
-    table_end = filter_blocks.shape[1] + table_blocks.shape[1]
-    grad_table = both[:, filter_blocks.shape[1] : table_end].reshape(groups, -1)[:, :table_items]
-    grad_table = grad_table.reshape(-1)[: char_table.size].reshape(char_table.shape)
+    grad_kernel, grad_bias = bank_filters(conv_sums, bank, bank_cols)
+    grad_table = table_sums[: char_table.shape[0], :EMBED]
     return (
         grad_table,
         grad_kernel,

time: 808 us -> 738 us (0.913)
  local copies, waits for them, and re-layouts: 110 us -> 51 us
  waiting for transfers between devices: 7.52 us -> 44.8 us
  Pallas kernels: 601 us -> 569 us
  other arithmetic: 20.5 us -> 11.7 us
    pallas_call x3, Pallas kernels: 300 us -> 257 us  [the longest x1 135 us: run_lstm(): pl.pallas_call(partial(lstm_kernel, team), in_specs=[vmem, vmem, hbm, hbm...]
    all_to_all x3, waiting for transfers between devices: 1.65 us -> 40.7 us  [swap_team(): return lax.all_to_all(values, TEAM, split_axis=0, concat_axis=0, tiled=True)]
    convert_element_type x6 -> x0, local copies, waits for them, and re-layouts: 31.5 us -> none  [the longest x3 16 us: shards(): lstm_weight_grad = whole_columns(lstm_returned, 4).astype(f32)]
    pallas_call x1, Pallas kernels: 182 us -> 193 us  [run_highway(): pl.pallas_call(partial(highway_kernel, tight_from), in_specs=[vmem] * 3 +...]
  transfers between devices with their start and end apart: 7 -> 7, of which waited for: 4 -> 3; matrix products, arithmetic and copies ran while one was open for 13% -> 7% of each run, Pallas kernels for 32% -> 33%
where the time goes in v5:
time: 738 us; the launch traced here: 727 us
  Pallas kernels  569 us (77%)
  local copies, waits for them, and re-layouts  51 us (7%)
  waiting for transfers between devices  44.8 us (6%)
  starting transfers between devices  32.2 us (4%)
  between operations  15 us (2%)
  other arithmetic  11.7 us (2%)
    pallas_call x1, Pallas kernels, run_highway(): pl.pallas_call(partial(highway_kernel, tight_from), in_specs=[vmem] * 3 +...  193 us
    pallas_call x1, Pallas kernels, run_lstm(): pl.pallas_call(partial(lstm_kernel, team), in_specs=[vmem, vmem, hbm, hbm...  135 us
    pallas_call x1, Pallas kernels, run_final(): pl.pallas_call(partial(final_kernel, tight_from, bank_counts), in_specs=[...  120 us
    pallas_call x1, Pallas kernels, run_highway_back(): pl.pallas_call(highway_back_kernel, in_specs=[vmem, hbm] + [vmem] * 5, ou...  119 us
    all_to_all x3, waiting for transfers between devices, swap_team(): return lax.all_to_all(values, TEAM, split_axis=0, concat_axis=0, tiled=True)  40.7 us
    all_to_all x3, starting transfers between devices, swap_team(): return lax.all_to_all(values, TEAM, split_axis=0, concat_axis=0, tiled=True)  17.4 us
  transfers between devices with their start and end apart: 7, of which 3 were waited for; matrix products, arithmetic and copies ran while one was open for 7% of the time, Pallas kernels for 33%

profile of v5, /device:TPU:14, one launch (start us, length us, event | category | flops | bytes accessed | tf_op | source)
XLA Modules:
  0.0 727.4 jit_solution(16356059656790319934)
XLA Ops:
  13.0 6.0 all-to-all-start.2
  20.0 4.2 all-to-all-done.2
  25.3 4.7 all-to-all-start
  30.8 2.5 copy.165
  33.3 4.4 reshape_reshape.18
  37.8 4.4 copy.164
  42.1 2.4 copy.167
  44.7 3.0 pad_maximum_fusion
  47.7 5.4 all-to-all-start.1
  55.0 3.3 convolution_convert_fusion
  64.7 26.8 %all-to-all-done.1 = bf16[8,416,512]{2,1,0:T(8,128)(2,1)} async-done(((bf16[8,416,512]{2,1,0:T(8,128)(2,1)}), bf16[8,416,512]{2,1,0:T(8,128)(2,1)}, u32[]{:S(2)}, u32[]{:S(2)}) %all-to-all-start.1) | async-done | bytes 3407904 | tf_op jit(solution)/shard_map/all_to_all | solution.py:236
  91.5 1.8 slice.151
  98.9 192.6 %highway_team.1 = (f32[128,2048]{1,0:T(8,128)}, bf16[4,1088,512]{2,1,0:T(8,128)(2,1)}, bf16[4,16,128,512]{3,2,1,0:T(8,128)(2,1)}, bf16[4,2,2,64,512]{4,3,2,1,0:T...) custom-call(bf16[128,64,128]{2,1,0:T(8,128)(2,1)} %bitcast.150, ...), custom_call_target="tpu_custom_call" | custom-call | tf_op jit(solution)/shard_map/highway_team/pallas_call | solution.py:1135
  291.5 135.3 %lstm_team.1 = (bf16[8,4,32,512]{3,2,1,0:T(8,128)(2,1)}, bf16[4,2,2,128,2048]{4,3,2,1,0:T(8,128)(2,1)}, bf16[4,2,2,64,512]{4,3,2,1,0:T(8,128)(2,1)}, f32[2,8,2048]{2,1,0:T(8,128)}) custom-call(bf16[8,4,32,512]{3,2,1,0:T(8,128)(2,1)} %bitcast.171, bf16[2,4,32,512]{3,2,1,0:T(8,128)(2,1)} %bitcast.172, bf16[4,2,2,4,128,512]{5,4,3,2,1,0:T(8,128)(2,1)} %bitcast.149, ...), custom_call_target="tpu_custom_call" | custom-call | tf_op jit(solution)/shard_map/lstm_team/pallas_call | solution.py:646
  426.8 4.1 all-to-all-start.3
  432.7 119.1 %highway_team_back.1 = (bf16[128,2048]{1,0:T(8,128)(2,1)}, bf16[4,1088,512]{2,1,0:T(8,128)(2,1)}, f32[2,8,512]{2,1,0:T(8,128)}) custom-call(bf16[8,128,512]{2,1,0:T(8,128)(2,1)} %bitcast.164, bf16[4,1088,512]{2,1,0:T(8,128)(2,1)} %get-tuple-element.40.first_hbm, bf16[8,128,2048]{2,1,0:T(8,128)(2,1)} %get-tuple-element.41.first_ref, ...), custom_call_target="tpu_custom_call" | custom-call | tf_op jit(solution)/shard_map/highway_team_back/pallas_call | solution.py:1401
  553.2 5.4 all-to-all-start.5
  561.4 119.7 %final_sums.1 = (f32[128,4096]{1,0:T(8,128)}, f32[64,512]{1,0:T(8,128)}, f32[16,128]{1,0:T(8,128)}, f32[1024,128]{1,0:T(8,128)}, f32[384,128]{1,0:T(8,128)}) custom-call(bf16[4,1088,512]{2,1,0:T(8,128)(2,1)} %get-tuple-element.46.grads_ref, bf16[128,64,128]{2,1,0:T(8,128)(2,1)} %bitcast.151, s32[8,1024]{1,0:T(8,128)} %reshape.236.ids_ref, ...), custom_call_target="tpu_custom_call" | custom-call | tf_op jit(solution)/shard_map/final_sums/pallas_call | solution.py:1791
  681.2 3.2 copy.185
  684.4 6.6 all-to-all-start.4
  692.9 2.0 copy.184
  696.1 1.8 copy.189
  701.9 13.8 %all-to-all-done.4.received_ref = bf16[8,64,2048]{2,1,0:T(8,128)(2,1)S(1)} async-done(((bf16[8,64,2048]{2,1,0:T(8,128)(2,1)}), bf16[8,64,2048]{2,1,0:T(8,128)(2,1)S(1)}, u32[]{:S(2)}, u32[]{:S(2)}) %all-to-all-start.4) | async-done | bytes 2097184 | tf_op jit(solution)/shard_map/all_to_all | solution.py:236
  715.7 2.3 pack_columns.1
  (156 shorter events, 37.6 us)
Async XLA Ops:
  7.2 45.9 %copy-start = (s32[128,4,50]{0,1,2:T(4,128)S(1)}, s32[128,4,50]{0,1,2:T(4,128)}, u32[]{:S(2)}) copy-start(s32[128,4,50]{0,1,2:T(4,128)} %param.14) | copy-start | bytes 307204
  7.2 22.8 %copy-start.3 = (bf16[2,32,16384]{2,1,0:T(8,128)(2,1)S(1)}, bf16[2,32,16384]{2,1,0:T(8,128)(2,1)}, u32[]{:S(2)}) copy-start(bf16[2,32,16384]{2,1,0:T(8,128)(2,1)} %param.24) | copy-start | bytes 6291460
  13.0 11.1 %all-to-all-start.2 = ((bf16[32,2,712]{2,1,0:T(2,128)(2,1)}), bf16[32,2,712]{2,1,0:T(2,128)(2,1)S(1)}, u32[]{:S(2)}, u32[]{:S(2)}) async-start(bf16[32,2,712]{2,1,0:T(2,128)(2,1)} %reshape.263), calls=%async_computation.2 | async-start | bytes 196608 | tf_op jit(solution)/shard_map/all_to_all | solution.py:1979
  25.3 22.4 %all-to-all-start = ((bf16[4,113,1024]{2,1,0:T(8,128)(2,1)}), bf16[4,113,1024]{2,1,0:T(8,128)(2,1)S(1)}, u32[]{:S(2)}, u32[]{:S(2)}) async-start(bf16[4,113,1024]{2,1,0:T(8,128)(2,1)} %broadcast_in_dim.69), calls=%async_computation | async-start | bytes 1966080 | tf_op jit(solution)/shard_map/all_to_all | solution.py:1961
  37.7 6.8 copy-start.7
  42.1 2.6 copy-start.2
  47.7 5.7 copy-start.8
  47.7 7.3 %copy-start.11 = (bf16[262,16]{0,1:T(8,128)(2,1)S(1)}, bf16[262,16]{0,1:T(8,128)(2,1)}, u32[]{:S(2)}) copy-start(bf16[262,16]{0,1:T(8,128)(2,1)} %param.17) | copy-start | bytes 25156
  47.7 43.8 %all-to-all-start.1 = ((bf16[8,416,512]{2,1,0:T(8,128)(2,1)}), bf16[8,416,512]{2,1,0:T(8,128)(2,1)}, u32[]{:S(2)}, u32[]{:S(2)}) async-start(bf16[8,416,512]{2,1,0:T(8,128)(2,1)} %pad_maximum_fusion), calls=%async_computation.1 | async-start | bytes 6815744 | tf_op jit(solution)/shard_map/all_to_all | solution.py:236
  53.1 628.0 %reduce-scatter.2.cloned.1.call-start = ((), (), s32[]{:S(2)}) async-start(), calls=%async_computation.7 | async-start | bytes 10485760 | tf_op jit(solution)/shard_map/reduce_scatter | solution.py:2074
  93.3 4.6 copy-start.10
  426.8 125.4 %all-to-all-start.3 = ((bf16[4,2,2,64,512]{4,3,2,1,0:T(8,128)(2,1)}), bf16[4,2,2,64,512]{4,3,2,1,0:T(8,128)(2,1)S(1)}, u32[]{:S(2)}, u32[]{:S(2)}) async-start(bf16[4,2,2,64,512]{4,3,2,1,0:T(8,128)(2,1)} %get-tuple-element.48), calls=%async_computation.3 | async-start | bytes 2097152 | tf_op jit(solution)/shard_map/all_to_all | solution.py:2075
  553.2 131.2 %all-to-all-start.5 = ((bf16[8,32,512]{2,1,0:T(8,128)(2,1)}), bf16[8,32,512]{2,1,0:T(8,128)(2,1)S(1)}, u32[]{:S(2)}, u32[]{:S(2)}) async-start(bf16[8,32,512]{2,1,0:T(8,128)(2,1)} %bitcast.70), calls=%async_computation.6 | async-start | bytes 524288 | tf_op jit(solution)/shard_map/all_to_all | solution.py:236
  681.2 9.8 %copy-start.5 = (s32[4,1024]{0,1:T(8,128)S(1)}, s32[4,1024]{0,1:T(8,128)}, u32[]{:S(2)}) copy-start(s32[4,1024]{0,1:T(8,128)} %constant.115.clone) | copy-start | bytes 49156
  684.4 7.0 copy-start.12
  684.4 7.5 %copy-start.6 = (f32[1024,128]{1,0:T(8,128)S(1)}, f32[1024,128]{1,0:T(8,128)}, u32[]{:S(2)}) copy-start(f32[1024,128]{1,0:T(8,128)} %get-tuple-element.54) | copy-start | bytes 1572868
  684.4 31.3 %all-to-all-start.4 = ((bf16[8,64,2048]{2,1,0:T(8,128)(2,1)}), bf16[8,64,2048]{2,1,0:T(8,128)(2,1)S(1)}, u32[]{:S(2)}, u32[]{:S(2)}) async-start(bf16[8,64,2048]{2,1,0:T(8,128)(2,1)} %bitcast.152), calls=%async_computation.5 | async-start | bytes 4194304 | tf_op jit(solution)/shard_map/all_to_all | solution.py:236
  715.7 2.4 copy-start.4
  715.7 4.4 copy-start.1
  718.0 1.5 copy-start.9
Sparse Core Ops, SparseCore 0:
  427.0 223.3 reduce-scatter.1

commit v6 on v5

--- a/solution.py
+++ b/solution.py
@@ -1181,9 +1181,15 @@
     mixed_ref,
     hidden_ref,
     top_ref,
+    lstm_hbm,
     features_ref,
     grads_hbm,
     bias_ref,
+    lstm_ref,
+    lstm_own,
+    lstm_y,
+    lstm_send,
+    lstm_g,
     weights,
     project,
     grad_mixed,
@@ -1208,6 +1214,10 @@
     row_sib_sems,
     row_sems,
     out_sems,
+    lstm_load_sems,
+    lstm_send_sems,
+    lstm_y_sems,
+    lstm_g_sems,
 ):
     team, tokens, features = first_ref.shape
     part = features // team
@@ -1219,8 +1229,49 @@
     sibling = member_at(1)
     near = list(range(1, chips))
     load_highway(first_hbm, weights, project, load_sems)
-    greet([1] + [chip * cores for chip in near])
+    greet([1] + [chip * cores for chip in near], True)
     f32, bf16 = jnp.float32, jnp.bfloat16
+    g_size, y_size = lax.axis_size("g"), lax.axis_size("y")
+    y_index = lax.axis_index("y")
+    other_y = lax.rem(y_index + 1, y_size)
+    chunks = lstm_ref.shape[0]
+
+    def lstm_block(dg, y):
+        return lax.rem(lax.axis_index("g") + dg, g_size) * y_size + y
+
+    @pl.loop(0, chunks)
+    def _(chunk):
+        for dg in list(range(1, g_size)) + [0]:
+            send_grid(
+                lstm_hbm.at[lstm_block(dg, other_y), chunk],
+                lstm_y.at[dg, chunk],
+                lstm_send_sems.at[0],
+                lstm_y_sems.at[chunk, dg],
+                0,
+                1,
+            )
+
+    pltpu.make_async_copy(
+        lstm_hbm.at[lstm_block(0, y_index)], lstm_ref, lstm_load_sems.at[0]
+    ).start()
+    for dg in range(1, g_size):
+        pltpu.make_async_copy(
+            lstm_hbm.at[lstm_block(dg, y_index)], lstm_own.at[dg - 1], lstm_load_sems.at[1]
+        ).start()
+
+    def pump(chunk):
+        for dg in range(1, g_size):
+            wait_bytes(lstm_y.at[dg, chunk], lstm_y_sems.at[chunk, dg])
+            both = lstm_own[dg - 1, chunk].astype(f32) + lstm_y[dg, chunk].astype(f32)
+            lstm_send[dg - 1, chunk] = both.astype(bf16)
+            send_grid(
+                lstm_send.at[dg - 1, chunk],
+                lstm_g.at[g_size - dg - 1, chunk],
+                lstm_send_sems.at[1],
+                lstm_g_sems.at[chunk, g_size - dg - 1],
+                dg,
+                0,
+            )
 
     def columns(member):
         return pl.ds(pl.multiple_of(member * part, part), part)
@@ -1266,6 +1317,9 @@
                 column_sib_sems.at[member],
                 sibling,
             )
+
+    wait_bytes(lstm_own, lstm_load_sems.at[1])
+    pump(0)
 
     @pl.loop(0, team)
     def _(member):
@@ -1319,7 +1373,9 @@
             preferred_element_type=f32,
         )
 
+    pump(1)
     weight_grads(1, second_ref)
+    pump(2)
 
     @pl.loop(0, team)
     def _(step):
@@ -1349,6 +1405,10 @@
         @pl.when(lax.rem(offset, cores) == 0)
         def _():
             row_keep[chip] = row_part[...].astype(bf16)
+
+        @pl.when((step == team // 2 - 1) | (step == team - 1))
+        def _():
+            pump(3 + (step + 1) // team)
 
     for chip in near[::-1] + [0]:
         wait_bytes(row_sibling.at[chip], row_sib_sems.at[chip])
@@ -1365,7 +1425,13 @@
                 member_at(chip * cores),
             )
 
+    pump(5)
     weight_grads(0, first_ref)
+
+    @pl.loop(6, chunks)
+    def _(chunk):
+        pump(chunk)
+
     grad_stage[0] = lax.dot_general(
         top_ref[...].reshape(team * tokens, part),
         grad_lin_ref[...].reshape(team * tokens, 2 * part),
@@ -1383,6 +1449,19 @@
         wait_bytes(row_recv.at[other - 1], row_sems.at[other - 1])
         total = total + row_recv[other - 1].astype(f32)
     features_ref[...] = total.astype(bf16)
+    wait_bytes(lstm_ref, lstm_load_sems.at[0])
+
+    @pl.loop(0, chunks)
+    def _(chunk):
+        wait_bytes(lstm_y.at[0, chunk], lstm_y_sems.at[chunk, 0])
+        whole = lstm_ref[chunk].astype(f32) + lstm_y[0, chunk].astype(f32)
+        for dg in range(1, g_size):
+            wait_bytes(lstm_g.at[dg - 1, chunk], lstm_g_sems.at[chunk, dg - 1])
+            whole = whole + lstm_g[dg - 1, chunk].astype(f32)
+        lstm_ref[chunk] = whole.astype(bf16)
+
+    wait_bytes(lstm_y, lstm_send_sems.at[0])
+    wait_bytes(lstm_g, lstm_send_sems.at[1])
     wait_bytes(grad_stage.at[0], out_sems.at[0])
     wait_bytes(column_sibling, send_sems.at[0])
     wait_bytes(column_send, send_sems.at[1])
@@ -1390,24 +1469,31 @@
     wait_bytes(row_send, send_sems.at[3])
 
 
-def run_highway_back(grad_lin, first_all, first, second, mixed, hidden, top):
+def run_highway_back(grad_lin, first_all, first, second, mixed, hidden, top, lstm_grads):
     team, tokens, features = first.shape
     part = features // team
     chips = team // lax.axis_size("c")
     width = first_all.shape[2]
     bf16, f32 = jnp.bfloat16, jnp.float32
+    g_size = lax.axis_size("g")
+    chunk_shape = lstm_grads.shape[1:]
     vmem = pl.BlockSpec(memory_space=pltpu.VMEM)
     hbm = pl.BlockSpec(memory_space=pl.ANY)
     return pl.pallas_call(
         highway_back_kernel,
-        in_specs=[vmem, hbm] + [vmem] * 5,
-        out_specs=[vmem, hbm, vmem],
+        in_specs=[vmem, hbm] + [vmem] * 5 + [hbm],
+        out_specs=[vmem, hbm, vmem, vmem],
         out_shape=[
             jax.ShapeDtypeStruct((tokens, features), bf16),
             jax.ShapeDtypeStruct(first_all.shape, bf16),
             jax.ShapeDtypeStruct((2, 8, 2 * part), f32),
+            jax.ShapeDtypeStruct(chunk_shape, bf16),
         ],
         scratch_shapes=[
+            pltpu.VMEM((g_size - 1,) + chunk_shape, bf16),
+            pltpu.VMEM((g_size,) + chunk_shape, bf16),
+            pltpu.VMEM((g_size - 1,) + chunk_shape, bf16),
+            pltpu.VMEM((g_size - 1,) + chunk_shape, bf16),
             pltpu.VMEM((2, features, 2 * part), bf16),
             pltpu.VMEM((part, width), bf16),
             pltpu.VMEM((2, team, tokens, 2 * part), bf16),
@@ -1432,12 +1518,16 @@
             pltpu.SemaphoreType.DMA((chips,)),
             pltpu.SemaphoreType.DMA((chips - 1,)),
             pltpu.SemaphoreType.DMA((2,)),
+            pltpu.SemaphoreType.DMA((2,)),
+            pltpu.SemaphoreType.DMA((2,)),
+            pltpu.SemaphoreType.DMA((chunk_shape[0], g_size)),
+            pltpu.SemaphoreType.DMA((chunk_shape[0], g_size - 1)),
         ],
         compiler_params=pltpu.CompilerParams(
-            collective_id=3, has_side_effects=True, vmem_limit_bytes=60 * 1024 * 1024
+            collective_id=3, has_side_effects=True, vmem_limit_bytes=63 * 1024 * 1024
         ),
         name="highway_team_back",
-    )(grad_lin, first_all, first, second, mixed, hidden, top)
+    )(grad_lin, first_all, first, second, mixed, hidden, top, lstm_grads)
 
 
 def every_coords(shift):
@@ -2071,12 +2161,11 @@
         lstm_bias_own,
         keep,
     )
-    lstm_summed = lax.psum_scatter(lstm_grads, GRID, scatter_dimension=0, tiled=False)
     turned_summed = lax.all_to_all(turned_grads, GRID, split_axis=0, concat_axis=0, tiled=True)
     turned_summed = turned_summed.astype(f32).sum(axis=0).astype(bf16)
     grad_input = lax.dynamic_index_in_dim(grad_lin_all, place, 0, False).reshape(tokens, width)
     grad_project_b = column_sum(grad_input)
-    grad_features, first_parts, highway_bias_sums = run_highway_back(
+    grad_features, first_parts, highway_bias_sums, lstm_summed = run_highway_back(
         grad_lin_all.reshape(team, tokens, width),
         first_all,
         first,
@@ -2084,7 +2173,9 @@
         mixed,
         hidden,
         top_own,
-    )
+        lstm_grads.reshape(grid, 8, -1, 4 * cells),
+    )
+    lstm_summed = lstm_summed.reshape(t, 2, -1, 4 * cells)
     turned_summed, grad_features = lax.optimization_barrier((turned_summed, grad_features))
     turned_grad = whole_columns(swap_team(member_rows(turned_summed)), 1).astype(f32)
     lstm_proj_grad = jnp.swapaxes(turned_grad, 1, 2)
@@ -2126,7 +2217,6 @@
         padded_rows(biases, bias_rows).astype(bf16),
         2 * highway_rows,
     )
-    lstm_summed, highway_weight_grad = lax.optimization_barrier((lstm_summed, highway_weight_grad))
     lstm_returned = swap_team(member_rows(lstm_summed))
     lstm_weight_grad = pack_columns(lstm_returned, 4).reshape(2, lstm_rows, -1)
     highway_weight_grad = highway_weight_grad.reshape(2, highway_rows, -1)

time: 738 us -> 694 us (0.940)
  Pallas kernels: 569 us -> 555 us
  between operations: 15 us -> 1.47 us
  waiting for transfers between devices: 44.8 us -> 34.1 us
    pallas_call x1, Pallas kernels: 120 us -> 95.8 us  [run_final(): pl.pallas_call(partial(final_kernel, tight_from, bank_counts), in_specs=[...]
    all_to_all x3, waiting for transfers between devices: 40.7 us -> 29.9 us  [swap_team(): return lax.all_to_all(values, TEAM, split_axis=0, concat_axis=0, tiled=True)]
    pallas_call x1, Pallas kernels: 119 us -> 128 us  [run_highway_back(): pl.pallas_call(highway_back_kernel, in_specs=[vmem, hbm] + [vmem] * 5 + [...]
  transfers between devices with their start and end apart: 7 -> 6, of which waited for: 3 -> 3; matrix products, arithmetic and copies ran while one was open for 7% -> 7% of each run, Pallas kernels for 33% -> 33%
where the time goes in v6:
time: 694 us; the launch traced here: 686 us
  Pallas kernels  555 us (80%)
  local copies, waits for them, and re-layouts  49.2 us (7%)
  waiting for transfers between devices  34.1 us (5%)
  starting transfers between devices  29.8 us (4%)
  other arithmetic  13.5 us (2%)
    pallas_call x1, Pallas kernels, run_highway(): pl.pallas_call(partial(highway_kernel, tight_from), in_specs=[vmem] * 3 +...  193 us
    pallas_call x1, Pallas kernels, run_lstm(): pl.pallas_call(partial(lstm_kernel, team), in_specs=[vmem, vmem, hbm, hbm...  136 us
    pallas_call x1, Pallas kernels, run_highway_back(): pl.pallas_call(highway_back_kernel, in_specs=[vmem, hbm] + [vmem] * 5 + [...  128 us
    pallas_call x1, Pallas kernels, run_final(): pl.pallas_call(partial(final_kernel, tight_from, bank_counts), in_specs=[...  95.8 us
    all_to_all x3, waiting for transfers between devices, swap_team(): return lax.all_to_all(values, TEAM, split_axis=0, concat_axis=0, tiled=True)  29.9 us
    all_to_all x3, starting transfers between devices, swap_team(): return lax.all_to_all(values, TEAM, split_axis=0, concat_axis=0, tiled=True)  14.8 us
  transfers between devices with their start and end apart: 6, of which 3 were waited for; matrix products, arithmetic and copies ran while one was open for 7% of the time, Pallas kernels for 33%

profile of v6, /device:TPU:14, one launch (start us, length us, event | category | flops | bytes accessed | tf_op | source)
XLA Modules:
  0.0 686.2 jit_solution(9937486188628395245)
XLA Ops:
  6.5 6.0 all-to-all-start.2
  13.4 4.2 all-to-all-done.2
  18.7 4.7 all-to-all-start
  24.3 2.5 copy.165
  26.7 4.4 reshape_reshape.21
  31.2 4.4 copy.164
  35.6 2.4 copy.167
  38.2 3.0 pad_maximum_fusion
  41.2 5.6 all-to-all-start.1
  48.7 3.3 convolution_convert_fusion
  58.4 26.7 %all-to-all-done.1 = bf16[8,416,512]{2,1,0:T(8,128)(2,1)} async-done(((bf16[8,416,512]{2,1,0:T(8,128)(2,1)}), bf16[8,416,512]{2,1,0:T(8,128)(2,1)}, u32[]{:S(2)}, u32[]{:S(2)}) %all-to-all-start.1) | async-done | bytes 3407904 | tf_op jit(solution)/shard_map/all_to_all | solution.py:236
  85.1 1.8 slice.151
  87.0 1.6 copy.168
  92.6 192.5 %highway_team.1 = (f32[128,2048]{1,0:T(8,128)}, bf16[4,1088,512]{2,1,0:T(8,128)(2,1)}, bf16[4,16,128,512]{3,2,1,0:T(8,128)(2,1)}, bf16[4,2,2,64,512]{4,3,2,1,0:T...) custom-call(bf16[128,64,128]{2,1,0:T(8,128)(2,1)} %bitcast.151, ...), custom_call_target="tpu_custom_call" | custom-call | tf_op jit(solution)/shard_map/highway_team/pallas_call | solution.py:1135
  285.1 135.6 %lstm_team.1 = (bf16[8,4,32,512]{3,2,1,0:T(8,128)(2,1)}, bf16[4,2,2,128,2048]{4,3,2,1,0:T(8,128)(2,1)}, bf16[4,2,2,64,512]{4,3,2,1,0:T(8,128)(2,1)}, f32[2,8,2048]{2,1,0:T(8,128)}) custom-call(bf16[8,4,32,512]{3,2,1,0:T(8,128)(2,1)} %bitcast.172, bf16[2,4,32,512]{3,2,1,0:T(8,128)(2,1)} %bitcast.173, bf16[4,2,2,4,128,512]{5,4,3,2,1,0:T(8,128)(2,1)} %bitcast.150, ...), custom_call_target="tpu_custom_call" | custom-call | tf_op jit(solution)/shard_map/lstm_team/pallas_call | solution.py:646
  420.8 4.2 all-to-all-start.3
  425.0 128.2 %highway_team_back.1 = (bf16[128,2048]{1,0:T(8,128)(2,1)}, bf16[4,1088,512]{2,1,0:T(8,128)(2,1)}, f32[2,8,512]{2,1,0:T(8,128)}, bf16[8,64,2048]{2,1,0:T(8,128)(2,1)}) custom-call(bf16[8,128,512]{2,1,0:T(8,128)(2,1)} %bitcast.165, bf16[4,1088,512]{2,1,0:T(8,128)(2,1)} %get-tuple-element.39.first_hbm, bf16[8,128,2048]{2,1,0:T(8,128)(2,1)} %get-tuple-element.40.first_ref, ...), custom_call_target="tpu_custom_call" | custom-call | tf_op jit(solution)/shard_map/highway_team_back/pallas_call | solution.py:1482
  553.3 1.6 reduce_sum.12
  555.6 4.2 all-to-all-start.5
  559.8 1.5 copy.185
  561.3 3.2 all-to-all-done.5
  564.4 5.0 all-to-all-start.4
  574.7 95.8 %final_sums.1 = (f32[128,4096]{1,0:T(8,128)}, f32[64,512]{1,0:T(8,128)}, f32[16,128]{1,0:T(8,128)}, f32[1024,128]{1,0:T(8,128)}, f32[384,128]{1,0:T(8,128)}) custom-call(bf16[4,1088,512]{2,1,0:T(8,128)(2,1)} %get-tuple-element.46.grads_ref, bf16[128,64,128]{2,1,0:T(8,128)(2,1)} %bitcast.152, s32[8,1024]{1,0:T(8,128)} %reshape.237.ids_ref, ...), custom_call_target="tpu_custom_call" | custom-call | tf_op jit(solution)/shard_map/final_sums/pallas_call | solution.py:1881
  681.5 2.3 pack_columns.1
  (151 shorter events, 40.0 us)
Async XLA Ops:
  0.6 46.2 %copy-start = (s32[128,4,50]{0,1,2:T(4,128)S(1)}, s32[128,4,50]{0,1,2:T(4,128)}, u32[]{:S(2)}) copy-start(s32[128,4,50]{0,1,2:T(4,128)} %param.14) | copy-start | bytes 307204
  0.7 22.8 %copy-start.3 = (bf16[2,32,16384]{2,1,0:T(8,128)(2,1)S(1)}, bf16[2,32,16384]{2,1,0:T(8,128)(2,1)}, u32[]{:S(2)}) copy-start(bf16[2,32,16384]{2,1,0:T(8,128)(2,1)} %param.24) | copy-start | bytes 6291460
  6.5 11.1 %all-to-all-start.2 = ((bf16[32,2,712]{2,1,0:T(2,128)(2,1)}), bf16[32,2,712]{2,1,0:T(2,128)(2,1)S(1)}, u32[]{:S(2)}, u32[]{:S(2)}) async-start(bf16[32,2,712]{2,1,0:T(2,128)(2,1)} %reshape.263), calls=%async_computation.2 | async-start | bytes 196608 | tf_op jit(solution)/shard_map/all_to_all | solution.py:2069
  18.7 22.4 %all-to-all-start = ((bf16[4,113,1024]{2,1,0:T(8,128)(2,1)}), bf16[4,113,1024]{2,1,0:T(8,128)(2,1)S(1)}, u32[]{:S(2)}, u32[]{:S(2)}) async-start(bf16[4,113,1024]{2,1,0:T(8,128)(2,1)} %broadcast_in_dim.69), calls=%async_computation | async-start | bytes 1966080 | tf_op jit(solution)/shard_map/all_to_all | solution.py:2051
  31.2 6.8 copy-start.7
  35.6 2.6 copy-start.2
  41.1 6.0 copy-start.8
  41.1 7.5 %copy-start.11 = (bf16[262,16]{0,1:T(8,128)(2,1)S(1)}, bf16[262,16]{0,1:T(8,128)(2,1)}, u32[]{:S(2)}) copy-start(bf16[262,16]{0,1:T(8,128)(2,1)} %param.17) | copy-start | bytes 25156
  41.2 44.0 %all-to-all-start.1 = ((bf16[8,416,512]{2,1,0:T(8,128)(2,1)}), bf16[8,416,512]{2,1,0:T(8,128)(2,1)}, u32[]{:S(2)}, u32[]{:S(2)}) async-start(bf16[8,416,512]{2,1,0:T(8,128)(2,1)} %pad_maximum_fusion), calls=%async_computation.1 | async-start | bytes 6815744 | tf_op jit(solution)/shard_map/all_to_all | solution.py:236
  86.9 4.6 copy-start.10
  420.8 132.5 %all-to-all-start.3 = ((bf16[4,2,2,64,512]{4,3,2,1,0:T(8,128)(2,1)}), bf16[4,2,2,64,512]{4,3,2,1,0:T(8,128)(2,1)}, u32[]{:S(2)}, u32[]{:S(2)}) async-start(bf16[4,2,2,64,512]{4,3,2,1,0:T(8,128)(2,1)} %get-tuple-element.48), calls=%async_computation.3 | async-start | bytes 2097152 | tf_op jit(solution)/shard_map/all_to_all | solution.py:2164
  553.3 6.5 copy-start.5
  555.6 8.8 %all-to-all-start.5 = ((bf16[8,32,512]{2,1,0:T(8,128)(2,1)}), bf16[8,32,512]{2,1,0:T(8,128)(2,1)S(1)}, u32[]{:S(2)}, u32[]{:S(2)}) async-start(bf16[8,32,512]{2,1,0:T(8,128)(2,1)} %bitcast.70), calls=%async_computation.5 | async-start | bytes 524288 | tf_op jit(solution)/shard_map/all_to_all | solution.py:236
  559.8 10.3 %copy-start.6 = (s32[4,1024]{0,1:T(8,128)S(1)}, s32[4,1024]{0,1:T(8,128)}, u32[]{:S(2)}) copy-start(s32[4,1024]{0,1:T(8,128)} %constant.115.clone) | copy-start | bytes 49156
  564.4 117.1 %all-to-all-start.4 = ((bf16[8,64,2048]{2,1,0:T(8,128)(2,1)}), bf16[8,64,2048]{2,1,0:T(8,128)(2,1)S(1)}, u32[]{:S(2)}, u32[]{:S(2)}) async-start(bf16[8,64,2048]{2,1,0:T(8,128)(2,1)} %bitcast.153), calls=%async_computation.4 | async-start | bytes 4194304 | tf_op jit(solution)/shard_map/all_to_all | solution.py:236
  681.5 2.4 copy-start.4
  681.5 4.4 copy-start.1
  683.8 1.5 copy-start.9

commit v7 on v6

--- a/solution.py
+++ b/solution.py
@@ -728,30 +728,30 @@
     pl.semaphore_wait(barrier, len(offsets) + extra)
 
 
-def load_highway(first_hbm, weights, project, sems):
+def load_level(first_hbm, weights, level, run, sem):
     grid = first_hbm.shape[0]
     team = team_size()
-    run = project.shape[0] // grid
 
     @pl.loop(0, team)
     def _(member):
         for block in range(grid):
-            for level in range(2):
-                pltpu.make_async_copy(
-                    first_hbm.at[
-                        block, pl.ds(pl.multiple_of((member * 2 + level) * run, run), run)
-                    ],
-                    weights.at[
-                        level, pl.ds(pl.multiple_of((member * grid + block) * run, run), run)
-                    ],
-                    sems.at[0],
-                ).start()
-
+            pltpu.make_async_copy(
+                first_hbm.at[
+                    block, pl.ds(pl.multiple_of((level * team + member) * run, run), run)
+                ],
+                weights.at[level, pl.ds(pl.multiple_of((member * grid + block) * run, run), run)],
+                sem,
+            ).start()
+
+
+def load_project(first_hbm, project, sem):
+    grid = first_hbm.shape[0]
+    run = project.shape[0] // grid
     for block in range(grid):
         pltpu.make_async_copy(
-            first_hbm.at[block, pl.ds(team * 2 * run, run)],
+            first_hbm.at[block, pl.ds(team_size() * 2 * run, run)],
             project.at[pl.ds(block * run, run)],
-            sems.at[1],
+            sem,
         ).start()
 
 
@@ -827,13 +827,9 @@
                 wait_bytes(self.blocks[piece], self.send_sem)
 
 
-def row_pieces(total, parts):
-    step = -(-total // (parts * 16)) * 16
-    return [(start, min(step, total - start)) for start in range(0, total, step)]
-
-
 def highway_kernel(
     tight_from,
+    direct,
     tiled_ref,
     filter_ref,
     count_ref,
@@ -868,6 +864,7 @@
     turned_sems,
     lstm_sems,
     lin_sems,
+    swap_sems,
 ):
     team, tokens, features = first_ref.shape
     part = features // team
@@ -876,10 +873,13 @@
     place = team_place()
     sibling = member_at(1)
     near = list(range(cores, team, cores))
-    chunks = lstm_block_hbm.shape[0]
-    greet([1] + near, True)
+    chips = team // cores
+    chunks = lstm_hbm.shape[1]
+    greet(list(range(1, team)) if direct else [1] + near, True)
     home = grid_block(0, 0)
-    places = [pl.ds(start, size) for start, size in row_pieces(block_hbm.shape[0], 8)]
+    run = project.shape[0] // first_hbm.shape[0]
+    quarter = team * run // 4
+    places = [pl.ds(k * quarter, quarter) for k in range(8)] + [pl.ds(8 * quarter, run)]
     block_gather = Gather(
         [block_hbm.at[rows] for rows in places],
         [lambda at, rows=rows: first_hbm.at[at, rows] for rows in places],
@@ -887,16 +887,54 @@
         block_sems,
     )
     turned_gather = Gather(
-        [turned_block_hbm],
+        [turned_hbm.at[home]],
         [lambda at: turned_hbm.at[at]],
         gather_send_sems.at[1],
         turned_sems,
     )
     all_places = list(range(len(places)))
-    block_gather.start(all_places)
-    pltpu.make_async_copy(block_hbm, first_hbm.at[home], load_sems.at[2]).start()
-    pltpu.make_async_copy(turned_block_hbm, turned_hbm.at[home], load_sems.at[3]).start()
-    pltpu.make_async_copy(lstm_block_hbm, lstm_hbm.at[home], load_sems.at[4]).start()
+    block_gather.start(all_places[:4])
+    pltpu.make_async_copy(block_hbm, first_hbm.at[home], load_sems.at[3]).start()
+    over_x = cores
+    over_t = lax.axis_size("x") * cores
+    across = over_t + over_x
+    x_peer = member_at(over_x)
+    if direct:
+        banks = lax.axis_size("x") * cores
+        t_index, bank = place // banks, lax.rem(place, banks)
+        each = lstm_block_hbm.shape[1] // 8
+        short = turned_block_hbm.shape[1] // 2
+
+        def routes(member):
+            for k in range(8):
+                rows = pl.ds(pl.multiple_of(bank * each, each), each)
+                yield (
+                    lstm_block_hbm.at[member, pl.ds(k * each, each)],
+                    lstm_hbm.at[home, t_index * 8 + k, rows],
+                    0,
+                )
+            for d in range(2):
+                rows = pl.ds(pl.multiple_of(bank * short, short), short)
+                yield (
+                    turned_block_hbm.at[member, pl.ds(d * short, short)],
+                    turned_hbm.at[home, t_index, d, rows],
+                    1,
+                )
+
+        def swap(offsets):
+            for offset in offsets:
+                member = member_at(offset)
+                for source, target, which in routes(member):
+                    send_block(
+                        source, target, swap_sems.at[which], swap_sems.at[2 + which], member
+                    )
+
+        swap(range(1, over_t))
+        for source, target, which in routes(place):
+            pltpu.make_async_copy(source, target, swap_sems.at[4 + which]).start()
+    else:
+        pltpu.make_async_copy(turned_block_hbm, turned_hbm.at[home], swap_sems.at[5]).start()
+        pltpu.make_async_copy(lstm_block_hbm, lstm_hbm.at[home], swap_sems.at[4]).start()
 
     def columns(member):
         return pl.ds(pl.multiple_of(member * part, part), part)
@@ -918,7 +956,6 @@
         )
 
     g, t, y, x, c = axis_sizes()
-    run = part // (g * y)
     natural = features_own[...]
     starts = [
         ((((gi * t + ti) * y + yi) * x + xi) * c + ci) * run
@@ -930,7 +967,7 @@
     ]
     features_own[...] = jnp.concatenate([natural[:, at : at + run] for at in starts], axis=1)
 
-    for offset in near + [1]:
+    for offset in (over_t, over_x, 1):
         send_block(
             features_own,
             first_ref.at[place],
@@ -939,12 +976,15 @@
             member_at(offset),
         )
     first_ref[place] = features_own[...]
-    block_gather.forward(all_places)
+    block_gather.start(all_places[4:])
+    if direct:
+        swap(range(over_t, team))
+    block_gather.forward(all_places[:4])
 
     def lstm_start(chunk):
         for dg in range(1, g_size):
             send_grid(
-                lstm_block_hbm.at[chunk],
+                lstm_hbm.at[home, chunk],
                 lstm_hbm.at[home, chunk],
                 gather_send_sems.at[2],
                 lstm_sems.at[chunk, g_size - dg, 0],
@@ -969,27 +1009,67 @@
             def _():
                 lstm_start(jnp.minimum(chunk + AHEAD, chunks - 1))
 
-    turned_gather.start([0])
-    for chunk in range(AHEAD):
+    for offset in (over_t, over_x, across):
+        member = member_at(offset)
+        block = first_ref.at[member]
+        wait_bytes(block, first_sems.at[offset])
+        if offset == over_t:
+            send_block(block, block, send_sems.at[0], first_sems.at[across], x_peer)
+        send_block(block, block, send_sems.at[0], first_sems.at[offset + 1], sibling)
+    block_gather.finish(all_places[:4])
+    wait_bytes(block_hbm, load_sems.at[3])
+    load_level(first_hbm, weights, 0, run, load_sems.at[0])
+    wait_bytes(weights.at[0], load_sems.at[0])
+
+    rows = cores * tokens
+
+    def mix(level, pair, operand):
+        mixed = (
+            jnp.dot(
+                operand.reshape(rows, features), weights[level], preferred_element_type=jnp.float32
+            )
+            + bias_ref[level : level + 1]
+        )
+        mixed_ref[level, pair] = mixed.reshape(cores, tokens, 2 * part)
+        gate = sigmoid(mixed[:, part:])
+        pre_act = mixed[:, :part]
+        return (gate, pre_act * sigmoid(pre_act))
+
+    for step in range(chips):
+        chip = member_at(step * cores) // cores
+        pair = pl.ds(chip * cores, cores)
+        wait_bytes(first_ref.at[member_at(step * cores + 1)], first_sems.at[step * cores + 1])
+        gate, act = mix(0, pair, first_ref[pair])
+        carried = first_ref[pair, :, columns(place)].astype(jnp.float32).reshape(rows, part)
+        hidden = gate * carried + (1.0 - gate) * act
+        hidden_ref[pair] = hidden.reshape(cores, tokens, part)
+        mine = second_ref.at[pair, :, columns(place)]
+        mine[...] = hidden.astype(jnp.bfloat16).reshape(cores, tokens, part)
+        for to in (over_t, over_x, 1):
+            send_block(
+                mine, mine, send_sems.at[1], second_sems.at[chip, opposite(to)], member_at(to)
+            )
+        block_gather.forward([4 + k for k in range(4 * step // chips, 4 * (step + 1) // chips)])
+
+    if direct:
+        wait_bytes(lstm_block_hbm.at[pl.ds(0, team - 1)], swap_sems.at[2])
+        wait_bytes(turned_block_hbm.at[pl.ds(0, team - 1)], swap_sems.at[3])
+        wait_bytes(lstm_block_hbm.at[0], swap_sems.at[4])
+        wait_bytes(turned_block_hbm.at[0], swap_sems.at[5])
+    else:
+        wait_bytes(lstm_block_hbm, swap_sems.at[4])
+        wait_bytes(turned_block_hbm, swap_sems.at[5])
+    for chunk in range(min(AHEAD, chunks)):
         lstm_start(chunk)
-    for offset in near:
-        member = member_at(offset)
-        wait_bytes(first_ref.at[member], first_sems.at[offset])
-        send_block(
-            first_ref.at[member],
-            first_ref.at[member],
-            send_sems.at[0],
-            first_sems.at[offset + 1],
-            sibling,
-        )
-    block_gather.finish(all_places)
-    wait_bytes(block_hbm, load_sems.at[2])
-    load_highway(first_hbm, weights, project, load_sems)
+    block_gather.forward(all_places[8:])
+    block_gather.finish(all_places[4:])
+    load_level(first_hbm, weights, 1, run, load_sems.at[1])
+    load_project(first_hbm, project, load_sems.at[2])
 
     @pl.loop(0, chunks)
     def _(chunk):
         send_grid(
-            lstm_block_hbm.at[chunk],
+            lstm_hbm.at[home, chunk],
             lstm_hbm.at[home, chunk],
             gather_send_sems.at[4],
             lstm_sems.at[chunk, 0, 1],
@@ -997,87 +1077,63 @@
             1,
         )
 
-    wait_bytes(weights, load_sems.at[0])
-    wait_bytes(project, load_sems.at[1])
-
-    def mix(level, member, operand):
-        mixed = (
-            jnp.dot(operand, weights[level], preferred_element_type=jnp.float32)
-            + bias_ref[level : level + 1]
-        )
-        mixed_ref[level, member] = mixed
-        gate = sigmoid(mixed[:, part:])
-        pre_act = mixed[:, :part]
-        return (gate, pre_act * sigmoid(pre_act))
-
-    @pl.loop(0, team)
-    def _(offset):
-        member = member_at(offset)
-
-        @pl.when(lax.rem(offset, cores) == 1)
-        def _():
-            wait_bytes(first_ref.at[member], first_sems.at[offset])
-
-        gate, act = mix(0, member, first_ref[member])
-        carried = first_ref[member, :, columns(place)].astype(jnp.float32)
-        hidden = gate * carried + (1.0 - gate) * act
-        hidden_ref[member] = hidden
-        mine = second_ref.at[member, :, columns(place)]
-        mine[...] = hidden.astype(jnp.bfloat16)
-        for to in near + [1]:
-            send_block(
-                mine,
-                mine,
-                send_sems.at[1],
-                second_sems.at[member, opposite(to)],
-                member_at(to),
+    wait_bytes(weights.at[1], load_sems.at[1])
+    wait_bytes(project, load_sems.at[2])
+    x_size, t_size = lax.axis_size("x"), lax.axis_size("t")
+
+    def ordered_chip(step):
+        t_at = lax.rem(lax.axis_index("t") + step // x_size, t_size)
+        return t_at * x_size + step % x_size
+
+    for step in range(chips + 1):
+        if step < chips:
+            chip = ordered_chip(step)
+            pair = pl.ds(chip * cores, cores)
+            for origin in (over_t, over_x, across):
+                piece = second_ref.at[pair, :, columns(member_at(origin))]
+                wait_bytes(piece, second_sems.at[chip, origin])
+                if origin == over_t:
+                    send_block(
+                        piece, piece, send_sems.at[1], second_sems.at[chip, across], x_peer
+                    )
+                send_block(
+                    piece, piece, send_sems.at[1], second_sems.at[chip, origin + 1], sibling
+                )
+        if step > 0:
+            chip = ordered_chip(step - 1)
+            pair = pl.ds(chip * cores, cores)
+            for origin in [0] + near:
+                piece = second_ref.at[pair, :, columns(member_at(origin + 1))]
+                wait_bytes(piece, second_sems.at[chip, origin + 1])
+            gate, act = mix(1, pair, second_ref[pair])
+            carried = hidden_ref[pair].reshape(rows, part)
+            top = (gate * carried + (1.0 - gate) * act).astype(jnp.bfloat16)
+            top_ref[pair] = top.reshape(cores, tokens, part)
+            parts[pair] = (
+                jnp.dot(top, project[...], preferred_element_type=jnp.float32)
+                .astype(jnp.bfloat16)
+                .reshape(cores, tokens, -1)
             )
-
-        pump(offset)
-
-    @pl.loop(0, team + 1)
-    def _(step):
-        @pl.when(step < team)
-        def _():
-            member = member_at(jnp.minimum(step, team - 1))
-            for origin in near:
-                piece = second_ref.at[member, :, columns(member_at(origin))]
-                wait_bytes(piece, second_sems.at[member, origin])
-                send_block(
-                    piece,
-                    piece,
-                    send_sems.at[1],
-                    second_sems.at[member, origin + 1],
-                    sibling,
-                )
-
-        @pl.when(step > 0)
-        def _():
-            member = member_at(jnp.maximum(step - 1, 0))
-            for origin in [0] + near:
-                piece = second_ref.at[member, :, columns(member_at(origin + 1))]
-                wait_bytes(piece, second_sems.at[member, origin + 1])
-            gate, act = mix(1, member, second_ref[member])
-            top = (gate * hidden_ref[member] + (1.0 - gate) * act).astype(jnp.bfloat16)
-            top_ref[member] = top
-            parts[member] = jnp.dot(
-                top, project[...], preferred_element_type=jnp.float32
-            ).astype(jnp.bfloat16)
-
-            @pl.when(step > 1)
-            def _():
-                send_block(
-                    parts.at[member],
-                    parts_recv.at[place],
-                    lin_sems.at[0],
-                    lin_sems.at[1],
-                    member,
-                )
-
-        pump(team + step)
-
+            for core in range(cores):
+                member = chip * cores + core
+
+                @pl.when(member != place)
+                def _():
+                    send_block(
+                        parts.at[member],
+                        parts_recv.at[place],
+                        lin_sems.at[0],
+                        lin_sems.at[1],
+                        member,
+                    )
+
+            pump(step - 1)
+
+    turned_gather.start([0])
     parts_recv[place] = parts[place]
     others = pl.ds(0, team - 1)
+    pump(chips)
+    pump(chips + 1)
     wait_bytes(parts_recv.at[others], lin_sems.at[1])
     lin = jnp.sum(parts_recv[...].astype(jnp.float32), axis=0) + lin_bias_ref[...]
     lin_ref[place] = lin.astype(jnp.bfloat16)
@@ -1090,7 +1146,7 @@
             member_at(offset),
         )
 
-    @pl.loop(2 * team + 1, max(chunks, 2 * team + 1))
+    @pl.loop(chips + 2, chunks)
     def _(chunk):
         pump(chunk)
 
@@ -1111,15 +1167,16 @@
     block_gather.sent(all_places)
     turned_gather.sent([0])
     for _ in range(g_size - 1):
-        wait_bytes(lstm_block_hbm, gather_send_sems.at[2])
-        wait_bytes(lstm_block_hbm, gather_send_sems.at[3])
-    wait_bytes(lstm_block_hbm, gather_send_sems.at[4])
-    wait_bytes(turned_block_hbm, load_sems.at[3])
-    wait_bytes(lstm_block_hbm, load_sems.at[4])
+        wait_bytes(lstm_hbm.at[0], gather_send_sems.at[2])
+        wait_bytes(lstm_hbm.at[0], gather_send_sems.at[3])
+    wait_bytes(lstm_hbm.at[0], gather_send_sems.at[4])
+    if direct:
+        wait_bytes(lstm_block_hbm.at[pl.ds(0, team - 1)], swap_sems.at[0])
+        wait_bytes(turned_block_hbm.at[pl.ds(0, team - 1)], swap_sems.at[1])
 
 
 def run_highway(
-    tight_from, tiled, filters, counts, block, lstm_block, turned_block, bias, lin_bias
+    tight_from, direct, tiled, filters, counts, block, lstm_block, turned_block, bias, lin_bias
 ):
     team = team_size()
     tokens, features = tiled.shape[0], filters.shape[1]
@@ -1130,17 +1187,24 @@
     bf16, f32 = jnp.bfloat16, jnp.float32
     vmem = pl.BlockSpec(memory_space=pltpu.VMEM)
     hbm = pl.BlockSpec(memory_space=pl.ANY)
-    pieces = len(row_pieces(block.shape[0], 8))
+    pieces = 9
+    if direct:
+        banks = lax.axis_size("x") * lax.axis_size("c")
+        halves = lax.axis_size("t")
+        lstm_shape = (8 * halves, banks * lstm_block.shape[1] // 8, lstm_block.shape[2])
+        turned_shape = (halves, 2, banks * turned_block.shape[1] // 2, turned_block.shape[2])
+    else:
+        lstm_shape, turned_shape = lstm_block.shape, turned_block.shape
     token_block = math.gcd(tokens, TOKEN_BLOCK)
     return pl.pallas_call(
-        partial(highway_kernel, tight_from),
+        partial(highway_kernel, tight_from, direct),
         in_specs=[vmem] * 3 + [hbm] * 3 + [vmem] * 2,
         out_specs=[vmem] + [hbm] * 3 + [vmem] * 6,
         out_shape=[
             jax.ShapeDtypeStruct((tokens, features), f32),
             jax.ShapeDtypeStruct((grid,) + block.shape, bf16),
-            jax.ShapeDtypeStruct((grid,) + lstm_block.shape, bf16),
-            jax.ShapeDtypeStruct((grid,) + turned_block.shape, bf16),
+            jax.ShapeDtypeStruct((grid,) + lstm_shape, bf16),
+            jax.ShapeDtypeStruct((grid,) + turned_shape, bf16),
             jax.ShapeDtypeStruct((team, tokens, features), bf16),
             jax.ShapeDtypeStruct((team, tokens, features), bf16),
             jax.ShapeDtypeStruct((2, team, tokens, 2 * part), f32),
@@ -1159,12 +1223,13 @@
             pltpu.SemaphoreType.DMA((5,)),
             pltpu.SemaphoreType.DMA((2,)),
             pltpu.SemaphoreType.DMA((team,)),
-            pltpu.SemaphoreType.DMA((team, team)),
+            pltpu.SemaphoreType.DMA((team // lax.axis_size("c"), team)),
             pltpu.SemaphoreType.DMA((5,)),
             pltpu.SemaphoreType.DMA((pieces, g_size, y_size)),
             pltpu.SemaphoreType.DMA((1, g_size, y_size)),
-            pltpu.SemaphoreType.DMA((lstm_block.shape[0], g_size, y_size)),
+            pltpu.SemaphoreType.DMA((lstm_shape[0], g_size, y_size)),
             pltpu.SemaphoreType.DMA((4,)),
+            pltpu.SemaphoreType.DMA((6,)),
         ],
         compiler_params=pltpu.CompilerParams(
             collective_id=2, has_side_effects=True, vmem_limit_bytes=60 * 1024 * 1024
@@ -1228,7 +1293,9 @@
     place = team_place()
     sibling = member_at(1)
     near = list(range(1, chips))
-    load_highway(first_hbm, weights, project, load_sems)
+    for level in range(2):
+        load_level(first_hbm, weights, level, run, load_sems.at[level])
+    load_project(first_hbm, project, load_sems.at[2])
     greet([1] + [chip * cores for chip in near], True)
     f32, bf16 = jnp.float32, jnp.bfloat16
     g_size, y_size = lax.axis_size("g"), lax.axis_size("y")
@@ -1279,8 +1346,9 @@
     def opposite_chip(chip):
         return opposite(chip * cores) // cores
 
-    wait_bytes(weights, load_sems.at[0])
-    wait_bytes(project, load_sems.at[1])
+    for level in range(2):
+        wait_bytes(weights.at[level], load_sems.at[level])
+    wait_bytes(project, load_sems.at[2])
 
     def mix_grads(level, member, grad, carried):
         pre_act = mixed_ref[level, member, :, pl.ds(0, part)]
@@ -1511,7 +1579,7 @@
             pltpu.VMEM((chips - 1, tokens, features), bf16),
             pltpu.VMEM((tokens, features), f32),
             pltpu.VMEM((2, part, width), bf16),
-            pltpu.SemaphoreType.DMA((2,)),
+            pltpu.SemaphoreType.DMA((3,)),
             pltpu.SemaphoreType.DMA((4,)),
             pltpu.SemaphoreType.DMA((team,)),
             pltpu.SemaphoreType.DMA((team, chips - 1)),
@@ -2093,26 +2161,21 @@
     highway_slices = team_first(highway_weight.reshape(2 * highway_rows, -1))
     turned_rows = lstm_proj.shape[2]
     gate_slices = lstm_weight.reshape(2, lstm_rows, 4, team, cells).transpose(3, 0, 2, 1, 4)
-    swapped = swap_team(
-        jnp.concatenate(
-            [
-                highway_slices.reshape(team, 2 * highway_rows, 2 * part),
-                gate_slices.reshape(team, 8 * lstm_rows, cells),
-                team_slices(jnp.swapaxes(lstm_proj, 1, 2), 1),
-            ],
-            axis=1,
+    swapped = swap_team(highway_slices.reshape(team, 2 * highway_rows, 2 * part))
+    block = swapped.reshape(team, 2, highway_rows, 2 * part).transpose(1, 0, 2, 3)
+    block = jnp.concatenate([block.reshape(-1, 2 * part), proj_weight], axis=0)
+    t, x, c = lax.axis_size("t"), lax.axis_size("x"), lax.axis_size("c")
+    lstm_block = gate_slices.reshape(team, 8 * lstm_rows, cells)
+    turned_block = team_slices(jnp.swapaxes(lstm_proj, 1, 2), 1)
+    direct = lstm_rows % 16 == 0 and turned_rows % 16 == 0
+    if not direct:
+        lstm_block = (
+            swap_team(lstm_block)
+            .reshape(t, x * c, 8, lstm_rows, cells)
+            .transpose(0, 2, 1, 3, 4)
+            .reshape(t * 8, x * c * lstm_rows, cells)
         )
-    )
-    ends = [2 * highway_rows, 2 * highway_rows + 8 * lstm_rows]
-    block = jnp.concatenate([swapped[:, : ends[0]].reshape(-1, 2 * part), proj_weight], axis=0)
-    t, x, c = lax.axis_size("t"), lax.axis_size("x"), lax.axis_size("c")
-    lstm_block = (
-        swapped[:, ends[0] : ends[1]]
-        .reshape(t, x * c, 8, lstm_rows, cells)
-        .transpose(0, 2, 1, 3, 4)
-        .reshape(t * 8, x * c * lstm_rows, cells)
-    )
-    turned_block = run_rows(swapped[:, ends[1] :])
+        turned_block = run_rows(swap_team(turned_block))
     cut_rows = team * 2 * highway_rows
     grid = lax.axis_size("g") * lax.axis_size("y")
     bank = lax.axis_index("x") * lax.axis_size("c") + lax.axis_index("c")
@@ -2136,6 +2199,7 @@
         lin_all,
     ) = run_highway(
         tight_from,
+        direct,
         tiled,
         filters,
         counts,

time: 694 us -> 685 us (0.987)
  waiting for transfers between devices: 34.1 us -> 21.8 us
    all_to_all x3, waiting for transfers between devices: 29.9 us -> 10.9 us  [swap_team(): return lax.all_to_all(values, TEAM, split_axis=0, concat_axis=0, tiled=True)]
    all_to_all x1, waiting for transfers between devices: 0.01 us -> 10.9 us  [shards(): lax.all_to_all(jnp.broadcast_to(conv_own[None], (banks,) + conv_own.shape...]
    pallas_call x1, Pallas kernels: 193 us -> 200 us  [run_highway(): pl.pallas_call(partial(highway_kernel, tight_from, direct), in_specs=[vme...]
where the time goes in v7:
time: 685 us; the launch traced here: 676 us
  Pallas kernels  561 us (82%)
  local copies, waits for them, and re-layouts  43.3 us (6%)
  starting transfers between devices  34.7 us (5%)
  waiting for transfers between devices  21.8 us (3%)
  other arithmetic  10.1 us (1%)
    pallas_call x1, Pallas kernels, run_highway(): pl.pallas_call(partial(highway_kernel, tight_from, direct), in_specs=[vme...  200 us
    pallas_call x1, Pallas kernels, run_lstm(): pl.pallas_call(partial(lstm_kernel, team), in_specs=[vmem, vmem, hbm, hbm...  134 us
    pallas_call x1, Pallas kernels, run_highway_back(): pl.pallas_call(highway_back_kernel, in_specs=[vmem, hbm] + [vmem] * 5 + [...  129 us
    pallas_call x1, Pallas kernels, run_final(): pl.pallas_call(partial(final_kernel, tight_from, bank_counts), in_specs=[...  95.8 us
    all_to_all x3, starting transfers between devices, swap_team(): return lax.all_to_all(values, TEAM, split_axis=0, concat_axis=0, tiled=True)  14.5 us
  transfers between devices with their start and end apart: 6, of which 3 were waited for; matrix products, arithmetic and copies ran while one was open for 7% of the time, Pallas kernels for 33%

profile of v7, /device:TPU:14, one launch (start us, length us, event | category | flops | bytes accessed | tf_op | source)
XLA Modules:
  0.0 675.8 jit_solution(3724069628965959270)
XLA Ops:
  6.4 6.0 all-to-all-start.2
  12.8 2.3 reshape_reshape.21
  15.1 4.3 copy.158
  19.5 2.4 copy.190
  21.9 2.5 copy.161
  26.1 3.3 convolution_convert_fusion
  31.2 4.0 all-to-all-start
  36.4 10.9 %all-to-all-done = bf16[4,113,1024]{2,1,0:T(8,128)(2,1)S(1)} async-done(((bf16[4,113,1024]{2,1,0:T(8,128)(2,1)}), bf16[4,113,1024]{2,1,0:T(8,128)(2,1)S(1)}, u32[]{:S(2)}, u32[]{:S(2)}) %all-to-all-start) | async-done | bytes 925728 | tf_op jit(solution)/shard_map/all_to_all | solution.py:2119
  47.3 5.4 all-to-all-start.1
  57.9 7.8 %all-to-all-done.1 = bf16[8,128,512]{1,2,0:T(8,128)(2,1)S(1)} async-done(((bf16[8,128,512]{1,2,0:T(8,128)(2,1)}), bf16[8,128,512]{1,2,0:T(8,128)(2,1)S(1)}, u32[]{:S(2)}, u32[]{:S(2)}) %all-to-all-start.1) | async-done | bytes 1048608 | tf_op jit(solution)/shard_map/all_to_all | solution.py:236
  67.3 199.9 %highway_team.1 = (f32[128,2048]{1,0:T(8,128)}, bf16[4,1088,512]{2,1,0:T(8,128)(2,1)}, bf16[4,16,128,512]{3,2,1,0:T(8,128)(2,1)}, bf16[4,2,2,64,512]{4,3,2,1,0:T...) custom-call(bf16[128,64,128]{2,1,0:T(8,128)(2,1)} %bitcast.146, ...), custom_call_target="tpu_custom_call" | custom-call | tf_op jit(solution)/shard_map/highway_team/pallas_call | solution.py:1199
  267.3 134.2 %lstm_team.1 = (bf16[8,4,32,512]{3,2,1,0:T(8,128)(2,1)}, bf16[4,2,2,128,2048]{4,3,2,1,0:T(8,128)(2,1)}, bf16[4,2,2,64,512]{4,3,2,1,0:T(8,128)(2,1)}, f32[2,8,2048]{2,1,0:T(8,128)}) custom-call(bf16[8,4,32,512]{3,2,1,0:T(8,128)(2,1)} %bitcast.165, bf16[2,4,32,512]{3,2,1,0:T(8,128)(2,1)} %bitcast.167, bf16[4,2,2,4,128,512]{5,4,3,2,1,0:T(8,128)(2,1)} %bitcast.145, ...), custom_call_target="tpu_custom_call" | custom-call | tf_op jit(solution)/shard_map/lstm_team/pallas_call | solution.py:646
  401.5 10.2 %all-to-all-start.3 = ((bf16[4,2,2,64,512]{4,3,2,1,0:T(8,128)(2,1)}), bf16[4,2,2,64,512]{4,3,2,1,0:T(8,128)(2,1)}, u32[]{:S(2)}, u32[]{:S(2)}) async-start(bf16[4,2,2,64,512]{4,3,2,1,0:T(8,128)(2,1)} %get-tuple-element.48), calls=%async_computation.3 | async-start | bytes 2097152 | tf_op jit(solution)/shard_map/all_to_all | solution.py:2228
  411.7 128.6 %highway_team_back.1 = (bf16[128,2048]{1,0:T(8,128)(2,1)}, bf16[4,1088,512]{2,1,0:T(8,128)(2,1)}, f32[2,8,512]{2,1,0:T(8,128)}, bf16[8,64,2048]{2,1,0:T(8,128)(2,1)}) custom-call(bf16[8,128,512]{2,1,0:T(8,128)(2,1)} %bitcast.158, bf16[4,1088,512]{2,1,0:T(8,128)(2,1)} %get-tuple-element.39.first_hbm, bf16[8,128,2048]{2,1,0:T(8,128)(2,1)} %get-tuple-element.40.first_ref, ...), custom_call_target="tpu_custom_call" | custom-call | tf_op jit(solution)/shard_map/highway_team_back/pallas_call | solution.py:1550
  540.3 1.6 reduce_sum.12
  542.6 4.2 all-to-all-start.5
  546.8 1.5 copy.178
  548.3 3.2 all-to-all-done.5
  551.4 5.0 all-to-all-start.4
  561.7 95.8 %final_sums.1 = (f32[128,4096]{1,0:T(8,128)}, f32[64,512]{1,0:T(8,128)}, f32[16,128]{1,0:T(8,128)}, f32[1024,128]{1,0:T(8,128)}, f32[384,128]{1,0:T(8,128)}) custom-call(bf16[4,1088,512]{2,1,0:T(8,128)(2,1)} %get-tuple-element.46.grads_ref, bf16[128,64,128]{2,1,0:T(8,128)(2,1)} %bitcast.147, s32[8,1024]{1,0:T(8,128)} %reshape.225.ids_ref, ...), custom_call_target="tpu_custom_call" | custom-call | tf_op jit(solution)/shard_map/final_sums/pallas_call | solution.py:1949
  659.5 2.0 slice_select_fusion.1
  661.5 2.0 copy.177
  664.7 1.8 copy.182
  671.2 2.3 pack_columns.1
  (150 shorter events, 33.4 us)
Async XLA Ops:
  0.6 11.9 %copy-start = (s32[128,4,50]{0,1,2:T(4,128)S(1)}, s32[128,4,50]{0,1,2:T(4,128)}, u32[]{:S(2)}) copy-start(s32[128,4,50]{0,1,2:T(4,128)} %param.14) | copy-start | bytes 307204
  0.7 12.2 %copy-start.6 = (bf16[2,64,4096]{2,1,0:T(8,128)(2,1)S(1)}, bf16[2,64,4096]{2,1,0:T(8,128)(2,1)}, u32[]{:S(2)}) copy-start(bf16[2,64,4096]{2,1,0:T(8,128)(2,1)} %param.20) | copy-start | bytes 3145732
  6.4 23.6 %all-to-all-start.2 = ((bf16[32,2,712]{2,1,0:T(2,128)(2,1)}), bf16[32,2,712]{2,1,0:T(2,128)(2,1)S(1)}, u32[]{:S(2)}, u32[]{:S(2)}) async-start(bf16[32,2,712]{2,1,0:T(2,128)(2,1)} %reshape.251), calls=%async_computation.2 | async-start | bytes 196608 | tf_op jit(solution)/shard_map/all_to_all | solution.py:2137
  21.8 2.5 copy-start.7
  21.8 3.4 copy-start.8
  21.8 4.3 copy-start.12
  26.1 3.9 copy-start.9
  26.1 3.9 copy-start.13
  31.2 16.1 %all-to-all-start = ((bf16[4,113,1024]{2,1,0:T(8,128)(2,1)}), bf16[4,113,1024]{2,1,0:T(8,128)(2,1)S(1)}, u32[]{:S(2)}, u32[]{:S(2)}) async-start(bf16[4,113,1024]{2,1,0:T(8,128)(2,1)} %broadcast_in_dim.69), calls=%async_computation | async-start | bytes 1966080 | tf_op jit(solution)/shard_map/all_to_all | solution.py:2119
  47.3 18.3 %all-to-all-start.1 = ((bf16[8,128,512]{1,2,0:T(8,128)(2,1)}), bf16[8,128,512]{1,2,0:T(8,128)(2,1)S(1)}, u32[]{:S(2)}, u32[]{:S(2)}) async-start(bf16[8,128,512]{1,2,0:T(8,128)(2,1)} %bitcast.18), calls=%async_computation.1 | async-start | bytes 2097152 | tf_op jit(solution)/shard_map/all_to_all | solution.py:236
  57.9 8.4 %copy-start.11 = (bf16[64,512]{1,0:T(8,128)(2,1)S(1)}, bf16[64,512]{1,0:T(8,128)(2,1)}, u32[]{:S(2)}) copy-start(bf16[64,512]{1,0:T(8,128)(2,1)} %param.22) | copy-start | bytes 196612
  401.5 138.8 %all-to-all-start.3 = ((bf16[4,2,2,64,512]{4,3,2,1,0:T(8,128)(2,1)}), bf16[4,2,2,64,512]{4,3,2,1,0:T(8,128)(2,1)}, u32[]{:S(2)}, u32[]{:S(2)}) async-start(bf16[4,2,2,64,512]{4,3,2,1,0:T(8,128)(2,1)} %get-tuple-element.48), calls=%async_computation.3 | async-start | bytes 2097152 | tf_op jit(solution)/shard_map/all_to_all | solution.py:2228
  540.3 6.5 copy-start.3
  542.6 8.8 %all-to-all-start.5 = ((bf16[8,32,512]{2,1,0:T(8,128)(2,1)}), bf16[8,32,512]{2,1,0:T(8,128)(2,1)S(1)}, u32[]{:S(2)}, u32[]{:S(2)}) async-start(bf16[8,32,512]{2,1,0:T(8,128)(2,1)} %bitcast.66), calls=%async_computation.5 | async-start | bytes 524288 | tf_op jit(solution)/shard_map/all_to_all | solution.py:236
  548.3 8.8 %copy-start.4 = (s32[4,1024]{0,1:T(8,128)S(1)}, s32[4,1024]{0,1:T(8,128)}, u32[]{:S(2)}) copy-start(s32[4,1024]{0,1:T(8,128)} %constant.115.clone) | copy-start | bytes 49156
  551.4 119.8 %all-to-all-start.4 = ((bf16[8,64,2048]{2,1,0:T(8,128)(2,1)}), bf16[8,64,2048]{2,1,0:T(8,128)(2,1)S(1)}, u32[]{:S(2)}, u32[]{:S(2)}) async-start(bf16[8,64,2048]{2,1,0:T(8,128)(2,1)} %bitcast.148), calls=%async_computation.4 | async-start | bytes 4194304 | tf_op jit(solution)/shard_map/all_to_all | solution.py:236
  657.5 6.0 copy-start.5
  671.2 2.4 copy-start.2
  673.5 1.5 copy-start.10
  673.5 2.1 copy-start.1

commit v8 on v7

--- a/solution.py
+++ b/solution.py
@@ -1994,12 +1994,12 @@
     for member in range(team):
         for part in range(parts):
             out_ref[:, pl.ds((part * team + member) * each, each)] = received_ref[
-                member, :, pl.ds(part * each, each)
+                member, pl.ds(0, out_ref.shape[0]), pl.ds(part * each, each)
             ].astype(jnp.float32)
 
 
-def pack_columns(received, parts):
-    team, rows, lanes = received.shape
+def pack_columns(received, parts, rows):
+    team, _, lanes = received.shape
     return pl.pallas_call(
         partial(pack_kernel, parts),
         in_specs=[pl.BlockSpec(memory_space=pltpu.VMEM)],
@@ -2240,9 +2240,15 @@
         lstm_grads.reshape(grid, 8, -1, 4 * cells),
     )
     lstm_summed = lstm_summed.reshape(t, 2, -1, 4 * cells)
-    turned_summed, grad_features = lax.optimization_barrier((turned_summed, grad_features))
-    turned_grad = whole_columns(swap_team(member_rows(turned_summed)), 1).astype(f32)
-    lstm_proj_grad = jnp.swapaxes(turned_grad, 1, 2)
+    lstm_returned = swap_team(
+        jnp.concatenate(
+            [
+                member_rows(lstm_summed),
+                member_rows(turned_summed).reshape(team, -1, 4 * cells),
+            ],
+            axis=1,
+        )
+    )
     g, t, y, x, c = axis_sizes()
 
     def own_place(values, parts):
@@ -2281,8 +2287,9 @@
         padded_rows(biases, bias_rows).astype(bf16),
         2 * highway_rows,
     )
-    lstm_returned = swap_team(member_rows(lstm_summed))
-    lstm_weight_grad = pack_columns(lstm_returned, 4).reshape(2, lstm_rows, -1)
+    lstm_weight_grad = pack_columns(lstm_returned, 4, 2 * lstm_rows).reshape(2, lstm_rows, -1)
+    turned_back = lstm_returned[:, 2 * lstm_rows :].reshape(team, 2 * turned_rows, cells)
+    lstm_proj_grad = jnp.swapaxes(whole_columns(turned_back, 1).astype(f32), 1, 2)
     highway_weight_grad = highway_weight_grad.reshape(2, highway_rows, -1)
     mine_biases = mine.reshape(-1)
     ends = [2 * lstm_bias.shape[1], 2 * lstm_bias.shape[1] + 2 * highway_bias.shape[1]]

time: 685 us -> 691 us (level)
  Pallas kernels: 561 us -> 570 us
    pallas_call x1, Pallas kernels: 95.8 us -> 105 us  [run_final(): pl.pallas_call(partial(final_kernel, tight_from, bank_counts), in_specs=[...]
    all_to_all x3 -> x2, starting transfers between devices: 14.5 us -> 9.95 us  [swap_team(): return lax.all_to_all(values, TEAM, split_axis=0, concat_axis=0, tiled=True)]
  transfers between devices with their start and end apart: 6 -> 5, of which waited for: 3 -> 2; matrix products, arithmetic and copies ran while one was open for 7% -> 7% of each run, Pallas kernels for 33% -> 34%
where the time goes in v8:
time: 691 us; the launch traced here: 681 us
  Pallas kernels  570 us (82%)
  local copies, waits for them, and re-layouts  45.3 us (7%)
  starting transfers between devices  30.1 us (4%)
  waiting for transfers between devices  18.7 us (3%)
  other arithmetic  11.4 us (2%)
    pallas_call x1, Pallas kernels, run_highway(): pl.pallas_call(partial(highway_kernel, tight_from, direct), in_specs=[vme...  200 us
    pallas_call x1, Pallas kernels, run_lstm(): pl.pallas_call(partial(lstm_kernel, team), in_specs=[vmem, vmem, hbm, hbm...  134 us
    pallas_call x1, Pallas kernels, run_highway_back(): pl.pallas_call(highway_back_kernel, in_specs=[vmem, hbm] + [vmem] * 5 + [...  128 us
    pallas_call x1, Pallas kernels, run_final(): pl.pallas_call(partial(final_kernel, tight_from, bank_counts), in_specs=[...  105 us
  transfers between devices with their start and end apart: 5, of which 2 were waited for; matrix products, arithmetic and copies ran while one was open for 7% of the time, Pallas kernels for 34%

profile of v8, /device:TPU:14, one launch (start us, length us, event | category | flops | bytes accessed | tf_op | source)
XLA Modules:
  0.0 680.6 jit_solution(14165930987746576574)
XLA Ops:
  2.3 1.4 concatenate.37
  6.4 6.0 all-to-all-start.2
  12.7 4.4 reshape_reshape.25
  17.2 4.3 copy.161
  21.5 2.4 copy.193
  23.9 2.5 copy.164
  28.2 3.3 convolution_convert_fusion
  33.3 4.0 all-to-all-start
  38.5 10.9 %all-to-all-done = bf16[4,113,1024]{2,1,0:T(8,128)(2,1)S(1)} async-done(((bf16[4,113,1024]{2,1,0:T(8,128)(2,1)}), bf16[4,113,1024]{2,1,0:T(8,128)(2,1)S(1)}, u32[]{:S(2)}, u32[]{:S(2)}) %all-to-all-start) | async-done | bytes 925728 | tf_op jit(solution)/shard_map/all_to_all | solution.py:2119
  49.4 5.4 all-to-all-start.1
  60.0 7.8 %all-to-all-done.1 = bf16[8,128,512]{1,2,0:T(8,128)(2,1)S(1)} async-done(((bf16[8,128,512]{1,2,0:T(8,128)(2,1)}), bf16[8,128,512]{1,2,0:T(8,128)(2,1)S(1)}, u32[]{:S(2)}, u32[]{:S(2)}) %all-to-all-start.1) | async-done | bytes 1048608 | tf_op jit(solution)/shard_map/all_to_all | solution.py:236
  69.4 200.0 %highway_team.1 = (f32[128,2048]{1,0:T(8,128)}, bf16[4,1088,512]{2,1,0:T(8,128)(2,1)}, bf16[4,16,128,512]{3,2,1,0:T(8,128)(2,1)}, bf16[4,2,2,64,512]{4,3,2,1,0:T...) custom-call(bf16[128,64,128]{2,1,0:T(8,128)(2,1)} %bitcast.144, ...), custom_call_target="tpu_custom_call" | custom-call | tf_op jit(solution)/shard_map/highway_team/pallas_call | solution.py:1199
  269.4 134.3 %lstm_team.1 = (bf16[8,4,32,512]{3,2,1,0:T(8,128)(2,1)}, bf16[4,2,2,128,2048]{4,3,2,1,0:T(8,128)(2,1)}, bf16[4,2,2,64,512]{4,3,2,1,0:T(8,128)(2,1)}, f32[2,8,2048]{2,1,0:T(8,128)}) custom-call(bf16[8,4,32,512]{3,2,1,0:T(8,128)(2,1)} %bitcast.164, bf16[2,4,32,512]{3,2,1,0:T(8,128)(2,1)} %bitcast.166, bf16[4,2,2,4,128,512]{5,4,3,2,1,0:T(8,128)(2,1)} %bitcast.143, ...), custom_call_target="tpu_custom_call" | custom-call | tf_op jit(solution)/shard_map/lstm_team/pallas_call | solution.py:646
  403.8 10.1 %all-to-all-start.3 = ((bf16[4,2,2,64,512]{4,3,2,1,0:T(8,128)(2,1)}), bf16[4,2,2,64,512]{4,3,2,1,0:T(8,128)(2,1)}, u32[]{:S(2)}, u32[]{:S(2)}) async-start(bf16[4,2,2,64,512]{4,3,2,1,0:T(8,128)(2,1)} %get-tuple-element.55), calls=%async_computation.3 | async-start | bytes 2097152 | tf_op jit(solution)/shard_map/all_to_all | solution.py:2228
  413.9 128.5 %highway_team_back.1 = (bf16[128,2048]{1,0:T(8,128)(2,1)}, bf16[4,1088,512]{2,1,0:T(8,128)(2,1)}, f32[2,8,512]{2,1,0:T(8,128)}, bf16[8,64,2048]{2,1,0:T(8,128)(2,1)}) custom-call(bf16[8,128,512]{2,1,0:T(8,128)(2,1)} %bitcast.157, bf16[4,1088,512]{2,1,0:T(8,128)(2,1)} %get-tuple-element.37.first_hbm, bf16[8,128,2048]{2,1,0:T(8,128)(2,1)} %get-tuple-element.38.first_ref, ...), custom_call_target="tpu_custom_call" | custom-call | tf_op jit(solution)/shard_map/highway_team_back/pallas_call | solution.py:1550
  542.4 1.7 copy.181
  544.2 1.4 reduce_sum.12
  545.8 1.6 pad_maximum_fusion
  547.3 4.6 all-to-all-start.4
  557.3 104.8 %final_sums.1 = (f32[128,4096]{1,0:T(8,128)}, f32[64,512]{1,0:T(8,128)}, f32[16,128]{1,0:T(8,128)}, f32[1024,128]{1,0:T(8,128)}, f32[384,128]{1,0:T(8,128)}) custom-call(bf16[4,1088,512]{2,1,0:T(8,128)(2,1)} %get-tuple-element.44.grads_ref, bf16[128,64,128]{2,1,0:T(8,128)(2,1)} %bitcast.145, s32[8,1024]{1,0:T(8,128)} %reshape.221.ids_ref, ...), custom_call_target="tpu_custom_call" | custom-call | tf_op jit(solution)/shard_map/final_sums/pallas_call | solution.py:1949
  664.1 2.0 slice_select_fusion.1
  666.1 2.0 copy.180
  669.3 1.8 copy.185
  675.9 2.3 pack_columns.1
  (147 shorter events, 31.5 us)
Async XLA Ops:
  0.6 11.8 %copy-start = (s32[128,4,50]{0,1,2:T(4,128)S(1)}, s32[128,4,50]{0,1,2:T(4,128)}, u32[]{:S(2)}) copy-start(s32[128,4,50]{0,1,2:T(4,128)} %param.14) | copy-start | bytes 307204
  6.4 25.8 %all-to-all-start.2 = ((bf16[32,2,712]{2,1,0:T(2,128)(2,1)}), bf16[32,2,712]{2,1,0:T(2,128)(2,1)S(1)}, u32[]{:S(2)}, u32[]{:S(2)}) async-start(bf16[32,2,712]{2,1,0:T(2,128)(2,1)} %reshape.246), calls=%async_computation.2 | async-start | bytes 196608 | tf_op jit(solution)/shard_map/all_to_all | solution.py:2137
  23.9 2.5 copy-start.5
  23.9 3.4 copy-start.6
  23.9 4.3 copy-start.10
  28.2 3.9 copy-start.7
  28.2 3.9 copy-start.11
  33.3 16.1 %all-to-all-start = ((bf16[4,113,1024]{2,1,0:T(8,128)(2,1)}), bf16[4,113,1024]{2,1,0:T(8,128)(2,1)S(1)}, u32[]{:S(2)}, u32[]{:S(2)}) async-start(bf16[4,113,1024]{2,1,0:T(8,128)(2,1)} %broadcast_in_dim.69), calls=%async_computation | async-start | bytes 1966080 | tf_op jit(solution)/shard_map/all_to_all | solution.py:2119
  49.4 18.3 %all-to-all-start.1 = ((bf16[8,128,512]{1,2,0:T(8,128)(2,1)}), bf16[8,128,512]{1,2,0:T(8,128)(2,1)S(1)}, u32[]{:S(2)}, u32[]{:S(2)}) async-start(bf16[8,128,512]{1,2,0:T(8,128)(2,1)} %bitcast.18), calls=%async_computation.1 | async-start | bytes 2097152 | tf_op jit(solution)/shard_map/all_to_all | solution.py:236
  60.0 8.4 %copy-start.9 = (bf16[64,512]{1,0:T(8,128)(2,1)S(1)}, bf16[64,512]{1,0:T(8,128)(2,1)}, u32[]{:S(2)}) copy-start(bf16[64,512]{1,0:T(8,128)(2,1)} %param.22) | copy-start | bytes 196612
  403.8 140.4 %all-to-all-start.3 = ((bf16[4,2,2,64,512]{4,3,2,1,0:T(8,128)(2,1)}), bf16[4,2,2,64,512]{4,3,2,1,0:T(8,128)(2,1)}, u32[]{:S(2)}, u32[]{:S(2)}) async-start(bf16[4,2,2,64,512]{4,3,2,1,0:T(8,128)(2,1)} %get-tuple-element.55), calls=%async_computation.3 | async-start | bytes 2097152 | tf_op jit(solution)/shard_map/all_to_all | solution.py:2228
  547.3 5.3 copy-start.3
  547.3 127.2 %all-to-all-start.4 = ((bf16[8,72,2048]{2,1,0:T(8,128)(2,1)}), bf16[8,72,2048]{2,1,0:T(8,128)(2,1)S(1)}, u32[]{:S(2)}, u32[]{:S(2)}) async-start(bf16[8,72,2048]{2,1,0:T(8,128)(2,1)} %pad_maximum_fusion), calls=%async_computation.4 | async-start | bytes 4718592 | tf_op jit(solution)/shard_map/all_to_all | solution.py:236
  662.1 6.0 copy-start.4
  675.9 2.4 copy-start.2
  675.9 4.4 copy-start.1
  678.2 1.5 copy-start.8
